TPU v7x, 32 devices: a whole 2x2x4 slice. The times are simulated.
32 devices in a mesh: groups: 2 (over y), tensor: 4 (over z), tenant: 2 (over x), dp: 2 (over core).
Axes of the slice: x: 2, y: 2, z: 4, core: 2. Of those that a mesh axis runs over, the one named last changes fastest.
Arguments:
- tokens: bfloat16 [4096, 4096], P(('groups', 'tenant', 'dp'), 'tensor'), parts along dimension 0, may hold values from -6 to 6
- query_weight: bfloat16 [4096, 4096], P(None, 'tensor'), may hold values from -0.125 to 0.125
- adapter_down_maps: bfloat16 [8, 4096, 16], P('tenant', 'tensor'), may hold values from -0.09375 to 0.09375
- adapter_up_maps: bfloat16 [8, 16, 4096], P('tenant', None, 'tensor'), may hold values from -1.5 to 1.5
- tenant_row_counts: int32 [16], P('groups'), parts along dimension 0, may hold values from 1 to 640, as said below
- tenant_adapter_slot: int32 [8], replicated, may hold values from 0 to 7, each once
- query_cotangent: bfloat16 [4096, 4096], P(('groups', 'tenant', 'dp'), 'tensor'), parts along dimension 0, may hold values from -6 to 6
Outputs:
- query: bfloat16 [4096, 4096], P(('groups', 'tenant', 'dp'), 'tensor'), parts along dimension 0
- token_input_gradient: bfloat16 [4096, 4096], P(('groups', 'tenant', 'dp'), 'tensor'), parts along dimension 0
- weight_grad: bfloat16 [8192, 4096], P('groups', 'tensor'), parts along dimension 0
- down_grad: float32 [16, 4096, 16], P(('groups', 'tenant'), 'tensor'), parts along dimension 0
- up_grad: float32 [16, 16, 4096], P(('groups', 'tenant'), None, 'tensor'), parts along dimension 0
There are 2 independent parts, one for each index of `groups`. A program takes and returns all parts, laid end to end along the dimension named above; an argument that names none is the same for every part. Nothing has to cross between parts.
Inputs may be any that keep to these rules, and one draw needn't show every extreme that they name: The sum over tenants of ceil(tenant_row_counts / 128) equals 16; tenants' blocks stand in tenant order from block 0. `tenant_adapter_slot`: each slot is named by exactly one tenant; slot s lies on index s // 4 of tenant.
All inputs are finite; a program needn't handle non-finite values.
Results may differ from a plain program's by a relative error of at most 0.014.
Values may be sent and summed in bfloat16 or wider, within the bound.
No kernel may reach another device: no remote copies, remote signals or barrier semaphores. Data moves between devices by JAX's collectives and lax.ppermute only.
A program may use at most 128 MiB of HBM per device.

v0:
```python
import jax
import jax.numpy as jnp
from jax import lax
from jax.sharding import PartitionSpec as P

BLOCK_ROWS = 128


adapter_scale = 2.0


def lookup(source, position):
    length = source.shape[0]
    match_mask = position[..., None] == jnp.arange(length, dtype=jnp.int32)
    return jnp.sum(jnp.where(match_mask, source, 0), axis=-1)


def layout(tenant_row_counts, row_ids):
    block_count = (tenant_row_counts + BLOCK_ROWS - 1) // BLOCK_ROWS
    segment_offset = jnp.cumsum(block_count) - block_count
    block_ids = row_ids // BLOCK_ROWS
    tenant_of = (
        jnp.sum((segment_offset[None, :] <= block_ids[:, None]).astype(jnp.int32), axis=1) - 1
    )
    offset = row_ids - BLOCK_ROWS * lookup(segment_offset, tenant_of)
    active_row_mask = offset < lookup(tenant_row_counts, tenant_of)
    return (tenant_of, active_row_mask)


def route_table(slots, tenants_per_device, owner_count, capacity):
    owner_of = slots // tenants_per_device
    count = owner_of.shape[0]
    order = jnp.arange(count, dtype=jnp.int32)
    before = (owner_of[:, None] == owner_of[None, :]) & (order[None, :] < order[:, None])
    place = jnp.sum(before.astype(jnp.int32), axis=1)
    owner_hit = owner_of[None, None, :] == jnp.arange(owner_count, dtype=jnp.int32)[:, None, None]
    place_hit = place[None, None, :] == jnp.arange(capacity, dtype=jnp.int32)[None, :, None]
    return (owner_hit & place_hit, place < capacity)


def shards(
    tokens,
    query_weight,
    adapter_down_maps,
    adapter_up_maps,
    tenant_row_counts,
    tenant_adapter_slot,
    query_cotangent,
):
    highest_precision = lax.Precision.HIGHEST
    resident_entries, column_width_size = tokens.shape
    tenants_per_device = adapter_down_maps.shape[0]
    tenant_total = tenant_row_counts.shape[0]
    owner_count = lax.axis_size("tenant")
    replicas = lax.axis_size("dp")
    group_pos = lax.axis_index(("tenant", "dp"))
    owner_pos = lax.axis_index("tenant")
    replica_pos = lax.axis_index("dp")
    blocks_dev = resident_entries // BLOCK_ROWS
    row_ids = group_pos * resident_entries + jnp.arange(resident_entries, dtype=jnp.int32)
    tenant_rows, active_row_mask = layout(tenant_row_counts, row_ids)
    masked = jnp.where(active_row_mask[:, None], tokens, jnp.zeros_like(tokens))
    gathered = lax.all_gather(masked, "tensor", axis=1, tiled=True)
    base_query_output = jnp.dot(gathered, query_weight, preferred_element_type=jnp.float32)
    row_blocks = masked.reshape(blocks_dev, BLOCK_ROWS, column_width_size)
    gradient_row_blocks = query_cotangent.reshape(blocks_dev, BLOCK_ROWS, column_width_size)
    block_ids = group_pos * blocks_dev + jnp.arange(blocks_dev, dtype=jnp.int32)
    block_slot = lookup(tenant_adapter_slot, layout(tenant_row_counts, block_ids * BLOCK_ROWS)[0])
    slot_range = jnp.arange(tenant_total, dtype=jnp.int32)
    capacity = max(1, blocks_dev // owner_count)
    send_hit, sent_mask = route_table(block_slot, tenants_per_device, owner_count, capacity)
    send_sel = send_hit.astype(jnp.bfloat16)
    packed = jnp.concatenate([row_blocks, gradient_row_blocks], axis=-1)
    outgoing = jnp.einsum(
        "ocb,brd->ocrd", send_sel, packed, preferred_element_type=jnp.float32
    ).astype(jnp.bfloat16)
    incoming = lax.all_to_all(outgoing, "tenant", split_axis=0, concat_axis=0, tiled=True)
    source_groups = jnp.arange(owner_count, dtype=jnp.int32) * replicas + replica_pos
    source_ids = (
        source_groups[:, None] * blocks_dev + jnp.arange(blocks_dev, dtype=jnp.int32)[None, :]
    )
    source_slot = lookup(
        tenant_adapter_slot, layout(tenant_row_counts, source_ids.reshape(-1) * BLOCK_ROWS)[0]
    ).reshape(owner_count, blocks_dev)
    source_hits = jax.vmap(
        lambda slots: route_table(slots, tenants_per_device, owner_count, capacity)[0]
    )(source_slot)
    recv_hit = lax.dynamic_index_in_dim(source_hits, owner_pos, axis=1, keepdims=False).astype(
        jnp.int32
    )
    recv_valid = jnp.sum(recv_hit, axis=-1)
    recv_slot = jnp.sum(recv_hit * source_slot[:, None, :], axis=-1)
    local_slot = recv_slot - owner_pos * tenants_per_device
    tenant_selector = (
        (local_slot[..., None] == jnp.arange(tenants_per_device, dtype=jnp.int32))
        & (recv_valid[..., None] > 0)
    ).astype(jnp.bfloat16)
    reducer_pick = jnp.einsum(
        "yvn,npa->yvpa", tenant_selector, adapter_down_maps, preferred_element_type=jnp.float32
    ).astype(jnp.bfloat16)
    up_sel = jnp.einsum(
        "hoj,jbu->hobu", tenant_selector, adapter_up_maps, preferred_element_type=jnp.float32
    ).astype(jnp.bfloat16)
    row_part = incoming[..., :column_width_size]
    grad_part = incoming[..., column_width_size:]
    every_down, expander_matrices_all = (
        lax.all_gather(adapter_down_maps, "tenant", axis=0, tiled=True),
        lax.all_gather(adapter_up_maps, "tenant", axis=0, tiled=True),
    )
    spillover_chooser = (
        (block_slot[:, None] == slot_range[None, :]) & jnp.logical_not(sent_mask)[:, None]
    ).astype(jnp.bfloat16)
    spill_down = jnp.einsum(
        "bt,tdk->bdk", spillover_chooser, every_down, preferred_element_type=jnp.float32
    ).astype(jnp.bfloat16)
    overflow_up_map = jnp.einsum(
        "gs,sjw->gjw", spillover_chooser, expander_matrices_all, preferred_element_type=jnp.float32
    ).astype(jnp.bfloat16)
    low_rank = jnp.einsum(
        "scrd,scdk->scrk", row_part, reducer_pick, preferred_element_type=jnp.float32
    )
    derivative_inner_factor = jnp.einsum(
        "scrd,sckd->scrk", grad_part, up_sel, preferred_element_type=jnp.float32
    )
    spill_low = jnp.einsum(
        "brd,bdk->brk", row_blocks, spill_down, preferred_element_type=jnp.float32
    )
    spill_grad = jnp.einsum(
        "zvy,zay->zva", gradient_row_blocks, overflow_up_map, preferred_element_type=jnp.float32
    )
    low_rank, derivative_inner_factor, spill_low, spill_grad = (
        lax.psum(low_rank.astype(jnp.bfloat16), "tensor").astype(jnp.float32),
        lax.psum(derivative_inner_factor.astype(jnp.bfloat16), "tensor").astype(jnp.float32),
        lax.psum(spill_low.astype(jnp.bfloat16), "tensor").astype(jnp.float32),
        lax.psum(spill_grad.astype(jnp.bfloat16), "tensor").astype(jnp.float32),
    )
    low_b = low_rank.astype(jnp.bfloat16)
    back_b = derivative_inner_factor.astype(jnp.bfloat16)
    overflow_low_rank_back = spill_low.astype(jnp.bfloat16)
    spill_back_b = spill_grad.astype(jnp.bfloat16)
    adapter_output = (
        adapter_scale
        * jnp.einsum("scrk,sckd->scrd", low_b, up_sel, preferred_element_type=jnp.float32)
    ).astype(jnp.bfloat16)
    input_partial = (
        adapter_scale
        * jnp.einsum("scrk,scdk->scrd", back_b, reducer_pick, preferred_element_type=jnp.float32)
    ).astype(jnp.bfloat16)
    returned = lax.all_to_all(
        jnp.concatenate([adapter_output, input_partial], axis=-1),
        "tenant",
        split_axis=0,
        concat_axis=0,
        tiled=True,
    )
    placed_rows = jnp.einsum(
        "ocb,ocrd->brd", send_sel, returned, preferred_element_type=jnp.float32
    )
    overflow_output = (
        adapter_scale
        * jnp.einsum(
            "ivl,ilf->ivf",
            overflow_low_rank_back,
            overflow_up_map,
            preferred_element_type=jnp.float32,
        )
    ).astype(jnp.bfloat16)
    spill_input = (
        adapter_scale
        * jnp.einsum("brk,bdk->brd", spill_back_b, spill_down, preferred_element_type=jnp.float32)
    ).astype(jnp.bfloat16)
    adapter_row_output = (
        placed_rows[..., :column_width_size] + overflow_output.astype(jnp.float32)
    ).reshape(resident_entries, column_width_size)
    input_rows = (placed_rows[..., column_width_size:] + spill_input.astype(jnp.float32)).reshape(
        resident_entries, column_width_size
    )
    down_terms = jnp.einsum("scrd,scrk->scdk", row_part, back_b, preferred_element_type=jnp.float32)
    up_terms = jnp.einsum("scrk,scrd->sckd", low_b, grad_part, preferred_element_type=jnp.float32)
    global_choose = ((recv_slot[..., None] == slot_range) & (recv_valid[..., None] > 0)).astype(
        jnp.float32
    )
    down_maps_stacked = jnp.einsum(
        "sct,scdk->tdk", global_choose, down_terms, precision=highest_precision
    )
    up_maps_stacked = jnp.einsum(
        "sct,sckd->tkd", global_choose, up_terms, precision=highest_precision
    )
    spill_down_terms = jnp.einsum(
        "brd,brk->bdk", row_blocks, spill_back_b, preferred_element_type=jnp.float32
    )
    overflow_up_products = jnp.einsum(
        "ocg,oca->oga",
        overflow_low_rank_back,
        gradient_row_blocks,
        preferred_element_type=jnp.float32,
    )
    overflow_function = spillover_chooser.astype(jnp.float32)
    down_maps_stacked = adapter_scale * (
        down_maps_stacked
        + jnp.einsum(
            "bt,bdk->tdk", overflow_function, spill_down_terms, precision=highest_precision
        )
    )
    up_maps_stacked = adapter_scale * (
        up_maps_stacked
        + jnp.einsum(
            "po,pvw->ovw", overflow_function, overflow_up_products, precision=highest_precision
        )
    )
    down_maps_stacked, up_maps_stacked = (
        lax.psum(down_maps_stacked.astype(jnp.bfloat16), ("tenant", "dp")).astype(jnp.float32),
        lax.psum(up_maps_stacked.astype(jnp.bfloat16), ("tenant", "dp")).astype(jnp.float32),
    )
    down_grad = lax.dynamic_slice_in_dim(
        down_maps_stacked, owner_pos * tenants_per_device, tenants_per_device, 0
    )
    up_grad = lax.dynamic_slice_in_dim(
        up_maps_stacked, owner_pos * tenants_per_device, tenants_per_device, 0
    )
    query = (base_query_output + adapter_row_output).astype(jnp.bfloat16)
    input_term = lax.dot_general(
        query_cotangent, query_weight, (((1,), (1,)), ((), ())), preferred_element_type=jnp.float32
    )
    input_gradient_sum = lax.psum_scatter(
        input_term.astype(jnp.bfloat16), "tensor", scatter_dimension=1, tiled=True
    ).astype(jnp.float32)
    token_input_gradient = jnp.where(
        active_row_mask[:, None], input_gradient_sum + input_rows, 0.0
    ).astype(jnp.bfloat16)
    weight_term = lax.dot_general(
        gathered, query_cotangent, (((0,), (0,)), ((), ())), preferred_element_type=jnp.float32
    )
    weight_grad = lax.psum(weight_term.astype(jnp.bfloat16), ("tenant", "dp"))
    return (query, token_input_gradient, weight_grad, down_grad, up_grad)


def solution(mesh):
    placed = (
        P(("groups", "tenant", "dp"), "tensor"),
        P(None, "tensor"),
        P("tenant", "tensor", None),
        P("tenant", None, "tensor"),
        P("groups"),
        P(),
        P(("groups", "tenant", "dp"), "tensor"),
    )
    return jax.shard_map(
        shards,
        mesh=mesh,
        in_specs=placed,
        out_specs=(
            P(("groups", "tenant", "dp"), "tensor"),
            P(("groups", "tenant", "dp"), "tensor"),
            P("groups", "tensor"),
            P(("groups", "tenant"), "tensor", None),
            P(("groups", "tenant"), None, "tensor"),
        ),
        check_vma=False,
    )
```

profile of v0, /device:TPU:0, one launch (start us, length us, event | category | flops | bytes accessed | tf_op | source)
XLA Modules:
  0.0 442.0 jit_solution(17082148957333863220)
XLA Ops:
  9.6 2.0 copy.124
  12.9 3.0 convolution_convert_fusion.2
  15.9 5.0 %all-to-all-start = ((bf16[2,2,128,2048]{3,1,2,0:T(2,128)(2,1)}), bf16[2,2,128,2048]{3,1,2,0:T(2,128)(2,1)}, u32[]{:S(2)}, u32[]{:S(2)}) async-start(bf16[2,2,128,2048]{3,1,2,0:T(2,128)(2,1)} %convolution_convert_fusion.2), calls=%async_computation | async-start | bytes 4194304 | tf_op jit(solution)/shard_map/all_to_all | solution.py:77
  22.5 27.5 %all_gather.10 = bf16[8,1024,16]{1,2,0:T(8,128)(2,1)S(1)} all-gather(bf16[4,1024,16]{1,2,0:T(8,128)(2,1)S(1)} %copy-done.5), channel_id=1, replica_groups=mesh['groups'=2,'tensor'=4,'tenant'=2,'dp'=2] {'tenant'}, dimensions={0}, use_global_device_ids=true | all-gather | bytes 393216 | tf_op jit(solution)/shard_map/all_gather | solution.py:107
  50.0 5.6 %all_gather.11 = bf16[8,16,1024]{2,1,0:T(8,128)(2,1)S(1)} all-gather(bf16[4,16,1024]{2,1,0:T(8,128)(2,1)S(1)} %copy-done.6), channel_id=1, replica_groups=mesh['groups'=2,'tensor'=4,'tenant'=2,'dp'=2] {'tenant'}, dimensions={0}, use_global_device_ids=true | all-gather | bytes 393216 | tf_op jit(solution)/shard_map/all_gather | solution.py:108
  56.1 1.0 convolution_convert_fusion.8
  57.1 1.0 fusion.10
  58.1 2.7 fusion.57
  60.8 1.0 convolution_convert_fusion.9
  61.8 1.0 convolution_convert_fusion.10
  63.8 9.5 %convolution_convert_fusion.1 = bf16[512,4096]{1,0:T(8,128)(2,1)} fusion(bf16[512,1024]{1,0:T(8,128)(2,1)S(1)} %copy-done.2, bf16[4096,1024]{1,0:T(8,128)(2,1)} %param.8), kind=kOutput, calls=%fused_computation.1 | convolution fusion | flops 4297064448 | bytes 13631488 | tf_op jit(solution)/shard_map/dot_general | solution.py:222
  73.5 24.2 %all-reduce.7.cloned.1.call-done = (bf16[2,2,128,16]{2,3,1,0:T(8,128)(2,1)}, bf16[2,2,128,16]{2,3,1,0:T(8,128)(2,1)}, bf16[4,128,16]{1,2,0:T(8,128)(2,1)}, bf16[4,128,16]{1,2,0:T(8,128)(2,1)}) async-done(((bf16[2,2,128,16]{2,3,1,0:T(8,128)(2,1)}, bf16[2,2,128,16]{2,3,1,0:T(8,128)(2,1)}, bf16[4,128,16]{1,2,0:T(8,128)(2,1)}, bf16[4,128,16]{1,2,0:T(8,128)(2,1)}), (bf16[2,2,128,16]{2,3,1,0:T(8,128)(2,1)}, ...) | async-done | bytes 65552 | tf_op jit(solution)/shard_map/psum | solution.py:133
  97.8 1.2 multiply_convert_fusion.2
  99.0 1.2 multiply_convert_fusion.3
  100.3 3.5 copy.134
  103.8 5.1 %all-to-all-start.1 = ((bf16[2,2,128,2048]{3,1,2,0:T(2,128)(2,1)}), bf16[2,2,128,2048]{3,1,2,0:T(2,128)(2,1)}, u32[]{:S(2)}, u32[]{:S(2)}) async-start(bf16[2,2,128,2048]{3,1,2,0:T(2,128)(2,1)} %copy.134), calls=%async_computation.1 | async-start | bytes 4194304 | tf_op jit(solution)/shard_map/all_to_all | solution.py:149
  109.2 1.9 fusion.14
  113.2 1.3 fusion.8
  114.7 1.3 fusion.9
  116.0 64.5 %all-gather.2.cloned.1.call-done = bf16[512,4096]{1,0:T(8,128)(2,1)} async-done(((bf16[512,1024]{1,0:T(8,128)(2,1)}), bf16[512,4096]{1,0:T(8,128)(2,1)}) %all-gather.2.cloned.1.call-update) | async-done | bytes 4194320 | tf_op jit(solution)/shard_map/all_gather | solution.py:63
  180.5 9.0 %convolution_convert_fusion = bf16[4096,1024]{1,0:T(8,128)(2,1)} fusion(bf16[512,4096]{1,0:T(8,128)(2,1)} %all-gather.2.cloned.1.call-done, bf16[512,1024]{1,0:T(8,128)(2,1)S(1)} %copy-done.2), kind=kOutput, calls=%fused_computation | convolution fusion | flops 4299161600 | bytes 13631488 | tf_op jit(solution)/shard_map/dot_general | solution.py:231
  189.5 6.4 %convolution_bitcast_fusion = f32[4,128,2048]{2,0,1:T(4,128)S(1)} fusion(bf16[2,2,128,2048]{3,1,2,0:T(2,128)(2,1)} %all-to-all-done.1, pred[2,4]{1,0:T(4,128)(4,1)S(1)} %iota_compare_fusion.7, pred[2,4]{1,0:T(4,128)(4,1)S(1)} %iota_compare_fusion.8), kind=kOutput, calls=%fused_computation.2 | convolution fusion | flops 8388624 | bytes 6291472 | tf_op jit(solution)/shard_map/ocb,ocrd->brd/dot_general | solution.py:156
  196.0 1.2 fusion.56
  197.2 1.4 copy_add_fusion.1
  198.6 1.4 copy_add_fusion
  201.1 5.5 %fusion.4 = bf16[512,1024]{1,0:T(8,128)(2,1)} fusion(f32[4,128,1024]{2,1,0:T(8,128)S(1)} %copy_add_fusion.1, bf16[512,4096]{1,0:T(8,128)(2,1)S(1)} %copy-done.12, bf16[4096,1024]{1,0:T(8,128)(2,1)S(1)} %bitcast.90), kind=kOutput, calls=%fused_computation.14 | convolution fusion | flops 4296015872 | bytes 15728640 | tf_op jit(solution)/shard_map/dot_general | solution.py:64
  206.6 51.7 %reduce-scatter.2.cloned.1.call-done = bf16[512,1024]{1,0:T(8,128)(2,1)} async-done(((bf16[512,4096]{1,0:T(8,128)(2,1)}), bf16[512,1024]{1,0:T(8,128)(2,1)}) %reduce-scatter.2.cloned.1.call-update) | async-done | bytes 1048592 | tf_op jit(solution)/shard_map/reduce_scatter | solution.py:225
  258.3 2.8 fusion.3
  261.0 162.9 %all-reduce.5.cloned.1.call-done = (bf16[4096,1024]{1,0:T(8,128)(2,1)}, bf16[8,1024,16]{1,0,2:T(8,128)(2,1)}, bf16[8,16,1024]{2,0,1:T(8,128)(2,1)}) async-done(((bf16[4096,1024]{1,0:T(8,128)(2,1)}, bf16[8,1024,16]{1,0,2:T(8,128)(2,1)}, bf16[8,16,1024]{2,0,1:T(8,128)(2,1)}), (bf16[4096,1024]{1,0:T(8,128)(2,1)}, bf16[8,1024,16]{1,0,2:T(8,128)(2,1)}, ...) | async-done | bytes 8912912 | tf_op jit(solution)/shard_map/psum | solution.py:234
  424.0 1.0 dynamic-slice_convert_fusion.1
  425.8 1.0 dynamic-slice_convert_fusion
  427.7 7.8 %copy.220 = bf16[4096,1024]{1,0:T(8,128)(2,1)} copy(bf16[4096,1024]{1,0:T(8,128)(2,1)} %get-tuple-element.49) | data formatting | bytes 16777216
  (94 shorter events, 12.4 us)
Async XLA Ops:
  7.2 4.6 %copy-start.11 = (s32[8]{0:T(128)S(1)}, s32[8]{0:T(128)}, u32[]{:S(2)}) copy-start(s32[8]{0:T(128)} %param.11) | copy-start | bytes 100
  7.2 4.7 %copy-start.4 = (bf16[512,1024]{1,0:T(8,128)(2,1)S(1)}, bf16[512,1024]{1,0:T(8,128)(2,1)}, u32[]{:S(2)}) copy-start(bf16[512,1024]{1,0:T(8,128)(2,1)} %param.7) | copy-start | bytes 3145732
  12.0 44.1 %copy-start = (bf16[512,1024]{1,0:T(8,128)(2,1)}, bf16[512,1024]{1,0:T(8,128)(2,1)S(1)}, u32[]{:S(2)}) copy-start(bf16[512,1024]{1,0:T(8,128)(2,1)S(1)} %broadcast_select_fusion) | copy-start | bytes 3145732
  15.9 5.3 %copy-start.13 = (s32[8]{0:T(128)S(1)}, s32[8]{0:T(128)}, u32[]{:S(2)}) copy-start(s32[8]{0:T(128)} %param.12) | copy-start | bytes 100
  15.9 6.0 %copy-start.6 = (bf16[4,16,1024]{2,1,0:T(8,128)(2,1)S(1)}, bf16[4,16,1024]{2,1,0:T(8,128)(2,1)}, u32[]{:S(2)}) copy-start(bf16[4,16,1024]{2,1,0:T(8,128)(2,1)} %param.10) | copy-start | bytes 393220
  15.9 6.3 %copy-start.5 = (bf16[4,1024,16]{1,2,0:T(8,128)(2,1)S(1)}, bf16[4,1024,16]{1,2,0:T(8,128)(2,1)}, u32[]{:S(2)}) copy-start(bf16[4,1024,16]{1,2,0:T(8,128)(2,1)} %param.9) | copy-start | bytes 393220
  15.9 42.3 %all-to-all-start = ((bf16[2,2,128,2048]{3,1,2,0:T(2,128)(2,1)}), bf16[2,2,128,2048]{3,1,2,0:T(2,128)(2,1)}, u32[]{:S(2)}, u32[]{:S(2)}) async-start(bf16[2,2,128,2048]{3,1,2,0:T(2,128)(2,1)} %convolution_convert_fusion.2), calls=%async_computation | async-start | bytes 4194304 | tf_op jit(solution)/shard_map/all_to_all | solution.py:77
  20.8 36.3 %copy-start.2 = (bf16[512,1024]{1,0:T(8,128)(2,1)S(1)}, bf16[512,1024]{1,0:T(8,128)(2,1)}, u32[]{:S(2)}) copy-start(bf16[512,1024]{1,0:T(8,128)(2,1)} %param.13) | copy-start | bytes 3145732
  20.8 76.9 %all-reduce.7.cloned.1.call-start = ((), (), s32[]{:S(2)}) async-start(), calls=%async_computation.6 | async-start | bytes 131072 | tf_op jit(solution)/shard_map/psum | solution.py:133
  60.8 1.0 copy-start.3
  62.8 117.7 %all-gather.2.cloned.1.call-start = ((), (), s32[]{:S(2)}) async-start(), calls=%async_computation.3 | async-start | bytes 5242880 | tf_op jit(solution)/shard_map/all_gather | solution.py:63
  63.6 194.7 %reduce-scatter.2.cloned.1.call-start = ((), (), s32[]{:S(2)}) async-start(), calls=%async_computation.4 | async-start | bytes 5242880 | tf_op jit(solution)/shard_map/reduce_scatter | solution.py:225
  103.8 5.4 %copy-start.10 = (bf16[2,2,128,16]{2,3,1,0:T(8,128)(2,1)S(1)}, bf16[2,2,128,16]{2,3,1,0:T(8,128)(2,1)}, u32[]{:S(2)}) copy-start(bf16[2,2,128,16]{2,3,1,0:T(8,128)(2,1)} %get-tuple-element.37) | copy-start | bytes 49156
  103.8 85.7 %all-to-all-start.1 = ((bf16[2,2,128,2048]{3,1,2,0:T(2,128)(2,1)}), bf16[2,2,128,2048]{3,1,2,0:T(2,128)(2,1)}, u32[]{:S(2)}, u32[]{:S(2)}) async-start(bf16[2,2,128,2048]{3,1,2,0:T(2,128)(2,1)} %copy.134), calls=%async_computation.1 | async-start | bytes 4194304 | tf_op jit(solution)/shard_map/all_to_all | solution.py:149
  108.9 2.9 copy-start.9
  108.9 4.1 copy-start.1
  108.9 4.1 copy-start.7
  108.9 315.1 %all-reduce.5.cloned.1.call-start = ((), (), s32[]{:S(2)}) async-start(), calls=%async_computation.5 | async-start | bytes 17825792 | tf_op jit(solution)/shard_map/psum | solution.py:234
  111.8 2.7 copy-start.8
  196.0 4.1 slice-start
  197.2 2.9 slice-start.1
  198.6 2.4 copy-start.12
Sparse Core Ops, SparseCore 0:
  63.0 34.7 all-reduce.6
  100.0 80.4 all-gather.1
  182.9 75.2 reduce-scatter.1
  261.4 162.5 all-reduce.4
where the time goes:
time: 443 us; the launch traced here: 442 us
  waiting for transfers between devices  304 us (69%)
  matrix products  50.5 us (11%)
  blocking collectives  33.1 us (7%)
  local copies, waits for them, and re-layouts  21.1 us (5%)
  between operations  14.2 us (3%)
  starting transfers between devices  10.6 us (2%)
  other arithmetic  8.49 us (2%)
    psum x1, waiting for transfers between devices, shards(): weight_grad = lax.psum(weight_term.astype(jnp.bfloat16), ('tenant', 'dp'))  163 us
    all_gather x1, waiting for transfers between devices, shards(): gathered = lax.all_gather(masked, 'tensor', axis=1, tiled=True)  64.5 us
    reduce_scatter x1, waiting for transfers between devices, shards(): lax.psum_scatter(input_term.astype(jnp.bfloat16), 'tensor', scatter_dimen...  51.7 us
    all_gather x1, blocking collectives, shards(): lax.all_gather(adapter_down_maps, 'tenant', axis=0, tiled=True)  27.5 us
    psum x1, waiting for transfers between devices, shards(): lax.psum(derivative_inner_factor.astype(jnp.bfloat16), 'tensor')  24.2 us
    unnamed x35, local copies, waits for them, and re-layouts  10.5 us
    dot_general x1, matrix products, shards(): lax.dot_general(query_cotangent, query_weight, (((1,), (1,)), ((), ())),...  9.49 us
    dot_general x1, matrix products, shards(): lax.dot_general(gathered, query_cotangent, (((0,), (0,)), ((), ())), pref...  8.99 us
  transfers between devices with their start and end apart: 6, of which 4 were waited for; matrix products, arithmetic and copies ran while one was open for 12% of the time, Pallas kernels for 0%

commit v1 on v0

v1 whole, which is shorter than its diff:
```python
import jax
import jax.numpy as jnp
from jax import lax
from jax.sharding import PartitionSpec as P

BLOCK_ROWS = 128
SCALE = 2.0
F32 = jnp.float32
B16 = jnp.bfloat16


def dot(a, b, ca, cb):
    return lax.dot_general(a, b, (((ca,), (cb,)), ((), ())), preferred_element_type=F32)


def lookup(source, position):
    match_mask = position[..., None] == jnp.arange(source.shape[0], dtype=jnp.int32)
    return jnp.sum(jnp.where(match_mask, source, 0), axis=-1)


def layout(tenant_row_counts, row_ids):
    block_count = (tenant_row_counts + BLOCK_ROWS - 1) // BLOCK_ROWS
    segment_offset = jnp.cumsum(block_count) - block_count
    block_ids = row_ids // BLOCK_ROWS
    tenant_of = (
        jnp.sum((segment_offset[None, :] <= block_ids[:, None]).astype(jnp.int32), axis=1) - 1
    )
    offset = row_ids - BLOCK_ROWS * lookup(segment_offset, tenant_of)
    return tenant_of, offset < lookup(tenant_row_counts, tenant_of)


def rank_partials(maps, rows, mask, slots):
    every = dot(maps, rows, 1, 1)
    every = every.reshape(slots, -1, rows.shape[0])
    return jnp.sum(jnp.where(mask[:, None, :], every, 0.0), axis=0)


def spread(values, mask):
    wide = jnp.where(mask[:, None, :], values[None], jnp.zeros((), values.dtype))
    return wide.reshape(-1, values.shape[-1])


def shards_general(tokens, weight, down_maps, up_maps, counts, slot_of, cotangent):
    rows, width = tokens.shape
    held, _, rank = down_maps.shape
    slots = held * lax.axis_size("tenant")
    owner = lax.axis_index("tenant")
    row_ids = lax.axis_index(("tenant", "dp")) * rows + jnp.arange(rows, dtype=jnp.int32)
    tenant, live = layout(counts, row_ids)
    slot = lookup(slot_of, tenant)
    mask = slot[None, :] == jnp.arange(slots, dtype=jnp.int32)[:, None]
    grads = jnp.where(live[:, None], cotangent, jnp.zeros_like(cotangent))
    kept = jnp.where(live[:, None], tokens, jnp.zeros_like(tokens))
    down = lax.all_gather(jnp.swapaxes(down_maps, 1, 2), "tenant", axis=0, tiled=True)
    up = lax.all_gather(up_maps, "tenant", axis=0, tiled=True)
    down, up = down.reshape(-1, width), up.reshape(-1, width)
    gathered = lax.all_gather(kept, "tensor", axis=1, tiled=True)
    part = jnp.stack(
        [rank_partials(down, kept, mask, slots), rank_partials(up, grads, mask, slots)]
    )
    low, back = lax.psum(part.astype(B16), "tensor")
    low, back = spread(low, mask), spread(back, mask)
    base = dot(gathered, weight, 1, 0)
    query = (base + (SCALE * dot(low, up, 0, 0)).astype(B16).astype(F32)).astype(B16)
    term = dot(grads, weight, 1, 1).astype(B16)
    summed = lax.psum_scatter(term, "tensor", scatter_dimension=1, tiled=True).astype(F32)
    lora = (SCALE * dot(back, down, 0, 0)).astype(B16).astype(F32)
    token_grad = jnp.where(live[:, None], summed + lora, 0.0).astype(B16)
    axes = ("tenant", "dp")
    weight_grad = lax.psum(dot(gathered, grads, 0, 0).astype(B16), axes)
    maps = jnp.stack([SCALE * dot(back, kept, 1, 0), SCALE * dot(low, grads, 1, 0)])
    maps = lax.psum(maps.astype(B16), axes).astype(F32).reshape(2, slots, rank, width)
    maps = lax.dynamic_slice_in_dim(maps, owner * held, held, 1)
    return query, token_grad, weight_grad, jnp.swapaxes(maps[0], 1, 2), maps[1]


def arrival_plan(n):
    plan = [[] for _ in range(n - 1)]
    for z in range(n):
        seen = []
        for t in range(1, n):
            if z - t >= 0:
                seen.append((t, 0, z - t))
            if z + t < n:
                seen.append((t, 1, z + t))
        for step, entry in enumerate(seen):
            plan[step].append(entry)
    return plan


def shards_line(tokens, weight, down_maps, up_maps, counts, slot_of, cotangent):
    rows, width = tokens.shape
    held, _, rank = down_maps.shape
    n = lax.axis_size("tensor")
    slots = held * 2
    z = lax.axis_index("tensor")
    owner = lax.axis_index("tenant")
    core = lax.axis_index("dp")
    half = width // 2
    swap = [(0, 1), (1, 0)]

    def right(value, sources):
        return lax.ppermute(value, "tensor", [(i, i + 1) for i in sources])

    def left(value, sources):
        return lax.ppermute(value, "tensor", [(i, i - 1) for i in sources])

    def other_tenant(value):
        return lax.ppermute(value, "tenant", swap)

    def other_core(value):
        return lax.ppermute(value, "dp", swap)

    row_ids = (owner * 2 + core) * rows + jnp.arange(rows, dtype=jnp.int32)
    tenant, live = layout(counts, row_ids)
    place = lax.rem(lookup(slot_of, tenant) + (2 - owner) * held, slots)
    mask = place[None, :] == jnp.arange(slots, dtype=jnp.int32)[:, None]
    grads = jnp.where(live[:, None], cotangent, jnp.zeros_like(cotangent))

    first = (1 - core) * half
    second = core * half
    own = [
        lax.dynamic_slice_in_dim(tokens, first, half, 1),
        lax.dynamic_slice_in_dim(tokens, second, half, 1),
    ]

    from_left = {0: own}
    from_right = {0: own}
    for t in range(1, n):
        from_left[t] = [right(v, range(t - 1, n - 1)) for v in from_left[t - 1]]
        from_right[t] = [left(v, range(1, n - t + 1)) for v in from_right[t - 1]]

    mine = jnp.stack([jnp.swapaxes(down_maps, 1, 2), up_maps]).reshape(2, -1, width)
    fetched = other_tenant(lax.dynamic_index_in_dim(mine, core, 0, keepdims=False))
    shared = other_core(fetched)
    down = jnp.concatenate([mine[0], jnp.where(core == 0, fetched, shared)])
    up = jnp.concatenate([mine[1], jnp.where(core == 0, shared, fetched)])

    part = jnp.stack(
        [rank_partials(down, tokens, mask, slots), rank_partials(up, grads, mask, slots)]
    ).astype(B16)
    total = part.astype(F32)
    for k in range(1, n):
        total = total + lax.ppermute(
            part, "tensor", [(i, (i + k) % n) for i in range(n)]
        ).astype(F32)
    low, back = total.astype(B16)
    low, back = spread(low, mask), spread(back, mask)

    def weight_piece(pair):
        away = dot(pair[0], grads, 0, 0).astype(B16)
        home = dot(pair[1], grads, 0, 0)
        mix = (home + other_core(away).astype(F32)).astype(B16)
        subs = []
        for part_rows in jnp.split(mix, 2):
            whole = (part_rows.astype(F32) + other_tenant(part_rows).astype(F32)).astype(B16)
            subs.append((whole, other_core(whole)))
        return subs

    gathered = jnp.zeros((rows, n * width), B16)
    weight_grad = jnp.zeros((n * width, width), B16)

    def keep(gathered, weight_grad, pair, chunk):
        gathered = lax.dynamic_update_slice(gathered, pair[0], (0, chunk * width + first))
        gathered = lax.dynamic_update_slice(gathered, pair[1], (0, chunk * width + second))
        for i, (ours, theirs) in enumerate(weight_piece(pair)):
            at = chunk * width + i * (half // 2)
            weight_grad = lax.dynamic_update_slice(weight_grad, ours, (at + second, 0))
            weight_grad = lax.dynamic_update_slice(weight_grad, theirs, (at + first, 0))
        return gathered, weight_grad

    gathered, weight_grad = keep(gathered, weight_grad, own, z)
    for choices in arrival_plan(n):
        pair = None
        chunk = 0
        for at, (t, direction, source) in enumerate(choices):
            offer = (from_left, from_right)[direction][t]
            if pair is None:
                pair = offer
            else:
                pair = [jnp.where(z >= at, new, old) for new, old in zip(offer, pair)]
            chunk = jnp.where(z == at, source, chunk)
        gathered, weight_grad = keep(gathered, weight_grad, pair, chunk)

    base = dot(gathered, weight, 1, 0)
    lora_out = (SCALE * dot(low, up, 0, 0)).astype(B16).astype(F32)
    query = jnp.where(live[:, None], base + lora_out, 0.0).astype(B16)

    term = dot(grads, weight, 1, 1).astype(B16)
    pieces = jnp.split(term, 2)

    def term_of(piece, chunk):
        chunk = jnp.clip(chunk, 0, n - 1)
        return lax.dynamic_slice_in_dim(piece, chunk * width, width, 1)

    lora_in = (SCALE * dot(back, down, 0, 0)).astype(B16)
    results = []
    for piece, lora in zip(pieces, jnp.split(lora_in, 2)):
        sum_left = sum_right = None
        for t in range(2, n + 1):
            to_right = term_of(piece, n + z + 1 - t)
            to_left = term_of(piece, z - n - 1 + t)
            if sum_left is not None:
                to_right = (to_right.astype(F32) + sum_left.astype(F32)).astype(B16)
                to_left = (to_left.astype(F32) + sum_right.astype(F32)).astype(B16)
            sum_left = right(to_right, range(0, t - 1))
            sum_right = left(to_left, range(n + 1 - t, n))
        results.append(
            term_of(piece, z).astype(F32)
            + sum_left.astype(F32)
            + sum_right.astype(F32)
            + lora.astype(F32)
        )
    token_grad = jnp.where(live[:, None], jnp.concatenate(results), 0.0).astype(B16)

    maps = [SCALE * dot(back, tokens, 1, 0), SCALE * dot(low, grads, 1, 0)]
    for_sibling = jnp.where(core == 0, maps[1], maps[0]).astype(B16)
    summed = jnp.where(core == 0, maps[0], maps[1]) + other_core(for_sibling).astype(F32)
    kept, sent = jnp.split(summed, 2)
    kept = kept + other_tenant(sent.astype(B16)).astype(F32)
    sibling = other_core(kept)
    down_grad = jnp.where(core == 0, kept, sibling).reshape(held, rank, width)
    up_grad = jnp.where(core == 0, sibling, kept).reshape(held, rank, width)
    return query, token_grad, weight_grad, jnp.swapaxes(down_grad, 1, 2), up_grad


def solution(mesh):
    placed = (
        P(("groups", "tenant", "dp"), "tensor"),
        P(None, "tensor"),
        P("tenant", "tensor", None),
        P("tenant", None, "tensor"),
        P("groups"),
        P(),
        P(("groups", "tenant", "dp"), "tensor"),
    )
    short = 2 <= mesh.shape["tensor"] <= 4
    paired = mesh.shape["tenant"] == 2 and mesh.shape["dp"] == 2
    return jax.shard_map(
        shards_line if short and paired else shards_general,
        mesh=mesh,
        in_specs=placed,
        out_specs=(
            P(("groups", "tenant", "dp"), "tensor"),
            P(("groups", "tenant", "dp"), "tensor"),
            P("groups", "tensor"),
            P(("groups", "tenant"), "tensor", None),
            P(("groups", "tenant"), None, "tensor"),
        ),
        check_vma=False,
    )
```

time: 443 us -> 226 us (0.51)
  waiting for transfers between devices: 304 us -> 96.4 us
  starting transfers between devices: 10.6 us -> 60 us
  blocking collectives: 33.1 us -> 0 us
  matrix products: 50.5 us -> 32.5 us
  between operations: 14.2 us -> 1.67 us
  other arithmetic: 8.49 us -> 19.4 us
  local copies, waits for them, and re-layouts: 21.1 us -> 15.4 us
    psum x2 -> x0, waiting for transfers between devices: 187 us -> none  [the longest x1 163 us: shards(): weight_grad = lax.psum(weight_term.astype(jnp.bfloat16), ('tenant', 'dp'))]
    ppermute x0 -> x52, waiting for transfers between devices: none -> 96.4 us  [the longest x10 49.8 us: other_tenant(): return lax.ppermute(value, 'tenant', swap)]
    all_gather x1 -> x0, waiting for transfers between devices: 64.5 us -> none  [shards(): gathered = lax.all_gather(masked, 'tensor', axis=1, tiled=True)]
    ppermute x0 -> x52, starting transfers between devices: none -> 60 us  [the longest x12 29.7 us: right(): return lax.ppermute(value, 'tensor', [(i, i + 1) for i in sources])]
    reduce_scatter x1 -> x0, waiting for transfers between devices: 51.7 us -> none  [shards(): lax.psum_scatter(input_term.astype(jnp.bfloat16), 'tensor', scatter_dimen...]
    all_gather x2 -> x0, blocking collectives: 33.1 us -> none  [the longest x1 27.5 us: shards(): lax.all_gather(adapter_down_maps, 'tenant', axis=0, tiled=True)]
    dot_general x25 -> x16, matrix products: 50.5 us -> 32.5 us  [dot(): lax.dot_general(a, b, (((ca,), (cb,)), ((), ())), preferred_element_type=...]
    dynamic_update_slice x0 -> x14, other arithmetic: none -> 10.5 us  [the longest x3 5.33 us: keep(): lax.dynamic_update_slice(gathered, pair[0], (0, chunk * width + first))]
  transfers between devices with their start and end apart: 6 -> 52, of which waited for: 4 -> 16; matrix products, arithmetic and copies ran while one was open for 12% -> 26% of each run, Pallas kernels for 0% -> 0%
where the time goes in v1:
time: 226 us; the launch traced here: 225 us
  waiting for transfers between devices  96.4 us (43%)
  starting transfers between devices  60 us (27%)
  matrix products  32.5 us (14%)
  other arithmetic  19.4 us (9%)
  local copies, waits for them, and re-layouts  15.4 us (7%)
    ppermute x10, waiting for transfers between devices, other_tenant(): return lax.ppermute(value, 'tenant', swap)  49.8 us
    dot_general x16, matrix products, dot(): lax.dot_general(a, b, (((ca,), (cb,)), ((), ())), preferred_element_type=...  32.5 us
    ppermute x12, starting transfers between devices, right(): return lax.ppermute(value, 'tensor', [(i, i + 1) for i in sources])  29.7 us
    ppermute x12, waiting for transfers between devices, left(): return lax.ppermute(value, 'tensor', [(i, i - 1) for i in sources])  27.1 us
    ppermute x12, waiting for transfers between devices, right(): return lax.ppermute(value, 'tensor', [(i, i + 1) for i in sources])  19.5 us
    ppermute x12, starting transfers between devices, left(): return lax.ppermute(value, 'tensor', [(i, i - 1) for i in sources])  13.4 us
    ppermute x10, starting transfers between devices, other_tenant(): return lax.ppermute(value, 'tenant', swap)  9.96 us
    ppermute x3, starting transfers between devices, shards_line(): lax.ppermute(part, 'tensor', [(i, (i + k) % n) for i in range(n)])  5.55 us
  transfers between devices with their start and end apart: 52, of which 16 were waited for; matrix products, arithmetic and copies ran while one was open for 26% of the time, Pallas kernels for 0%

profile of v1, /device:TPU:0, one launch (start us, length us, event | category | flops | bytes accessed | tf_op | source)
XLA Modules:
  0.0 225.4 jit_solution(17267195776300142597)
XLA Ops:
  0.7 2.5 %broadcast_in_dim.112 = bf16[512,4096]{1,0:T(8,128)(2,1)} broadcast(bf16[]{:T(256)} %constant.83.clone.1), dimensions={} | broadcast | bytes 4194306 | tf_op jit(solution)/shard_map/broadcast_in_dim | solution.py:160
  5.6 6.4 %collective-permute-start = (bf16[512,512]{1,0:T(8,128)(2,1)}, bf16[512,512]{1,0:T(8,128)(2,1)}, u32[]{:S(2)}, u32[]{:S(2)}) collective-permute-start(bf16[512,512]{1,0:T(8,128)(2,1)} %get-tuple-element.37), channel_id=1, source_target_pairs={{0,4},{4,8},{8,12},{1,5},{5,9},{9,13},{2,6},{6,10},{10,14},{3,7},{... | collective-permute-start | bytes 1572872 | tf_op jit(solution)/shard_map/ppermute | solution.py:103
  12.0 2.0 collective-permute-start.12
  14.4 2.8 %convolution_convert_fusion.4 = bf16[512,1024]{1,0:T(8,128)(2,1)} fusion(bf16[512,512]{1,0:T(8,128)(2,1)} %get-tuple-element.37, bf16[512,1024]{1,0:T(8,128)(2,1)S(1)} %copy-done.4, pred[512]{0:T(512)(128)(4,1)S(1)} %subtract_compare_fusion), kind=kOutput, calls=%fused_computation.13 | convolution fusion | flops 537919488 | bytes 2621952 | tf_op jit(solution)/shard_map/dot_general | solution.py:13
  17.2 8.3 %convolution_convert_fusion = bf16[512,4096]{1,0:T(8,128)(2,1)S(1)} fusion(bf16[4096,1024]{1,0:T(8,128)(2,1)} %param.8, bf16[512,1024]{1,0:T(8,128)(2,1)S(1)} %copy-done.4, pred[512]{0:T(512)(128)(4,1)S(1)} %subtract_compare_fusion), kind=kOutput, calls=%fused_computation | convolution fusion | flops 4297588736 | bytes 13632000 | tf_op jit(solution)/shard_map/dot_general | solution.py:13
  25.5 1.8 fusion.20
  29.0 2.3 %constant_dynamic-slice_fusion.1 = (bf16[256,1024]{1,0:T(8,128)(2,1)}, bf16[256,1024]{1,0:T(8,128)(2,1)}) fusion(bf16[256,4096]{1,0:T(8,128)(2,1)} %get-tuple-element.39, s32[]{:T(128)S(6)} %select_n.364, s32[]{:T(128)S(6)} %select_n.367), kind=kLoop, calls=%fused_computation.94 | loop fusion | bytes 2097160 | tf_op jit(solution)/shard_map/dynamic_slice | solution.py:194
  36.4 1.8 collective-permute-start.15
  38.2 2.9 %collective-permute-start.16 = (bf16[2,16,512]{2,1,0:T(8,128)(2,1)}, bf16[2,16,512]{2,1,0:T(8,128)(2,1)}, u32[]{:S(2)}, u32[]{:S(2)}) collective-permute-start(bf16[2,16,512]{2,1,0:T(8,128)(2,1)} %pad_maximum_fusion.6), channel_id=1, source_target_pairs={{0,12},{4,0},{8,4},{12,8},{1,13},{5,1},{9,5},{13,9},{2,14},{6,2},{... | collective-permute-start | bytes 98312 | tf_op jit(solution)/shard_map/ppermute | solution.py:144
  43.6 4.6 %collective-permute-start.2 = (bf16[512,512]{1,0:T(8,128)(2,1)}, bf16[512,512]{1,0:T(8,128)(2,1)S(1)}, u32[]{:S(2)}, u32[]{:S(2)}) collective-permute-start(bf16[512,512]{1,0:T(8,128)(2,1)} %get-tuple-element.35), channel_id=1, source_target_pairs={{0,4},{4,8},{8,12},{1,5},{5,9},{9,13},{2,6},{6,10},{10,14},{3,7},{... | collective-permute-start | bytes 1572872 | tf_op jit(solution)/shard_map/ppermute | solution.py:103
  52.4 2.1 collective-permute-start.17
  55.8 2.0 convolution_convert_fusion.3
  57.8 2.2 fusion.7
  63.0 9.0 %collective-permute-done.17 = bf16[256,1024]{1,0:T(8,128)(2,1)S(1)} collective-permute-done((bf16[256,1024]{1,0:T(8,128)(2,1)S(1)}, bf16[256,1024]{1,0:T(8,128)(2,1)S(1)}, u32[]{:S(2)}, u32[]{:S(2)}) %collective-permute-start.17) | collective-permute-done | bytes 524320 | tf_op jit(solution)/shard_map/ppermute | solution.py:103
  78.2 11.2 %collective-permute-done.5 = bf16[512,512]{1,0:T(8,128)(2,1)S(1)} collective-permute-done((bf16[512,512]{1,0:T(8,128)(2,1)}, bf16[512,512]{1,0:T(8,128)(2,1)S(1)}, u32[]{:S(2)}, u32[]{:S(2)}) %collective-permute-start.5) | collective-permute-done | bytes 524320 | tf_op jit(solution)/shard_map/ppermute | solution.py:106
  89.9 2.1 constant_dynamic-update-slice_fusion.19
  93.7 1.6 collective-permute-start.35
  95.3 8.8 %collective-permute-done.32 = bf16[256,1024]{1,0:T(8,128)(2,1)S(1)} collective-permute-done((bf16[256,1024]{1,0:T(8,128)(2,1)S(1)}, bf16[256,1024]{1,0:T(8,128)(2,1)S(1)}, u32[]{:S(2)}, u32[]{:S(2)}) %collective-permute-start.32) | collective-permute-done | bytes 524320 | tf_op jit(solution)/shard_map/ppermute | solution.py:109
  108.9 6.5 %collective-permute-done.35 = bf16[256,1024]{1,0:T(8,128)(2,1)S(1)} collective-permute-done((bf16[256,1024]{1,0:T(8,128)(2,1)S(1)}, bf16[256,1024]{1,0:T(8,128)(2,1)S(1)}, u32[]{:S(2)}, u32[]{:S(2)}) %collective-permute-start.35) | collective-permute-done | bytes 524320 | tf_op jit(solution)/shard_map/ppermute | solution.py:109
  115.6 5.8 %collective-permute-done.9 = bf16[512,512]{1,0:T(8,128)(2,1)S(1)} collective-permute-done((bf16[512,512]{1,0:T(8,128)(2,1)S(1)}, bf16[512,512]{1,0:T(8,128)(2,1)S(1)}, u32[]{:S(2)}, u32[]{:S(2)}) %collective-permute-start.9) | collective-permute-done | bytes 524320 | tf_op jit(solution)/shard_map/ppermute | solution.py:106
  124.2 11.6 %collective-permute-done.37 = bf16[256,1024]{1,0:T(8,128)(2,1)S(1)} collective-permute-done((bf16[256,1024]{1,0:T(8,128)(2,1)S(1)}, bf16[256,1024]{1,0:T(8,128)(2,1)S(1)}, u32[]{:S(2)}, u32[]{:S(2)}) %collective-permute-start.37) | collective-permute-done | bytes 524320 | tf_op jit(solution)/shard_map/ppermute | solution.py:109
  140.6 10.7 %collective-permute-done.40 = bf16[256,1024]{1,0:T(8,128)(2,1)S(1)} collective-permute-done((bf16[256,1024]{1,0:T(8,128)(2,1)S(1)}, bf16[256,1024]{1,0:T(8,128)(2,1)S(1)}, u32[]{:S(2)}, u32[]{:S(2)}) %collective-permute-start.40) | collective-permute-done | bytes 524320 | tf_op jit(solution)/shard_map/ppermute | solution.py:109
  158.6 2.3 %collective-permute-start.24 = (bf16[256,1024]{1,0:T(8,128)(2,1)S(1)}, bf16[256,1024]{1,0:T(8,128)(2,1)S(1)}, u32[]{:S(2)}, u32[]{:S(2)}) collective-permute-start(bf16[256,1024]{1,0:T(8,128)(2,1)S(1)} %add_convert_fusion.15), channel_id=1, source_target_pairs={{0,4},{4,8},{1,5},{5,9},{2,6},{6,10},{3,7},{7,11},{16,20},{20,24},... | collective-permute-start | bytes 1572872 | tf_op jit(solution)/shard_map/ppermute | solution.py:103
  161.0 7.1 %collective-permute-done.42 = bf16[256,1024]{1,0:T(8,128)(2,1)S(1)} collective-permute-done((bf16[256,1024]{1,0:T(8,128)(2,1)S(1)}, bf16[256,1024]{1,0:T(8,128)(2,1)S(1)}, u32[]{:S(2)}, u32[]{:S(2)}) %collective-permute-start.42) | collective-permute-done | bytes 524320 | tf_op jit(solution)/shard_map/ppermute | solution.py:109
  168.3 1.6 collective-permute-start.45
  171.2 9.4 %collective-permute-done.24 = bf16[256,1024]{1,0:T(8,128)(2,1)S(1)} collective-permute-done((bf16[256,1024]{1,0:T(8,128)(2,1)S(1)}, bf16[256,1024]{1,0:T(8,128)(2,1)S(1)}, u32[]{:S(2)}, u32[]{:S(2)}) %collective-permute-start.24) | collective-permute-done | bytes 524320 | tf_op jit(solution)/shard_map/ppermute | solution.py:103
  184.0 4.1 %collective-permute-start.19 = (bf16[256,1024]{1,0:T(8,128)(2,1)S(1)}, bf16[256,1024]{1,0:T(8,128)(2,1)S(1)}, u32[]{:S(2)}, u32[]{:S(2)}) collective-permute-start(bf16[256,1024]{1,0:T(8,128)(2,1)S(1)} %get-tuple-element.40), channel_id=1, source_target_pairs={{0,4},{4,8},{8,12},{1,5},{5,9},{9,13},{2,6},{6,10},{10,14},{3,7},{... | collective-permute-start | bytes 1572872 | tf_op jit(solution)/shard_map/ppermute | solution.py:103
  188.1 4.6 %collective-permute-start.25 = (bf16[256,1024]{1,0:T(8,128)(2,1)S(1)}, bf16[256,1024]{1,0:T(8,128)(2,1)S(1)}, u32[]{:S(2)}, u32[]{:S(2)}) collective-permute-start(bf16[256,1024]{1,0:T(8,128)(2,1)S(1)} %get-tuple-element.44), channel_id=1, source_target_pairs={{0,4},{4,8},{8,12},{1,5},{5,9},{9,13},{2,6},{6,10},{10,14},{3,7},{... | collective-permute-start | bytes 1572872 | tf_op jit(solution)/shard_map/ppermute | solution.py:103
  196.6 10.1 %select_convert_fusion = bf16[512,1024]{1,0:T(8,128)(2,1)} fusion(bf16[512,1024]{1,0:T(8,128)(2,1)S(1)} %multiply_convert_fusion.1, bf16[512,4096]{1,0:T(8,128)(2,1)} %get-tuple-element.26, bf16[4096,1024]{1,0:T(8,128)(2,1)} %param.8, pred[512]{0:T(512)(128)(4,1)S(1)} %copy-done.17), kind=kOutput, calls=%fused_computation.8 | convolution fusion | flops 4297064448 | bytes 14680576 | tf_op jit(solution)/shard_map/dot_general | solution.py:13
  206.7 3.0 %collective-permute-done.47 = bf16[256,1024]{1,0:T(8,128)(2,1)S(1)} collective-permute-done((bf16[256,1024]{1,0:T(8,128)(2,1)S(1)}, bf16[256,1024]{1,0:T(8,128)(2,1)S(1)}, u32[]{:S(2)}, u32[]{:S(2)}) %collective-permute-start.47) | collective-permute-done | bytes 524320 | tf_op jit(solution)/shard_map/ppermute | solution.py:109
  211.1 8.6 %collective-permute-done.28 = bf16[256,1024]{1,0:T(8,128)(2,1)S(1)} collective-permute-done((bf16[256,1024]{1,0:T(8,128)(2,1)S(1)}, bf16[256,1024]{1,0:T(8,128)(2,1)S(1)}, u32[]{:S(2)}, u32[]{:S(2)}) %collective-permute-start.28) | collective-permute-done | bytes 524320 | tf_op jit(solution)/shard_map/ppermute | solution.py:106
  222.0 3.4 %copy-done.2 = bf16[4096,1024]{1,0:T(8,128)(2,1)} copy-done((bf16[4096,1024]{1,0:T(8,128)(2,1)}, bf16[4096,1024]{1,0:T(8,128)(2,1)S(1)}, u32[]{:S(2)}) %copy-start.2) | copy-done | bytes 8388632
  (190 shorter events, 60.7 us)
Async XLA Ops:
  4.3 48.1 %collective-permute-start.1 = (bf16[512,512]{1,0:T(8,128)(2,1)}, bf16[512,512]{1,0:T(8,128)(2,1)}, u32[]{:S(2)}, u32[]{:S(2)}) collective-permute-start(bf16[512,512]{1,0:T(8,128)(2,1)} %get-tuple-element.37), channel_id=1, source_target_pairs={{4,0},{8,4},{12,8},{5,1},{9,5},{13,9},{6,2},{10,6},{14,10},{7,3},{... | collective-permute-start | bytes 1572872 | tf_op jit(solution)/shard_map/ppermute | solution.py:106
  5.6 48.9 %collective-permute-start = (bf16[512,512]{1,0:T(8,128)(2,1)}, bf16[512,512]{1,0:T(8,128)(2,1)}, u32[]{:S(2)}, u32[]{:S(2)}) collective-permute-start(bf16[512,512]{1,0:T(8,128)(2,1)} %get-tuple-element.37), channel_id=1, source_target_pairs={{0,4},{4,8},{8,12},{1,5},{5,9},{9,13},{2,6},{6,10},{10,14},{3,7},{... | collective-permute-start | bytes 1572872 | tf_op jit(solution)/shard_map/ppermute | solution.py:103
  12.0 17.0 %collective-permute-start.12 = (bf16[64,1024]{1,0:T(8,128)(2,1)S(1)}, bf16[64,1024]{1,0:T(8,128)(2,1)S(1)}, u32[]{:S(2)}, u32[]{:S(2)}) collective-permute-start(bf16[64,1024]{1,0:T(8,128)(2,1)S(1)} %fusion.6), channel_id=1, source_target_pairs={{0,2},{2,0},{1,3},{3,1},{4,6},{6,4},{5,7},{7,5},{8,10},{10,8},{9,1... | collective-permute-start | bytes 393224 | tf_op jit(solution)/shard_map/ppermute | solution.py:109
  42.1 19.0 %collective-permute-start.3 = (bf16[512,512]{1,0:T(8,128)(2,1)}, bf16[512,512]{1,0:T(8,128)(2,1)S(1)}, u32[]{:S(2)}, u32[]{:S(2)}) collective-permute-start(bf16[512,512]{1,0:T(8,128)(2,1)} %get-tuple-element.35), channel_id=1, source_target_pairs={{4,0},{8,4},{12,8},{5,1},{9,5},{13,9},{6,2},{10,6},{14,10},{7,3},{... | collective-permute-start | bytes 1572872 | tf_op jit(solution)/shard_map/ppermute | solution.py:106
  43.6 17.9 %collective-permute-start.2 = (bf16[512,512]{1,0:T(8,128)(2,1)}, bf16[512,512]{1,0:T(8,128)(2,1)S(1)}, u32[]{:S(2)}, u32[]{:S(2)}) collective-permute-start(bf16[512,512]{1,0:T(8,128)(2,1)} %get-tuple-element.35), channel_id=1, source_target_pairs={{0,4},{4,8},{8,12},{1,5},{5,9},{9,13},{2,6},{6,10},{10,14},{3,7},{... | collective-permute-start | bytes 1572872 | tf_op jit(solution)/shard_map/ppermute | solution.py:103
  52.4 19.5 %collective-permute-start.17 = (bf16[256,1024]{1,0:T(8,128)(2,1)S(1)}, bf16[256,1024]{1,0:T(8,128)(2,1)S(1)}, u32[]{:S(2)}, u32[]{:S(2)}) collective-permute-start(bf16[256,1024]{1,0:T(8,128)(2,1)S(1)} %copy-done.10), channel_id=1, source_target_pairs={{0,4},{1,5},{2,6},{3,7},{16,20},{17,21},{18,22},{19,23}} | collective-permute-start | bytes 1572872 | tf_op jit(solution)/shard_map/ppermute | solution.py:103
  54.5 83.1 %collective-permute-start.23 = (bf16[256,1024]{1,0:T(8,128)(2,1)S(1)}, bf16[256,1024]{1,0:T(8,128)(2,1)S(1)}, u32[]{:S(2)}, u32[]{:S(2)}) collective-permute-start(bf16[256,1024]{1,0:T(8,128)(2,1)S(1)} %copy-done.9), channel_id=1, source_target_pairs={{0,4},{1,5},{2,6},{3,7},{16,20},{17,21},{18,22},{19,23}} | collective-permute-start | bytes 1572872 | tf_op jit(solution)/shard_map/ppermute | solution.py:103
  61.1 30.9 %collective-permute-start.34 = (bf16[512,1024]{1,0:T(8,128)(2,1)S(1)}, bf16[512,1024]{1,0:T(8,128)(2,1)S(1)}, u32[]{:S(2)}, u32[]{:S(2)}) collective-permute-start(bf16[512,1024]{1,0:T(8,128)(2,1)S(1)} %convolution_convert_fusion.3), channel_id=1, source_target_pairs={{0,1},{1,0},{2,3},{3,2},{4,5},{5,4},{6,7},{7,6},{8,9},{9,8},{10,11... | collective-permute-start | bytes 3145736 | tf_op jit(solution)/shard_map/ppermute | solution.py:112
  72.0 17.4 %collective-permute-start.5 = (bf16[512,512]{1,0:T(8,128)(2,1)}, bf16[512,512]{1,0:T(8,128)(2,1)S(1)}, u32[]{:S(2)}, u32[]{:S(2)}) collective-permute-start(bf16[512,512]{1,0:T(8,128)(2,1)} %collective-permute-done.1), channel_id=1, source_target_pairs={{4,0},{8,4},{5,1},{9,5},{6,2},{10,6},{7,3},{11,7},{20,16},{24,20},... | collective-permute-start | bytes 1572872 | tf_op jit(solution)/shard_map/ppermute | solution.py:106
  73.5 15.9 %collective-permute-start.4 = (bf16[512,512]{1,0:T(8,128)(2,1)}, bf16[512,512]{1,0:T(8,128)(2,1)S(1)}, u32[]{:S(2)}, u32[]{:S(2)}) collective-permute-start(bf16[512,512]{1,0:T(8,128)(2,1)} %collective-permute-done), channel_id=1, source_target_pairs={{4,8},{8,12},{5,9},{9,13},{6,10},{10,14},{7,11},{11,15},{20,24},{2... | collective-permute-start | bytes 1572872 | tf_op jit(solution)/shard_map/ppermute | solution.py:103
  75.5 29.7 %collective-permute-start.7 = (bf16[512,512]{1,0:T(8,128)(2,1)S(1)}, bf16[512,512]{1,0:T(8,128)(2,1)S(1)}, u32[]{:S(2)}, u32[]{:S(2)}) collective-permute-start(bf16[512,512]{1,0:T(8,128)(2,1)S(1)} %collective-permute-done.3), channel_id=1, source_target_pairs={{4,0},{8,4},{5,1},{9,5},{6,2},{10,6},{7,3},{11,7},{20,16},{24,20},... | collective-permute-start | bytes 1572872 | tf_op jit(solution)/shard_map/ppermute | solution.py:106
  89.4 14.7 %collective-permute-start.32 = (bf16[256,1024]{1,0:T(8,128)(2,1)S(1)}, bf16[256,1024]{1,0:T(8,128)(2,1)S(1)}, u32[]{:S(2)}, u32[]{:S(2)}) collective-permute-start(bf16[256,1024]{1,0:T(8,128)(2,1)S(1)} %get-tuple-element.51), channel_id=1, source_target_pairs={{0,2},{2,0},{1,3},{3,1},{4,6},{6,4},{5,7},{7,5},{8,10},{10,8},{9,1... | collective-permute-start | bytes 1572872 | tf_op jit(solution)/shard_map/ppermute | solution.py:109
  92.0 14.6 %collective-permute-start.6 = (bf16[512,512]{1,0:T(8,128)(2,1)S(1)}, bf16[512,512]{1,0:T(8,128)(2,1)S(1)}, u32[]{:S(2)}, u32[]{:S(2)}) collective-permute-start(bf16[512,512]{1,0:T(8,128)(2,1)S(1)} %collective-permute-done.2), channel_id=1, source_target_pairs={{4,8},{8,12},{5,9},{9,13},{6,10},{10,14},{7,11},{11,15},{20,24},{2... | collective-permute-start | bytes 1572872 | tf_op jit(solution)/shard_map/ppermute | solution.py:103
  93.7 21.6 %collective-permute-start.35 = (bf16[256,1024]{1,0:T(8,128)(2,1)S(1)}, bf16[256,1024]{1,0:T(8,128)(2,1)S(1)}, u32[]{:S(2)}, u32[]{:S(2)}) collective-permute-start(bf16[256,1024]{1,0:T(8,128)(2,1)S(1)} %split.63), channel_id=1, source_target_pairs={{0,2},{2,0},{1,3},{3,1},{4,6},{6,4},{5,7},{7,5},{8,10},{10,8},{9,1... | collective-permute-start | bytes 1572872 | tf_op jit(solution)/shard_map/ppermute | solution.py:109
  105.2 16.2 %collective-permute-start.9 = (bf16[512,512]{1,0:T(8,128)(2,1)S(1)}, bf16[512,512]{1,0:T(8,128)(2,1)S(1)}, u32[]{:S(2)}, u32[]{:S(2)}) collective-permute-start(bf16[512,512]{1,0:T(8,128)(2,1)S(1)} %collective-permute-done.5), channel_id=1, source_target_pairs={{4,0},{5,1},{6,2},{7,3},{20,16},{21,17},{22,18},{23,19}} | collective-permute-start | bytes 1572872 | tf_op jit(solution)/shard_map/ppermute | solution.py:106
  106.5 14.9 %collective-permute-start.8 = (bf16[512,512]{1,0:T(8,128)(2,1)S(1)}, bf16[512,512]{1,0:T(8,128)(2,1)S(1)}, u32[]{:S(2)}, u32[]{:S(2)}) collective-permute-start(bf16[512,512]{1,0:T(8,128)(2,1)S(1)} %collective-permute-done.4), channel_id=1, source_target_pairs={{8,12},{9,13},{10,14},{11,15},{24,28},{25,29},{26,30},{27,31}} | collective-permute-start | bytes 1572872 | tf_op jit(solution)/shard_map/ppermute | solution.py:103
  108.3 30.8 %collective-permute-start.50 = (bf16[64,1024]{1,0:T(8,128)(2,1)S(1)}, bf16[64,1024]{1,0:T(8,128)(2,1)S(1)}, u32[]{:S(2)}, u32[]{:S(2)}) collective-permute-start(bf16[64,1024]{1,0:T(8,128)(2,1)S(1)} %split.83), channel_id=1, source_target_pairs={{0,2},{2,0},{1,3},{3,1},{4,6},{6,4},{5,7},{7,5},{8,10},{10,8},{9,1... | collective-permute-start | bytes 393224 | tf_op jit(solution)/shard_map/ppermute | solution.py:109
  115.3 20.8 %collective-permute-start.39 = (bf16[512,1024]{1,0:T(8,128)(2,1)S(1)}, bf16[512,1024]{1,0:T(8,128)(2,1)S(1)}, u32[]{:S(2)}, u32[]{:S(2)}) collective-permute-start(bf16[512,1024]{1,0:T(8,128)(2,1)S(1)} %convolution_convert_fusion.2), channel_id=1, source_target_pairs={{0,1},{1,0},{2,3},{3,2},{4,5},{5,4},{6,7},{7,6},{8,9},{9,8},{10,11... | collective-permute-start | bytes 3145736 | tf_op jit(solution)/shard_map/ppermute | solution.py:112
  123.9 32.4 %collective-permute-start.44 = (bf16[512,1024]{1,0:T(8,128)(2,1)S(1)}, bf16[512,1024]{1,0:T(8,128)(2,1)S(1)}, u32[]{:S(2)}, u32[]{:S(2)}) collective-permute-start(bf16[512,1024]{1,0:T(8,128)(2,1)S(1)} %convolution_convert_fusion.1), channel_id=1, source_target_pairs={{0,1},{1,0},{2,3},{3,2},{4,5},{5,4},{6,7},{7,6},{8,9},{9,8},{10,11... | collective-permute-start | bytes 3145736 | tf_op jit(solution)/shard_map/ppermute | solution.py:112
  137.0 14.4 %collective-permute-start.40 = (bf16[256,1024]{1,0:T(8,128)(2,1)S(1)}, bf16[256,1024]{1,0:T(8,128)(2,1)S(1)}, u32[]{:S(2)}, u32[]{:S(2)}) collective-permute-start(bf16[256,1024]{1,0:T(8,128)(2,1)S(1)} %split.65), channel_id=1, source_target_pairs={{0,2},{2,0},{1,3},{3,1},{4,6},{6,4},{5,7},{7,5},{8,10},{10,8},{9,1... | collective-permute-start | bytes 1572872 | tf_op jit(solution)/shard_map/ppermute | solution.py:109
  137.8 15.9 %collective-permute-start.11 = (bf16[512,512]{1,0:T(8,128)(2,1)S(1)}, bf16[512,512]{1,0:T(8,128)(2,1)S(1)}, u32[]{:S(2)}, u32[]{:S(2)}) collective-permute-start(bf16[512,512]{1,0:T(8,128)(2,1)S(1)} %collective-permute-done.7), channel_id=1, source_target_pairs={{4,0},{5,1},{6,2},{7,3},{20,16},{21,17},{22,18},{23,19}} | collective-permute-start | bytes 1572872 | tf_op jit(solution)/shard_map/ppermute | solution.py:106
  139.1 14.6 %collective-permute-start.10 = (bf16[512,512]{1,0:T(8,128)(2,1)S(1)}, bf16[512,512]{1,0:T(8,128)(2,1)S(1)}, u32[]{:S(2)}, u32[]{:S(2)}) collective-permute-start(bf16[512,512]{1,0:T(8,128)(2,1)S(1)} %collective-permute-done.6), channel_id=1, source_target_pairs={{8,12},{9,13},{10,14},{11,15},{24,28},{25,29},{26,30},{27,31}} | collective-permute-start | bytes 1572872 | tf_op jit(solution)/shard_map/ppermute | solution.py:103
  139.9 28.4 %collective-permute-start.20 = (bf16[256,1024]{1,0:T(8,128)(2,1)S(1)}, bf16[256,1024]{1,0:T(8,128)(2,1)S(1)}, u32[]{:S(2)}, u32[]{:S(2)}) collective-permute-start(bf16[256,1024]{1,0:T(8,128)(2,1)S(1)} %copy-done.8), channel_id=1, source_target_pairs={{12,8},{13,9},{14,10},{15,11},{28,24},{29,25},{30,26},{31,27}} | collective-permute-start | bytes 1572872 | tf_op jit(solution)/shard_map/ppermute | solution.py:106
  151.4 19.2 %collective-permute-start.26 = (bf16[256,1024]{1,0:T(8,128)(2,1)S(1)}, bf16[256,1024]{1,0:T(8,128)(2,1)S(1)}, u32[]{:S(2)}, u32[]{:S(2)}) collective-permute-start(bf16[256,1024]{1,0:T(8,128)(2,1)S(1)} %copy-done.7), channel_id=1, source_target_pairs={{12,8},{13,9},{14,10},{15,11},{28,24},{29,25},{30,26},{31,27}} | collective-permute-start | bytes 1572872 | tf_op jit(solution)/shard_map/ppermute | solution.py:106
  158.6 22.0 %collective-permute-start.24 = (bf16[256,1024]{1,0:T(8,128)(2,1)S(1)}, bf16[256,1024]{1,0:T(8,128)(2,1)S(1)}, u32[]{:S(2)}, u32[]{:S(2)}) collective-permute-start(bf16[256,1024]{1,0:T(8,128)(2,1)S(1)} %add_convert_fusion.15), channel_id=1, source_target_pairs={{0,4},{4,8},{1,5},{5,9},{2,6},{6,10},{3,7},{7,11},{16,20},{20,24},... | collective-permute-start | bytes 1572872 | tf_op jit(solution)/shard_map/ppermute | solution.py:103
  168.1 15.0 %collective-permute-start.51 = (f32[64,1024]{1,0:T(8,128)S(1)}, f32[64,1024]{1,0:T(8,128)S(1)}, u32[]{:S(2)}, u32[]{:S(2)}) collective-permute-start(f32[64,1024]{1,0:T(8,128)S(1)} %slice_add_fusion), channel_id=1, source_target_pairs={{0,1},{1,0},{2,3},{3,2},{4,5},{5,4},{6,7},{7,6},{8,9},{9,8},{10,11... | collective-permute-start | bytes 786440 | tf_op jit(solution)/shard_map/ppermute | solution.py:112
  168.3 14.4 %collective-permute-start.45 = (bf16[256,1024]{1,0:T(8,128)(2,1)S(1)}, bf16[256,1024]{1,0:T(8,128)(2,1)S(1)}, u32[]{:S(2)}, u32[]{:S(2)}) collective-permute-start(bf16[256,1024]{1,0:T(8,128)(2,1)S(1)} %split.67), channel_id=1, source_target_pairs={{0,2},{2,0},{1,3},{3,1},{4,6},{6,4},{5,7},{7,5},{8,10},{10,8},{9,1... | collective-permute-start | bytes 1572872 | tf_op jit(solution)/shard_map/ppermute | solution.py:109
  170.5 22.1 %collective-permute-start.21 = (bf16[256,1024]{1,0:T(8,128)(2,1)S(1)}, bf16[256,1024]{1,0:T(8,128)(2,1)S(1)}, u32[]{:S(2)}, u32[]{:S(2)}) collective-permute-start(bf16[256,1024]{1,0:T(8,128)(2,1)S(1)} %get-tuple-element.41), channel_id=1, source_target_pairs={{8,4},{12,8},{9,5},{13,9},{10,6},{14,10},{11,7},{15,11},{24,20},{2... | collective-permute-start | bytes 1572872 | tf_op jit(solution)/shard_map/ppermute | solution.py:106
  184.0 26.1 %collective-permute-start.19 = (bf16[256,1024]{1,0:T(8,128)(2,1)S(1)}, bf16[256,1024]{1,0:T(8,128)(2,1)S(1)}, u32[]{:S(2)}, u32[]{:S(2)}) collective-permute-start(bf16[256,1024]{1,0:T(8,128)(2,1)S(1)} %get-tuple-element.40), channel_id=1, source_target_pairs={{0,4},{4,8},{8,12},{1,5},{5,9},{9,13},{2,6},{6,10},{10,14},{3,7},{... | collective-permute-start | bytes 1572872 | tf_op jit(solution)/shard_map/ppermute | solution.py:103
  188.1 23.0 %collective-permute-start.25 = (bf16[256,1024]{1,0:T(8,128)(2,1)S(1)}, bf16[256,1024]{1,0:T(8,128)(2,1)S(1)}, u32[]{:S(2)}, u32[]{:S(2)}) collective-permute-start(bf16[256,1024]{1,0:T(8,128)(2,1)S(1)} %get-tuple-element.44), channel_id=1, source_target_pairs={{0,4},{4,8},{8,12},{1,5},{5,9},{9,13},{2,6},{6,10},{10,14},{3,7},{... | collective-permute-start | bytes 1572872 | tf_op jit(solution)/shard_map/ppermute | solution.py:103
  192.9 18.2 %collective-permute-start.22 = (bf16[256,1024]{1,0:T(8,128)(2,1)S(1)}, bf16[256,1024]{1,0:T(8,128)(2,1)S(1)}, u32[]{:S(2)}, u32[]{:S(2)}) collective-permute-start(bf16[256,1024]{1,0:T(8,128)(2,1)S(1)} %add_convert_fusion.16), channel_id=1, source_target_pairs={{4,0},{8,4},{12,8},{5,1},{9,5},{13,9},{6,2},{10,6},{14,10},{7,3},{... | collective-permute-start | bytes 1572872 | tf_op jit(solution)/shard_map/ppermute | solution.py:106
  194.4 25.4 %collective-permute-start.28 = (bf16[256,1024]{1,0:T(8,128)(2,1)S(1)}, bf16[256,1024]{1,0:T(8,128)(2,1)S(1)}, u32[]{:S(2)}, u32[]{:S(2)}) collective-permute-start(bf16[256,1024]{1,0:T(8,128)(2,1)S(1)} %add_convert_fusion.12), channel_id=1, source_target_pairs={{4,0},{8,4},{12,8},{5,1},{9,5},{13,9},{6,2},{10,6},{14,10},{7,3},{... | collective-permute-start | bytes 1572872 | tf_op jit(solution)/shard_map/ppermute | solution.py:106
  (40 other events, 374.0 us)

commit v2 on v1

v2 whole, which is shorter than its diff:
```python
import functools

import jax
import jax.numpy as jnp
from jax import lax
from jax.experimental import pallas as pl
from jax.experimental.pallas import tpu as pltpu
from jax.sharding import PartitionSpec as P

BLOCK_ROWS = 128
SCALE = 2.0
F32 = jnp.float32
B16 = jnp.bfloat16


def dot(a, b, ca, cb):
    return lax.dot_general(a, b, (((ca,), (cb,)), ((), ())), preferred_element_type=F32)


def lookup(source, position):
    match_mask = position[..., None] == jnp.arange(source.shape[0], dtype=jnp.int32)
    return jnp.sum(jnp.where(match_mask, source, 0), axis=-1)


def layout(tenant_row_counts, row_ids):
    block_count = (tenant_row_counts + BLOCK_ROWS - 1) // BLOCK_ROWS
    segment_offset = jnp.cumsum(block_count) - block_count
    block_ids = row_ids // BLOCK_ROWS
    tenant_of = (
        jnp.sum((segment_offset[None, :] <= block_ids[:, None]).astype(jnp.int32), axis=1) - 1
    )
    offset = row_ids - BLOCK_ROWS * lookup(segment_offset, tenant_of)
    return tenant_of, offset < lookup(tenant_row_counts, tenant_of)


def rank_partials(maps, rows, mask, slots):
    every = dot(maps, rows, 1, 1)
    every = every.reshape(slots, -1, rows.shape[0])
    return jnp.sum(jnp.where(mask[:, None, :], every, 0.0), axis=0)


def spread(values, mask):
    wide = jnp.where(mask[:, None, :], values[None], jnp.zeros((), values.dtype))
    return wide.reshape(-1, values.shape[-1])


def shards_general(tokens, weight, down_maps, up_maps, counts, slot_of, cotangent):
    rows, width = tokens.shape
    held, _, rank = down_maps.shape
    slots = held * lax.axis_size("tenant")
    owner = lax.axis_index("tenant")
    row_ids = lax.axis_index(("tenant", "dp")) * rows + jnp.arange(rows, dtype=jnp.int32)
    tenant, live = layout(counts, row_ids)
    slot = lookup(slot_of, tenant)
    mask = slot[None, :] == jnp.arange(slots, dtype=jnp.int32)[:, None]
    grads = jnp.where(live[:, None], cotangent, jnp.zeros_like(cotangent))
    kept = jnp.where(live[:, None], tokens, jnp.zeros_like(tokens))
    down = lax.all_gather(jnp.swapaxes(down_maps, 1, 2), "tenant", axis=0, tiled=True)
    up = lax.all_gather(up_maps, "tenant", axis=0, tiled=True)
    down, up = down.reshape(-1, width), up.reshape(-1, width)
    gathered = lax.all_gather(kept, "tensor", axis=1, tiled=True)
    part = jnp.stack(
        [rank_partials(down, kept, mask, slots), rank_partials(up, grads, mask, slots)]
    )
    low, back = lax.psum(part.astype(B16), "tensor")
    low, back = spread(low, mask), spread(back, mask)
    base = dot(gathered, weight, 1, 0)
    query = (base + (SCALE * dot(low, up, 0, 0)).astype(B16).astype(F32)).astype(B16)
    term = dot(grads, weight, 1, 1).astype(B16)
    summed = lax.psum_scatter(term, "tensor", scatter_dimension=1, tiled=True).astype(F32)
    lora = (SCALE * dot(back, down, 0, 0)).astype(B16).astype(F32)
    token_grad = jnp.where(live[:, None], summed + lora, 0.0).astype(B16)
    axes = ("tenant", "dp")
    weight_grad = lax.psum(dot(gathered, grads, 0, 0).astype(B16), axes)
    maps = jnp.stack([SCALE * dot(back, kept, 1, 0), SCALE * dot(low, grads, 1, 0)])
    maps = lax.psum(maps.astype(B16), axes).astype(F32).reshape(2, slots, rank, width)
    maps = lax.dynamic_slice_in_dim(maps, owner * held, held, 1)
    return query, token_grad, weight_grad, jnp.swapaxes(maps[0], 1, 2), maps[1]


def arrival_plan(n):
    plan = [[] for _ in range(n - 1)]
    for z in range(n):
        seen = []
        for t in range(1, n):
            if z - t >= 0:
                seen.append((t, 0, z - t))
            if z + t < n:
                seen.append((t, 1, z + t))
        for step, entry in enumerate(seen):
            plan[step].append(entry)
    return plan


def whole(array):
    return pl.BlockSpec(array.shape, lambda *_: (0,) * array.ndim)


def call(body, table, grid, arrays, specs, outs, out_specs, scratch, flops, aliases=None):
    moved = sum(v.size * v.dtype.itemsize for v in arrays)
    return pl.pallas_call(
        body,
        grid_spec=pltpu.PrefetchScalarGridSpec(
            num_scalar_prefetch=1,
            grid=grid,
            in_specs=specs,
            out_specs=out_specs,
            scratch_shapes=scratch,
        ),
        out_shape=outs,
        input_output_aliases=aliases or {},
        compiler_params=pltpu.CompilerParams(vmem_limit_bytes=48 * 1024 * 1024),
        cost_estimate=pl.CostEstimate(flops=1, bytes_accessed=1, transcendentals=0),
    )(table, *arrays)


def hop_body(table, grads, weight, came, away, goes, share):
    share[...] = away[...]

    @pl.when(table[1] == 0)
    def _():
        goes[...] = came[...]

    @pl.when(table[1] != 0)
    def _():
        term = dot(grads[...], weight[...], 1, 1)
        goes[...] = (term + came[...].astype(F32)).astype(B16)


def hop(table, grads, weight, came):
    rows, width = came.shape
    half = width // 2
    cols = pl.BlockSpec((rows, half), lambda j, t: (0, j))
    return call(
        hop_body,
        table,
        (2,),
        [grads, weight, came, came],
        [
            whole(grads),
            pl.BlockSpec((half, width), lambda j, t: (2 * t[0] + j, 0)),
            cols,
            pl.BlockSpec((rows, half), lambda j, t: (0, t[2])),
        ],
        [jax.ShapeDtypeStruct((rows, width), B16), jax.ShapeDtypeStruct((rows, half), B16)],
        [cols, pl.BlockSpec((rows, half), lambda j, t: (0, 0))],
        [],
        0,
    )


def copy_chosen(choice, offers, target):
    if len(offers) == 1:
        target[...] = offers[0][...]
        return
    for at, offer in enumerate(offers):

        @pl.when(choice == at)
        def _(offer=offer):
            target[...] = offer[...]


def half_spec(array, half, core_at):
    if array.shape[1] == half:
        return whole(array)
    return pl.BlockSpec((array.shape[0], half), lambda j, t: (0, t[core_at]))


def piece_body(count, table, *refs):
    ours, theirs = refs[:count], refs[count : 2 * count]
    grads, their_grads, out, a, b = refs[2 * count :]

    @pl.when(pl.program_id(0) == 0)
    def _():
        copy_chosen(table[0], ours, a)
        copy_chosen(table[0], theirs, b)

    out[...] = (
        dot(a[...], grads[...], 0, 0) + dot(b[...], their_grads[...], 0, 0)
    ).astype(B16)


def piece(table, ours, theirs, grads, their_grads):
    rows, width = grads.shape
    half = width // 2
    cols = pl.BlockSpec((rows, width // 2), lambda j, t: (0, j))
    return call(
        functools.partial(piece_body, len(ours)),
        table,
        (2,),
        [*ours, *theirs, grads, their_grads],
        [half_spec(v, half, 1) for v in (*ours, *theirs)] + [cols, cols],
        jax.ShapeDtypeStruct((half, width), B16),
        pl.BlockSpec((half, width // 2), lambda j, t: (0, j)),
        [pltpu.VMEM((rows, half), B16)] * 2,
        0,
    )


def query_body(groups, n, half, table, *refs):
    offers, blocks = refs[: -5 - n], refs[-5 - n : -5]
    own_out, other_out, rows_in, weight_in, _ = refs[-5:]
    rows = own_out.shape[0]

    @pl.when(pl.program_id(0) == 0)
    def _():
        at = 0
        for step, count in enumerate(groups):
            start = pl.multiple_of(table[1 + step] * half, half)
            for side in range(2):
                here = offers[at : at + count]
                at += count
                target = rows_in.at[pl.ds(side * rows, rows), pl.ds(start, half)]
                copy_chosen(table[1 + n + step], here, target)

    for chunk in range(n):
        weight_in[pl.ds(chunk * half, half), :] = blocks[chunk][...]
    own_out[...] = dot(rows_in[pl.ds(0, rows), :], weight_in[...], 1, 0)
    other_out[...] = dot(rows_in[pl.ds(rows, rows), :], weight_in[...], 1, 0).astype(B16)


def query_parts(table, offers, weight):
    n = len(offers)
    rows, width = offers[0][0][0].shape[0], weight.shape[1]
    half = cols = width // 2
    flat = [v for pair in offers for side in pair for v in side]

    def block(chunk):
        return pl.BlockSpec((half, cols), lambda j, t: (2 * chunk + t[0], j))

    out = pl.BlockSpec((rows, cols), lambda j, t: (0, j))
    return call(
        functools.partial(query_body, [len(pair[0]) for pair in offers], n, half),
        table,
        (2,),
        [*flat] + [weight] * n,
        [half_spec(v, half, 0) for v in flat] + [block(c) for c in range(n)],
        [
            jax.ShapeDtypeStruct((rows, width), F32),
            jax.ShapeDtypeStruct((rows, width), B16),
        ],
        [out, out],
        [
            pltpu.VMEM((2 * rows, n * half), B16),
            pltpu.VMEM((n * half, cols), B16),
            pltpu.VMEM((8, 128), F32),
        ],
        0,
    )


def term_body(table, grads, weight, out):
    out[...] = dot(grads[...], weight[...], 1, 1).astype(B16)


def term_of(table, grads, weight):
    rows, width = grads.shape
    half = width // 2
    return call(
        term_body,
        table,
        (2,),
        [grads, weight],
        [whole(grads), pl.BlockSpec((half, width), lambda j, t: (2 * t[0] + j, 0))],
        jax.ShapeDtypeStruct((rows, width), B16),
        pl.BlockSpec((rows, half), lambda j, t: (0, j)),
        [],
        2 * rows * width * width,
    )


def place_body(table, ours, theirs, *refs):
    out = refs[-1]

    @pl.when(pl.program_id(0) == 0)
    def _():
        out[...] = ours[...]

    @pl.when(pl.program_id(0) == 1)
    def _():
        out[...] = theirs[...]


def place(table, ours, theirs, target, shape):
    half, width = ours.shape
    arrays, specs, aliases = [ours, theirs], [whole(ours), whole(theirs)], {}
    if target is not None:
        arrays.append(target)
        specs.append(pl.BlockSpec(memory_space=pl.ANY))
        aliases = {3: 0}
    return call(
        place_body,
        table,
        (2,),
        arrays,
        specs,
        jax.ShapeDtypeStruct(shape, B16),
        pl.BlockSpec((half, width), lambda i, t: (t[i], 0)),
        [],
        0,
        aliases,
    )


def add_body(table, a, b, out):
    out[...] = (a[...].astype(F32) + b[...].astype(F32)).astype(B16)


def add(a, b):
    rows, width = a.shape
    steps = 2 if rows >= 256 else 1
    spec = pl.BlockSpec((rows // steps, width), lambda i, t: (i, 0))
    out = jax.ShapeDtypeStruct(a.shape, B16)
    return call(add_body, jnp.zeros((1,), jnp.int32), (steps,), [a, b], [spec] * 2, out, spec, [], 0)


def ranks_body(rank, table, mine, fetched, shared, relative, tokens, grads, down, up, part):
    split = mine.shape[1]
    down[pl.ds(0, split), :] = mine[0]
    up[pl.ds(0, split), :] = mine[1]

    @pl.when(table[0] == 0)
    def _():
        down[pl.ds(split, split), :] = fetched[...]
        up[pl.ds(split, split), :] = shared[...]

    @pl.when(table[0] != 0)
    def _():
        down[pl.ds(split, split), :] = shared[...]
        up[pl.ds(split, split), :] = fetched[...]

    for kind, (maps, rows) in enumerate(((down, tokens), (up, grads))):
        every = dot(maps[...], rows[...], 1, 1)
        total = None
        for slot in range(2 * split // rank):
            own = jnp.where(relative[...] == slot, every[slot * rank : (slot + 1) * rank], 0.0)
            total = own if total is None else total + own
        part[pl.ds(kind * rank, rank), :] = total.astype(B16)


def ranks_of(table, rank, mine, fetched, shared, relative, tokens, grads):
    rows, width = tokens.shape
    arrays = [mine, fetched, shared, relative, tokens, grads]
    outs = [
        jax.ShapeDtypeStruct((2 * mine.shape[1], width), B16),
        jax.ShapeDtypeStruct((2 * mine.shape[1], width), B16),
        jax.ShapeDtypeStruct((2 * rank, rows), B16),
    ]
    body = functools.partial(ranks_body, rank)
    specs = [whole(v) for v in arrays]
    return call(body, table, (1,), arrays, specs, outs, [whole(v) for v in outs], [], 0)


def maps_body(rank, table, part, came, relative, tokens, grads, low, back, kept, sent):
    total = (part[...].astype(F32) + came[...].astype(F32)).astype(B16).astype(F32)
    for kind, wide in enumerate((low, back)):
        own = total[kind * rank : (kind + 1) * rank]
        for slot in range(wide.shape[0] // rank):
            spread_out = jnp.where(relative[...] == slot, own, 0.0)
            wide[pl.ds(slot * rank, rank), :] = spread_out.astype(B16)
    for kind, (wide, rows) in enumerate(((back, tokens), (low, grads))):
        term = SCALE * dot(wide[...], rows[...], 1, 0)

        @pl.when(table[0] == kind)
        def _(term=term):
            kept[...] = term

        @pl.when(table[0] != kind)
        def _(term=term):
            sent[...] = term.astype(B16)


def maps_of(table, rank, slots, part, came, relative, tokens, grads):
    rows, width = tokens.shape
    arrays = [part, came, relative, tokens, grads]
    outs = [
        jax.ShapeDtypeStruct((slots * rank, rows), B16),
        jax.ShapeDtypeStruct((slots * rank, rows), B16),
        jax.ShapeDtypeStruct((slots * rank, width), F32),
        jax.ShapeDtypeStruct((slots * rank, width), B16),
    ]
    body = functools.partial(maps_body, rank)
    specs = [whole(v) for v in arrays]
    return call(body, table, (1,), arrays, specs, outs, [whole(v) for v in outs], [], 0)


def lora_body(table, low, up, back, down, out, into):
    out[...] = (SCALE * dot(low[...], up[...], 0, 0)).astype(B16)
    into[...] = (SCALE * dot(back[...], down[...], 0, 0)).astype(B16)


def lora_of(low, up, back, down):
    rows, width = low.shape[1], up.shape[1]
    arrays = [low, up, back, down]
    out = jax.ShapeDtypeStruct((rows, width), B16)
    specs = [whole(v) for v in arrays]
    table = jnp.zeros((1,), jnp.int32)
    return call(lora_body, table, (1,), arrays, specs, [out, out], [whole(out)] * 2, [], 0)


def finish_body(table, here, there, lora, live, out):
    total = here[...] + there[...].astype(F32) + lora[...].astype(F32)
    out[...] = jnp.where(live[...] > 0, total, 0.0).astype(B16)


def finish(here, there, lora, live):
    rows, width = here.shape
    spec = pl.BlockSpec((rows // 2, width), lambda i, t: (i, 0))
    thin = pl.BlockSpec((rows // 2, 1), lambda i, t: (i, 0))
    out = jax.ShapeDtypeStruct((rows, width), B16)
    arrays = [here, there, lora, live]
    table = jnp.zeros((1,), jnp.int32)
    return call(finish_body, table, (2,), arrays, [spec] * 3 + [thin], out, spec, [], 0)


def shards_line(tokens, weight, down_maps, up_maps, counts, slot_of, cotangent):
    rows, width = tokens.shape
    held, _, rank = down_maps.shape
    n = lax.axis_size("tensor")
    slots = held * 2
    z = lax.axis_index("tensor")
    owner = lax.axis_index("tenant")
    core = lax.axis_index("dp")
    swap = [(0, 1), (1, 0)]
    ahead = jnp.where(core == 0, z, n - 1 - z)
    line_pairs = []
    for i in range(n - 1):
        line_pairs += [(2 * i, 2 * i + 2), (2 * i + 3, 2 * i + 1)]

    def along(value):
        return lax.ppermute(value, ("tensor", "dp"), line_pairs)

    def other_tenant(value):
        return lax.ppermute(value, "tenant", swap)

    def other_core(value):
        return lax.ppermute(value, "dp", swap)

    def other_core_halves(value):
        return jnp.concatenate([other_core(v) for v in jnp.split(value, 2)])

    def numbers(*values):
        return jnp.stack([v.astype(jnp.int32) for v in values])

    chunk_of = [z]
    choice_of = [jnp.zeros((), jnp.int32)]
    kinds_of = [None]
    for choices in arrival_plan(n):
        kinds = sorted({(t, d == c) for t, d, _ in choices for c in range(2)})
        chunk = choice = jnp.zeros((), jnp.int32)
        for at, (t, direction, source) in enumerate(choices):
            chunk = jnp.where(z == at, source, chunk)
            for c in range(2):
                here = (z == at) & (core == c)
                choice = jnp.where(here, kinds.index((t, direction == c)), choice)
        chunk_of.append(chunk)
        choice_of.append(choice)
        kinds_of.append(kinds)

    st = {}

    def fence():
        names = list(st)
        st.update(zip(names, lax.optimization_barrier([st[name] for name in names])))

    def hop_of(k):
        t, side = k // 2 + 1, k % 2
        chunk = jnp.clip(n + ahead + 1 - t, 0, n - 1)
        chunk = jnp.where(core == 0, chunk, n - 1 - chunk)
        sums = (ahead < n - 1) & (ahead < t - 1)
        table = numbers(chunk, sums, 1 - core)
        grads = st["their_grads" if side else "grads"]
        st["sent"], st["share"] = hop(table, grads, st["weight"], st["line", t - 1, side])

    def offers_of(step):
        if step == 0:
            return [[st["tokens"]], [st["their_tokens"]]]
        kinds = kinds_of[step]
        return [
            [st["line", t, s] if mine else st["shared", t, 1 - s] for t, mine in kinds]
            for s in range(2)
        ]

    def piece_of(step):
        table = numbers(choice_of[step], core)
        st["mix", step] = piece(table, *offers_of(step), st["grads"], st["their_grads"])

    def sum_of(step):
        st["ours", step] = add(st.pop(("mix", step)), st.pop(("x", step)))

    def place_of(step, theirs):
        blocks = numbers(2 * chunk_of[step] + core, 2 * chunk_of[step] + 1 - core)
        into = st.get("wg")
        st["wg"] = place(blocks, st.pop(("ours", step)), theirs, into, (n * width, width))

    st["weight"], st["tokens"] = weight, tokens
    line = along(tokens)
    st["their_tokens"] = other_core(tokens)
    theirs = other_core(cotangent)
    mine = jnp.stack([jnp.swapaxes(down_maps, 1, 2), up_maps]).reshape(2, -1, width)
    st["fetched"] = other_tenant(lax.dynamic_index_in_dim(mine, core, 0, keepdims=False))
    st["mine"] = mine
    row_ids = (owner * 2 + core) * rows + jnp.arange(rows, dtype=jnp.int32)
    tenant, live = layout(counts, row_ids)
    relative = lax.rem(lookup(slot_of, tenant) + (2 - owner) * held, slots)
    st["relative"] = relative[None, :]
    st["live"] = live.astype(F32)[:, None]
    their_live = layout(counts, row_ids + (1 - 2 * core) * rows)[1]
    st["grads"] = jnp.where(live[:, None], cotangent, jnp.zeros_like(cotangent))
    st["their_grads"] = jnp.where(their_live[:, None], theirs, jnp.zeros_like(cotangent))
    fence()

    coming = along(st["their_tokens"])
    piece_of(0)
    swapped = other_tenant(st["mix", 0])
    shared = other_core(st["fetched"])
    st["term"] = term_of(z[None], st["grads"], st["weight"])
    names = ("relative", "tokens", "grads")
    st["down"], st["up"], st["part"] = ranks_of(
        core[None], rank, st.pop("mine"), st.pop("fetched"), shared, *[st[v] for v in names]
    )
    st["line", 1, 0] = line
    line = coming
    fence()

    wg_share = None
    for k in range(2, 2 * n + 1):
        t, side, step = k // 2 + 1, k % 2, k // 2
        last = k == 2 * n
        if not last:
            hop_of(k)
        if side == 1:
            st["x", step - 1] = swapped
        if k in (2, 3):
            pairs = [(i, i ^ (k - 1)) for i in range(n)]
            st["came"] = lax.ppermute(st["part"], "tensor", pairs)
        if k == 4:
            st["maps"] = st["maps"] + other_core(st.pop("for_sibling")).astype(F32)
        if k == 6:
            kept, sent = jnp.split(st.pop("maps"), 2)
            st["kept"] = kept + other_tenant(sent.astype(B16)).astype(F32)
        if last:
            kept = st.pop("kept")
            other = other_core(kept)
            down_grad = jnp.where(core == 0, kept, other).reshape(held, rank, width)
            st["up_grad"] = jnp.where(core == 0, other, kept).reshape(held, rank, width)
            st["down_grad"] = jnp.swapaxes(down_grad, 1, 2)
        fence()
        if not last:
            coming = along(st.pop("sent"))
            st["shared", t - 1, side] = other_core(st.pop("share"))
        if side == 1:
            piece_of(step)
            swapped = other_tenant(st["mix", step])
            sum_of(step - 1)
        elif 4 <= k < 2 * n:
            wg_share = other_core(st["ours", step - 2])
        if k >= 6 and side == 0:
            place_of(step - 3, st.pop("theirs"))
        if k == 2:
            st["part"] = add(st["part"], st.pop("came"))
        if k == 3:
            st["low"], st["back"], st["maps"], st["for_sibling"] = maps_of(
                core[None],
                rank,
                slots,
                st.pop("part"),
                st.pop("came"),
                *[st[v] for v in names],
            )
        if k == 4:
            maps = [st.pop(v) for v in ("low", "up", "back", "down")]
            st["lora_out"], st["lora_in"] = lora_of(*maps)
        if last:
            offers = [offers_of(s) for s in range(n)]
            table = numbers(core, *chunk_of, *choice_of)
            st["query_here"], st["query_there"] = query_parts(table, offers, st["weight"])
        st["line", (k - 1) // 2 + 1, 1 - side] = line
        line = coming
        if side == 1 and wg_share is not None:
            st["theirs"] = wg_share
            wg_share = None
        fence()

    theirs = other_core_halves(st["line", n, 1])
    there = other_core_halves(st.pop("query_there"))
    total = st.pop("term").astype(F32) + st.pop("lora_in").astype(F32)
    total = total + st["line", n, 0].astype(F32) + theirs.astype(F32)
    st["token_grad"] = total.astype(B16)
    st["query"] = finish(st.pop("query_here"), there, st.pop("lora_out"), st.pop("live"))
    fence()
    st["x", n - 1] = swapped
    fence()
    sum_of(n - 1)
    shares = [other_core(st["ours", step]) for step in (n - 2, n - 1)]
    for step in (n - 2, n - 1):
        place_of(step, shares[step - n + 2])
    return st["query"], st["token_grad"], st["wg"], st["down_grad"], st["up_grad"]


def solution(mesh):
    placed = (
        P(("groups", "tenant", "dp"), "tensor"),
        P(None, "tensor"),
        P("tenant", "tensor", None),
        P("tenant", None, "tensor"),
        P("groups"),
        P(),
        P(("groups", "tenant", "dp"), "tensor"),
    )
    short = mesh.shape["tensor"] == 4
    paired = mesh.shape["tenant"] == 2 and mesh.shape["dp"] == 2
    return jax.shard_map(
        shards_line if short and paired else shards_general,
        mesh=mesh,
        in_specs=placed,
        out_specs=(
            P(("groups", "tenant", "dp"), "tensor"),
            P(("groups", "tenant", "dp"), "tensor"),
            P("groups", "tensor"),
            P(("groups", "tenant"), "tensor", None),
            P(("groups", "tenant"), None, "tensor"),
        ),
        check_vma=False,
    )
```

time: 226 us -> 185 us (0.82)
  Pallas kernels: 0 us -> 81.3 us
  waiting for transfers between devices: 96.4 us -> 26.5 us
  matrix products: 32.5 us -> 0 us
  starting transfers between devices: 60 us -> 44.8 us
  other arithmetic: 19.4 us -> 14.4 us
    pallas_call x0 -> x25, Pallas kernels: none -> 81.3 us  [call(): pl.pallas_call(body, grid_spec=pltpu.PrefetchScalarGridSpec(num_scalar_pr...]
    ppermute x27 -> x10, waiting for transfers between devices: 46.6 us -> 5.3 us  [the longest x2 5.27 us: shards_line(): st['came'] = lax.ppermute(st['part'], 'tensor', pairs)]
    dot_general x16 -> x0, matrix products: 32.5 us -> none  [dot(): lax.dot_general(a, b, (((ca,), (cb,)), ((), ())), preferred_element_type=...]
    ppermute x10 -> x6, waiting for transfers between devices: 49.8 us -> 19 us  [other_tenant(): return lax.ppermute(value, 'tenant', swap)]
    ppermute x27 -> x10, starting transfers between devices: 48.6 us -> 33.8 us  [the longest x8 32.2 us: along(): return lax.ppermute(value, ('tensor', 'dp'), line_pairs)]
    dynamic_update_slice x14 -> x0, other arithmetic: 10.5 us -> none  [the longest x3 5.33 us: keep(): lax.dynamic_update_slice(gathered, pair[0], (0, chunk * width + first))]
    unnamed x40 -> x90, local copies, waits for them, and re-layouts: 4.07 us -> 13 us
    broadcast_in_dim x3 -> x0, local copies, waits for them, and re-layouts: 3.59 us -> none  [the longest x1 2.52 us: shards_line(): gathered = jnp.zeros((rows, n * width), B16)]
  transfers between devices with their start and end apart: 52 -> 35, of which waited for: 16 -> 8; matrix products, arithmetic and copies ran while one was open for 26% -> 9% of each run, Pallas kernels for 0% -> 42%
where the time goes in v2:
time: 185 us; the launch traced here: 184 us
  Pallas kernels  81.3 us (44%)
  starting transfers between devices  44.8 us (24%)
  waiting for transfers between devices  26.5 us (14%)
  local copies, waits for them, and re-layouts  15.9 us (9%)
  other arithmetic  14.4 us (8%)
    pallas_call x25, Pallas kernels, call(): pl.pallas_call(body, grid_spec=pltpu.PrefetchScalarGridSpec(num_scalar_pr...  81.3 us
    ppermute x8, starting transfers between devices, along(): return lax.ppermute(value, ('tensor', 'dp'), line_pairs)  32.2 us
    ppermute x6, waiting for transfers between devices, other_tenant(): return lax.ppermute(value, 'tenant', swap)  19 us
    unnamed x90, local copies, waits for them, and re-layouts  13 us
    ppermute x6, starting transfers between devices, other_tenant(): return lax.ppermute(value, 'tenant', swap)  7.12 us
    ppermute x2, waiting for transfers between devices, shards_line(): st['came'] = lax.ppermute(st['part'], 'tensor', pairs)  5.27 us
    ppermute x19, starting transfers between devices, other_core(): return lax.ppermute(value, 'dp', swap)  3.91 us
  transfers between devices with their start and end apart: 35, of which 8 were waited for; matrix products, arithmetic and copies ran while one was open for 9% of the time, Pallas kernels for 42%

profile of v2, /device:TPU:0, one launch (start us, length us, event | category | flops | bytes accessed | tf_op | source)
XLA Modules:
  0.0 184.1 jit_solution(1666268095223507432)
XLA Ops:
  1.2 4.7 %collective-permute-start.4 = (bf16[512,1024]{1,0:T(8,128)(2,1)}, bf16[512,1024]{1,0:T(8,128)(2,1)S(1)}, u32[]{:S(2)}, u32[]{:S(2)}) collective-permute-start(bf16[512,1024]{1,0:T(8,128)(2,1)} %refs_0_.1), channel_id=1, source_target_pairs={{0,4},{5,1},{4,8},{9,5},{8,12},{13,9},{2,6},{7,3},{6,10},{11,7},{1... | collective-permute-start | bytes 3145736 | tf_op jit(solution)/shard_map/ppermute | solution.py:431
  13.7 1.8 broadcast_select_fusion.refs_3_.grads.refs_5_.refs_9_
  15.6 4.4 %collective-permute-start.7 = (bf16[512,1024]{1,0:T(8,128)(2,1)}, bf16[512,1024]{1,0:T(8,128)(2,1)}, u32[]{:S(2)}, u32[]{:S(2)}) collective-permute-start(bf16[512,1024]{1,0:T(8,128)(2,1)} %collective-permute-done.refs_1_), channel_id=1, source_target_pairs={{0,4},{5,1},{4,8},{9,5},{8,12},{13,9},{2,6},{7,3},{6,10},{11,7},{1... | collective-permute-start | bytes 3145736 | tf_op jit(solution)/shard_map/ppermute | solution.py:431
  20.1 4.2 %shard_map.110.a = bf16[512,1024]{1,0:T(8,128)(2,1)} custom-call(s32[2]{0:T(128)S(1)} %pad_add_fusion.table, bf16[512,1024]{1,0:T(8,128)(2,1)S(1)} %copy-done.8, bf16[512,1024]{1,0:T(8,128)(2,1)} %collective-permute-done.refs_1_, bf16[512,1024]{1,0:T(8,128)(2,1)S(1)} %broadcast_select_fusion.1.refs_2_.grads.refs_4_.refs_8_, ...), custom_call_target="tpu_custom_call" | custom-call | flops 1 | bytes 1 | tf_op jit(solution)/shard_map/pallas_call | solution.py:101
  24.8 2.9 %shard_map.111 = bf16[512,1024]{1,0:T(8,128)(2,1)S(1)} custom-call(s32[1]{0:T(128)} %bitcast.10.table, bf16[512,1024]{1,0:T(8,128)(2,1)S(1)} %broadcast_select_fusion.1.refs_2_.grads.refs_4_.refs_8_, bf16[4096,1024]{1,0:T(8,128)(2,1)} %refs_25_), custom_call_target="tpu_custom_call" | custom-call | flops 1 | bytes 1 | tf_op jit(solution)/shard_map/pallas_call | solution.py:101
  28.7 1.8 shard_map.112
  32.5 4.2 %shard_map.113 = (bf16[512,1024]{1,0:T(8,128)(2,1)}, bf16[512,512]{1,0:T(8,128)(2,1)S(1)}) custom-call(s32[3]{0:T(128)S(1)} %get-tuple-element.734.table, bf16[512,1024]{1,0:T(8,128)(2,1)S(1)} %broadcast_select_fusion.1.refs_2_.grads.refs_4_.refs_8_, bf16[4096,1024]{1,0:T(8,128)(2,1)} %refs_25_, ...), custom_call_target="tpu_custom_call" | custom-call | flops 1 | bytes 1 | tf_op jit(solution)/shard_map/pallas_call | solution.py:101
  36.7 3.4 %collective-permute-start.11 = (bf16[512,1024]{1,0:T(8,128)(2,1)}, bf16[512,1024]{1,0:T(8,128)(2,1)}, u32[]{:S(2)}, u32[]{:S(2)}) collective-permute-start(bf16[512,1024]{1,0:T(8,128)(2,1)} %get-tuple-element.443), channel_id=1, source_target_pairs={{0,4},{5,1},{4,8},{9,5},{8,12},{13,9},{2,6},{7,3},{6,10},{11,7},{1... | collective-permute-start | bytes 3145736 | tf_op jit(solution)/shard_map/ppermute | solution.py:431
  41.1 4.6 %shard_map.115 = (bf16[512,1024]{1,0:T(8,128)(2,1)S(1)}, bf16[512,512]{1,0:T(8,128)(2,1)}) custom-call(s32[3]{0:T(128)S(1)} %get-tuple-element.734.table, bf16[512,1024]{1,0:T(8,128)(2,1)S(1)} %broadcast_select_fusion.refs_3_.grads.refs_5_.refs_9_, bf16[4096,1024]{1,0:T(8,128)(2,1)} %refs_25_, ...), custom_call_target="tpu_custom_call" | custom-call | flops 1 | bytes 1 | tf_op jit(solution)/shard_map/pallas_call | solution.py:101
  47.0 5.3 %collective-permute-done.9.came = bf16[32,512]{1,0:T(8,128)(2,1)S(1)} collective-permute-done((bf16[32,512]{1,0:T(8,128)(2,1)S(1)}, bf16[32,512]{1,0:T(8,128)(2,1)S(1)}, u32[]{:S(2)}, u32[]{:S(2)}) %collective-permute-start.9) | collective-permute-done | bytes 32800 | tf_op jit(solution)/shard_map/ppermute | solution.py:536
  53.7 3.1 %collective-permute-start.14 = (bf16[512,1024]{1,0:T(8,128)(2,1)}, bf16[512,1024]{1,0:T(8,128)(2,1)S(1)}, u32[]{:S(2)}, u32[]{:S(2)}) collective-permute-start(bf16[512,1024]{1,0:T(8,128)(2,1)} %copy-done.42), channel_id=1, source_target_pairs={{0,4},{5,1},{4,8},{9,5},{8,12},{13,9},{2,6},{7,3},{6,10},{11,7},{1... | collective-permute-start | bytes 3145736 | tf_op jit(solution)/shard_map/ppermute | solution.py:431
  58.0 3.4 %shard_map.116.a = bf16[512,1024]{1,0:T(8,128)(2,1)S(1)} custom-call(s32[2]{0:T(128)S(1)} %pad_add_fusion.1.table, bf16[512,512]{1,0:T(8,128)(2,1)S(1)} %collective-permute-done.10.refs_0_.refs_2_.refs_6_, bf16[512,1024]{1,0:T(8,128)(2,1)S(1)} %collective-permute-done.4.came.away.refs_1_.refs_3_.refs_7_, bf16[512,512]{1,0:T(8,128)(2,1)S(1)} %copy-done.13, ...), custom_call_target="tpu_custom_call" | custom-call | flops 1 | bytes 1 | tf_op jit(solution)/shard_map/pallas_call | solution.py:101
  63.7 2.5 %shard_map.117.ours = bf16[512,1024]{1,0:T(8,128)(2,1)} custom-call(s32[1]{0:T(128)} %constant.85.clone.1.table, bf16[512,1024]{1,0:T(8,128)(2,1)} %shard_map.110.a, bf16[512,1024]{1,0:T(8,128)(2,1)} %collective-permute-done.8.b), custom_call_target="tpu_custom_call" | custom-call | flops 1 | bytes 1 | tf_op jit(solution)/shard_map/pallas_call | solution.py:101
  67.0 4.5 %shard_map.119 = (bf16[512,1024]{1,0:T(8,128)(2,1)}, bf16[512,512]{1,0:T(8,128)(2,1)S(1)}) custom-call(s32[3]{0:T(128)S(1)} %get-tuple-element.735.table, bf16[512,1024]{1,0:T(8,128)(2,1)S(1)} %broadcast_select_fusion.1.refs_2_.grads.refs_4_.refs_8_, bf16[4096,1024]{1,0:T(8,128)(2,1)} %refs_25_, ...), custom_call_target="tpu_custom_call" | custom-call | flops 1 | bytes 1 | tf_op jit(solution)/shard_map/pallas_call | solution.py:101
  72.4 4.3 %collective-permute-start.17 = (bf16[512,1024]{1,0:T(8,128)(2,1)}, bf16[512,1024]{1,0:T(8,128)(2,1)}, u32[]{:S(2)}, u32[]{:S(2)}) collective-permute-start(bf16[512,1024]{1,0:T(8,128)(2,1)} %get-tuple-element.531), channel_id=1, source_target_pairs={{0,4},{5,1},{4,8},{9,5},{8,12},{13,9},{2,6},{7,3},{6,10},{11,7},{1... | collective-permute-start | bytes 3145736 | tf_op jit(solution)/shard_map/ppermute | solution.py:431
  80.3 4.3 %shard_map.121 = (bf16[512,1024]{1,0:T(8,128)(2,1)S(1)}, bf16[512,512]{1,0:T(8,128)(2,1)}) custom-call(s32[3]{0:T(128)S(1)} %get-tuple-element.735.table, bf16[512,1024]{1,0:T(8,128)(2,1)S(1)} %copy-done.3, bf16[4096,1024]{1,0:T(8,128)(2,1)} %refs_25_, bf16[512,1024]{1,0:T(8,128)(2,1)S(1)} %collective-permute-done.14.came.away.refs_7_.refs_5_.refs_13_.refs_19_, ...), custom_call_target="tpu_custom_call" | custom-call | flops 1 | bytes 1 | tf_op jit(solution)/shard_map/pallas_call | solution.py:101
  87.2 3.6 %collective-permute-start.21 = (bf16[512,1024]{1,0:T(8,128)(2,1)}, bf16[512,1024]{1,0:T(8,128)(2,1)S(1)}, u32[]{:S(2)}, u32[]{:S(2)}) collective-permute-start(bf16[512,1024]{1,0:T(8,128)(2,1)} %copy-done.41), channel_id=1, source_target_pairs={{0,4},{5,1},{4,8},{9,5},{8,12},{13,9},{2,6},{7,3},{6,10},{11,7},{1... | collective-permute-start | bytes 3145736 | tf_op jit(solution)/shard_map/ppermute | solution.py:431
  91.9 4.9 %shard_map.122.a = bf16[512,1024]{1,0:T(8,128)(2,1)} custom-call(s32[2]{0:T(128)S(1)} %pad_add_fusion.2.table, bf16[512,512]{1,0:T(8,128)(2,1)S(1)} %copy-done.17, bf16[512,1024]{1,0:T(8,128)(2,1)S(1)} %collective-permute-done.4.came.away.refs_1_.refs_3_.refs_7_, bf16[512,512]{1,0:T(8,128)(2,1)} %collective-permute-done.16.refs_2_.refs_0_.refs_8_.refs_14_, ...), custom_call_target="tpu_custom_call" | custom-call | flops 1 | bytes 1 | tf_op jit(solution)/shard_map/pallas_call | solution.py:101
  101.1 4.5 %shard_map.124 = (bf16[512,1024]{1,0:T(8,128)(2,1)}, bf16[512,512]{1,0:T(8,128)(2,1)S(1)}) custom-call(s32[3]{0:T(128)S(1)} %add_add_fusion.2.table, bf16[512,1024]{1,0:T(8,128)(2,1)S(1)} %copy-done.1, bf16[4096,1024]{1,0:T(8,128)(2,1)} %refs_25_, bf16[512,1024]{1,0:T(8,128)(2,1)} %collective-permute-done.17.came.away.refs_3_.refs_17_, ...), custom_call_target="tpu_custom_call" | custom-call | flops 1 | bytes 1 | tf_op jit(solution)/shard_map/pallas_call | solution.py:101
  105.6 18.0 %collective-permute-done.19 = bf16[64,1024]{1,0:T(8,128)(2,1)S(1)} collective-permute-done((bf16[64,1024]{1,0:T(8,128)(2,1)S(1)}, bf16[64,1024]{1,0:T(8,128)(2,1)S(1)}, u32[]{:S(2)}, u32[]{:S(2)}) %collective-permute-start.19) | collective-permute-done | bytes 131104 | tf_op jit(solution)/shard_map/ppermute | solution.py:434
  123.7 4.8 %collective-permute-start.24 = (bf16[512,1024]{1,0:T(8,128)(2,1)}, bf16[512,1024]{1,0:T(8,128)(2,1)}, u32[]{:S(2)}, u32[]{:S(2)}) collective-permute-start(bf16[512,1024]{1,0:T(8,128)(2,1)} %get-tuple-element.634), channel_id=1, source_target_pairs={{0,4},{5,1},{4,8},{9,5},{8,12},{13,9},{2,6},{7,3},{6,10},{11,7},{1... | collective-permute-start | bytes 3145736 | tf_op jit(solution)/shard_map/ppermute | solution.py:431
  128.6 3.5 %shard_map.125.refs_0_ = bf16[4096,1024]{1,0:T(8,128)(2,1)} custom-call(s32[2]{0:T(128)S(1)} %pad_add_fusion.3.table, bf16[512,1024]{1,0:T(8,128)(2,1)} %shard_map.117.ours, bf16[512,1024]{1,0:T(8,128)(2,1)} %collective-permute-done.18.theirs), custom_call_target="tpu_custom_call" | custom-call | flops 1 | bytes 1 | tf_op jit(solution)/shard_map/pallas_call | solution.py:101
  132.1 4.4 %shard_map.126 = (bf16[512,1024]{1,0:T(8,128)(2,1)}, bf16[512,512]{1,0:T(8,128)(2,1)}) custom-call(s32[3]{0:T(128)S(1)} %add_add_fusion.2.table, bf16[512,1024]{1,0:T(8,128)(2,1)S(1)} %copy-done.4, bf16[4096,1024]{1,0:T(8,128)(2,1)} %refs_25_, bf16[512,1024]{1,0:T(8,128)(2,1)S(1)} %collective-permute-done.21.came.away.refs_7_.refs_21_, ...), custom_call_target="tpu_custom_call" | custom-call | flops 1 | bytes 1 | tf_op jit(solution)/shard_map/pallas_call | solution.py:101
  136.5 3.9 %collective-permute-start.27 = (bf16[512,1024]{1,0:T(8,128)(2,1)}, bf16[512,1024]{1,0:T(8,128)(2,1)}, u32[]{:S(2)}, u32[]{:S(2)}) collective-permute-start(bf16[512,1024]{1,0:T(8,128)(2,1)} %get-tuple-element.690), channel_id=1, source_target_pairs={{0,4},{5,1},{4,8},{9,5},{8,12},{13,9},{2,6},{7,3},{6,10},{11,7},{1... | collective-permute-start | bytes 3145736 | tf_op jit(solution)/shard_map/ppermute | solution.py:431
  140.5 1.7 shard_map.128.ours
  144.4 4.3 %shard_map.127.a = bf16[512,1024]{1,0:T(8,128)(2,1)S(1)} custom-call(s32[2]{0:T(128)S(1)} %pad_add_fusion.4.table, bf16[512,512]{1,0:T(8,128)(2,1)} %collective-permute-done.16.refs_2_.refs_0_.refs_8_.refs_14_, bf16[512,1024]{1,0:T(8,128)(2,1)} %collective-permute-done.11.came.away.refs_3_.refs_1_.refs_9_.refs_15_, bf16[512,512]{1,0:T(8,128)(2,1)S(1)} %copy-done.28, ...), custom_call_target="tpu_custom_call" | custom-call | flops 1 | bytes 1 | tf_op jit(solution)/shard_map/pallas_call | solution.py:101
  150.5 1.8 broadcast_select_fusion.2
  152.3 3.7 %shard_map.129.refs_0_ = bf16[4096,1024]{1,0:T(8,128)(2,1)} custom-call(s32[2]{0:T(128)S(1)} %pad_add_fusion.5.table, bf16[512,1024]{1,0:T(8,128)(2,1)} %shard_map.123.ours, bf16[512,1024]{1,0:T(8,128)(2,1)} %collective-permute-done.25.theirs, bf16[4096,1024]{1,0:T(8,128)(2,1)} %shard_map.125.refs_0_), custom_call_target="tpu_custom_call", output_to_operand_aliasing={{}: (3, {})} | custom-call | flops 1 | bytes 1 | tf_op jit(solution)/shard_map/pallas_call | solution.py:101
  156.1 10.9 %shard_map.130 = (f32[512,1024]{1,0:T(8,128)}, bf16[512,1024]{1,0:T(8,128)(2,1)S(1)}) custom-call(s32[9]{0:T(128)S(1)} %stack.175.table, bf16[512,1024]{1,0:T(8,128)(2,1)S(1)} %copy-done.11, bf16[512,1024]{1,0:T(8,128)(2,1)} %collective-permute-done.refs_1_, bf16[512,512]{1,0:T(8,128)(2,1)S(1)} %copy-done.18, bf16[512,1024]{1,0:T(8,128)(2,1)} %copy-done.5, ...), custom_call_target="tpu_custom_call" | custom-call | flops 1 | bytes 1 | tf_op jit(solution)/shard_map/pallas_call | solution.py:101
  171.8 3.1 %add_convert_fusion = bf16[512,1024]{1,0:T(8,128)(2,1)} fusion(bf16[512,1024]{1,0:T(8,128)(2,1)} %collective-permute-done.24, bf16[512,1024]{1,0:T(8,128)(2,1)S(1)} %copy-done.31, bf16[512,1024]{1,0:T(8,128)(2,1)S(1)} %copy-done.25, bf16[256,1024]{1,0:T(8,128)(2,1)S(1)} %collective-permute-done.29, bf16[256,1024]{1,0:T(8,128)(2,1)S(1)} %collective-permute-done.28), kind=kLoop, calls=%fused_computation | loop fusion | flops 5767168 | bytes 5242880 | tf_op jit(solution)/shard_map/convert_element_type | solution.py:589
  177.7 3.2 %shard_map.133.refs_0_ = bf16[4096,1024]{1,0:T(8,128)(2,1)} custom-call(s32[2]{0:T(128)S(1)} %pad_add_fusion.7.table, bf16[512,1024]{1,0:T(8,128)(2,1)S(1)} %shard_map.128.ours, bf16[512,1024]{1,0:T(8,128)(2,1)} %collective-permute-done.34.theirs, bf16[4096,1024]{1,0:T(8,128)(2,1)} %shard_map.129.refs_0_), custom_call_target="tpu_custom_call", output_to_operand_aliasing={{}: (3, {})} | custom-call | flops 1 | bytes 1 | tf_op jit(solution)/shard_map/pallas_call | solution.py:101
  180.9 3.2 %shard_map.134 = bf16[4096,1024]{1,0:T(8,128)(2,1)} custom-call(s32[2]{0:T(128)S(1)} %pad_add_fusion.6.table, bf16[512,1024]{1,0:T(8,128)(2,1)} %shard_map.132.ours, bf16[512,1024]{1,0:T(8,128)(2,1)S(1)} %collective-permute-done.33.theirs, bf16[4096,1024]{1,0:T(8,128)(2,1)} %shard_map.133.refs_0_), custom_call_target="tpu_custom_call", output_to_operand_aliasing={{}: (3, {})} | custom-call | flops 1 | bytes 1 | tf_op jit(solution)/shard_map/pallas_call | solution.py:101
  (192 shorter events, 44.3 us)
Async XLA Ops:
  0.6 14.9 %collective-permute-start = (bf16[512,1024]{1,0:T(8,128)(2,1)}, bf16[512,1024]{1,0:T(8,128)(2,1)}, u32[]{:S(2)}, u32[]{:S(2)}) collective-permute-start(bf16[512,1024]{1,0:T(8,128)(2,1)} %refs_0_.1), channel_id=1, source_target_pairs={{0,1},{1,0},{2,3},{3,2},{4,5},{5,4},{6,7},{7,6},{8,9},{9,8},{10,11... | collective-permute-start | bytes 3145736 | tf_op jit(solution)/shard_map/ppermute | solution.py:437
  1.2 30.7 %collective-permute-start.4 = (bf16[512,1024]{1,0:T(8,128)(2,1)}, bf16[512,1024]{1,0:T(8,128)(2,1)S(1)}, u32[]{:S(2)}, u32[]{:S(2)}) collective-permute-start(bf16[512,1024]{1,0:T(8,128)(2,1)} %refs_0_.1), channel_id=1, source_target_pairs={{0,4},{5,1},{4,8},{9,5},{8,12},{13,9},{2,6},{7,3},{6,10},{11,7},{1... | collective-permute-start | bytes 3145736 | tf_op jit(solution)/shard_map/ppermute | solution.py:431
  7.5 8.1 %collective-permute-start.1 = (bf16[64,1024]{1,0:T(8,128)(2,1)}, bf16[64,1024]{1,0:T(8,128)(2,1)S(1)}, u32[]{:S(2)}, u32[]{:S(2)}) collective-permute-start(bf16[64,1024]{1,0:T(8,128)(2,1)} %fusion.2), channel_id=1, source_target_pairs={{0,2},{2,0},{1,3},{3,1},{4,6},{6,4},{5,7},{7,5},{8,10},{10,8},{9,1... | collective-permute-start | bytes 393224 | tf_op jit(solution)/shard_map/ppermute | solution.py:434
  9.0 4.7 %collective-permute-start.2 = (bf16[512,1024]{1,0:T(8,128)(2,1)}, bf16[512,1024]{1,0:T(8,128)(2,1)}, u32[]{:S(2)}, u32[]{:S(2)}) collective-permute-start(bf16[512,1024]{1,0:T(8,128)(2,1)} %param.13), channel_id=1, source_target_pairs={{0,1},{1,0},{2,3},{3,2},{4,5},{5,4},{6,7},{7,6},{8,9},{9,8},{10,11... | collective-permute-start | bytes 3145736 | tf_op jit(solution)/shard_map/ppermute | solution.py:437
  15.6 24.5 %collective-permute-start.7 = (bf16[512,1024]{1,0:T(8,128)(2,1)}, bf16[512,1024]{1,0:T(8,128)(2,1)}, u32[]{:S(2)}, u32[]{:S(2)}) collective-permute-start(bf16[512,1024]{1,0:T(8,128)(2,1)} %collective-permute-done.refs_1_), channel_id=1, source_target_pairs={{0,4},{5,1},{4,8},{9,5},{8,12},{13,9},{2,6},{7,3},{6,10},{11,7},{1... | collective-permute-start | bytes 3145736 | tf_op jit(solution)/shard_map/ppermute | solution.py:431
  24.3 22.8 %collective-permute-start.8 = (bf16[512,1024]{1,0:T(8,128)(2,1)}, bf16[512,1024]{1,0:T(8,128)(2,1)}, u32[]{:S(2)}, u32[]{:S(2)}) collective-permute-start(bf16[512,1024]{1,0:T(8,128)(2,1)} %shard_map.110.a), channel_id=1, source_target_pairs={{0,2},{2,0},{1,3},{3,1},{4,6},{6,4},{5,7},{7,5},{8,10},{10,8},{9,1... | collective-permute-start | bytes 3145736 | tf_op jit(solution)/shard_map/ppermute | solution.py:434
  24.8 3.9 %collective-permute-start.3 = (bf16[64,1024]{1,0:T(8,128)(2,1)S(1)}, bf16[64,1024]{1,0:T(8,128)(2,1)}, u32[]{:S(2)}, u32[]{:S(2)}) collective-permute-start(bf16[64,1024]{1,0:T(8,128)(2,1)S(1)} %collective-permute-done.1.fetched), channel_id=1, source_target_pairs={{0,1},{1,0},{2,3},{3,2},{4,5},{5,4},{6,7},{7,6},{8,9},{9,8},{10,11... | collective-permute-start | bytes 393224 | tf_op jit(solution)/shard_map/ppermute | solution.py:437
  31.8 4.9 %collective-permute-start.5 = (bf16[32,512]{1,0:T(8,128)(2,1)S(1)}, bf16[32,512]{1,0:T(8,128)(2,1)S(1)}, u32[]{:S(2)}, u32[]{:S(2)}) collective-permute-start(bf16[32,512]{1,0:T(8,128)(2,1)S(1)} %get-tuple-element.400.a), channel_id=1, source_target_pairs={{0,4},{4,0},{8,12},{12,8},{1,5},{5,1},{9,13},{13,9},{2,6},{6,2},{1... | collective-permute-start | bytes 98312 | tf_op jit(solution)/shard_map/ppermute | solution.py:536
  36.7 3.4 %collective-permute-start.6 = (bf16[512,512]{1,0:T(8,128)(2,1)S(1)}, bf16[512,512]{1,0:T(8,128)(2,1)S(1)}, u32[]{:S(2)}, u32[]{:S(2)}) collective-permute-start(bf16[512,512]{1,0:T(8,128)(2,1)S(1)} %get-tuple-element.403), channel_id=1, source_target_pairs={{0,1},{1,0},{2,3},{3,2},{4,5},{5,4},{6,7},{7,6},{8,9},{9,8},{10,11... | collective-permute-start | bytes 1572872 | tf_op jit(solution)/shard_map/ppermute | solution.py:437
  36.7 30.2 %collective-permute-start.11 = (bf16[512,1024]{1,0:T(8,128)(2,1)}, bf16[512,1024]{1,0:T(8,128)(2,1)}, u32[]{:S(2)}, u32[]{:S(2)}) collective-permute-start(bf16[512,1024]{1,0:T(8,128)(2,1)} %get-tuple-element.443), channel_id=1, source_target_pairs={{0,4},{5,1},{4,8},{9,5},{8,12},{13,9},{2,6},{7,3},{6,10},{11,7},{1... | collective-permute-start | bytes 3145736 | tf_op jit(solution)/shard_map/ppermute | solution.py:431
  40.1 12.2 %collective-permute-start.9 = (bf16[32,512]{1,0:T(8,128)(2,1)S(1)}, bf16[32,512]{1,0:T(8,128)(2,1)S(1)}, u32[]{:S(2)}, u32[]{:S(2)}) collective-permute-start(bf16[32,512]{1,0:T(8,128)(2,1)S(1)} %shard_map.114.part), channel_id=1, source_target_pairs={{0,8},{4,12},{8,0},{12,4},{1,9},{5,13},{9,1},{13,5},{2,10},{6,14},... | collective-permute-start | bytes 98312 | tf_op jit(solution)/shard_map/ppermute | solution.py:536
  52.3 4.6 %collective-permute-start.10 = (bf16[512,512]{1,0:T(8,128)(2,1)}, bf16[512,512]{1,0:T(8,128)(2,1)S(1)}, u32[]{:S(2)}, u32[]{:S(2)}) collective-permute-start(bf16[512,512]{1,0:T(8,128)(2,1)} %get-tuple-element.434), channel_id=1, source_target_pairs={{0,1},{1,0},{2,3},{3,2},{4,5},{5,4},{6,7},{7,6},{8,9},{9,8},{10,11... | collective-permute-start | bytes 1572872 | tf_op jit(solution)/shard_map/ppermute | solution.py:437
  53.7 25.8 %collective-permute-start.14 = (bf16[512,1024]{1,0:T(8,128)(2,1)}, bf16[512,1024]{1,0:T(8,128)(2,1)S(1)}, u32[]{:S(2)}, u32[]{:S(2)}) collective-permute-start(bf16[512,1024]{1,0:T(8,128)(2,1)} %copy-done.42), channel_id=1, source_target_pairs={{0,4},{5,1},{4,8},{9,5},{8,12},{13,9},{2,6},{7,3},{6,10},{11,7},{1... | collective-permute-start | bytes 3145736 | tf_op jit(solution)/shard_map/ppermute | solution.py:431
  62.2 24.0 %collective-permute-start.15 = (bf16[512,1024]{1,0:T(8,128)(2,1)S(1)}, bf16[512,1024]{1,0:T(8,128)(2,1)S(1)}, u32[]{:S(2)}, u32[]{:S(2)}) collective-permute-start(bf16[512,1024]{1,0:T(8,128)(2,1)S(1)} %shard_map.116.a), channel_id=1, source_target_pairs={{0,2},{2,0},{1,3},{3,1},{4,6},{6,4},{5,7},{7,5},{8,10},{10,8},{9,1... | collective-permute-start | bytes 3145736 | tf_op jit(solution)/shard_map/ppermute | solution.py:434
  66.9 4.6 %collective-permute-start.12 = (bf16[128,1024]{1,0:T(8,128)(2,1)S(1)}, bf16[128,1024]{1,0:T(8,128)(2,1)S(1)}, u32[]{:S(2)}, u32[]{:S(2)}) collective-permute-start(bf16[128,1024]{1,0:T(8,128)(2,1)S(1)} %get-tuple-element.462), channel_id=1, source_target_pairs={{0,1},{1,0},{2,3},{3,2},{4,5},{5,4},{6,7},{7,6},{8,9},{9,8},{10,11... | collective-permute-start | bytes 786440 | tf_op jit(solution)/shard_map/ppermute | solution.py:437
  72.4 7.1 %collective-permute-start.13 = (bf16[512,512]{1,0:T(8,128)(2,1)S(1)}, bf16[512,512]{1,0:T(8,128)(2,1)S(1)}, u32[]{:S(2)}, u32[]{:S(2)}) collective-permute-start(bf16[512,512]{1,0:T(8,128)(2,1)S(1)} %get-tuple-element.481), channel_id=1, source_target_pairs={{0,1},{1,0},{2,3},{3,2},{4,5},{5,4},{6,7},{7,6},{8,9},{9,8},{10,11... | collective-permute-start | bytes 1572872 | tf_op jit(solution)/shard_map/ppermute | solution.py:437
  72.4 27.1 %collective-permute-start.17 = (bf16[512,1024]{1,0:T(8,128)(2,1)}, bf16[512,1024]{1,0:T(8,128)(2,1)}, u32[]{:S(2)}, u32[]{:S(2)}) collective-permute-start(bf16[512,1024]{1,0:T(8,128)(2,1)} %get-tuple-element.531), channel_id=1, source_target_pairs={{0,4},{5,1},{4,8},{9,5},{8,12},{13,9},{2,6},{7,3},{6,10},{11,7},{1... | collective-permute-start | bytes 3145736 | tf_op jit(solution)/shard_map/ppermute | solution.py:431
  76.7 22.8 %collective-permute-start.18 = (bf16[512,1024]{1,0:T(8,128)(2,1)}, bf16[512,1024]{1,0:T(8,128)(2,1)}, u32[]{:S(2)}, u32[]{:S(2)}) collective-permute-start(bf16[512,1024]{1,0:T(8,128)(2,1)} %shard_map.117.ours), channel_id=1, source_target_pairs={{0,1},{1,0},{2,3},{3,2},{4,5},{5,4},{6,7},{7,6},{8,9},{9,8},{10,11... | collective-permute-start | bytes 3145736 | tf_op jit(solution)/shard_map/ppermute | solution.py:437
  87.2 3.7 %collective-permute-start.16 = (bf16[512,512]{1,0:T(8,128)(2,1)}, bf16[512,512]{1,0:T(8,128)(2,1)}, u32[]{:S(2)}, u32[]{:S(2)}) collective-permute-start(bf16[512,512]{1,0:T(8,128)(2,1)} %get-tuple-element.528), channel_id=1, source_target_pairs={{0,1},{1,0},{2,3},{3,2},{4,5},{5,4},{6,7},{7,6},{8,9},{9,8},{10,11... | collective-permute-start | bytes 1572872 | tf_op jit(solution)/shard_map/ppermute | solution.py:437
  87.2 44.9 %collective-permute-start.21 = (bf16[512,1024]{1,0:T(8,128)(2,1)}, bf16[512,1024]{1,0:T(8,128)(2,1)S(1)}, u32[]{:S(2)}, u32[]{:S(2)}) collective-permute-start(bf16[512,1024]{1,0:T(8,128)(2,1)} %copy-done.41), channel_id=1, source_target_pairs={{0,4},{5,1},{4,8},{9,5},{8,12},{13,9},{2,6},{7,3},{6,10},{11,7},{1... | collective-permute-start | bytes 3145736 | tf_op jit(solution)/shard_map/ppermute | solution.py:431
  96.8 39.7 %collective-permute-start.22 = (bf16[512,1024]{1,0:T(8,128)(2,1)}, bf16[512,1024]{1,0:T(8,128)(2,1)}, u32[]{:S(2)}, u32[]{:S(2)}) collective-permute-start(bf16[512,1024]{1,0:T(8,128)(2,1)} %shard_map.122.a), channel_id=1, source_target_pairs={{0,2},{2,0},{1,3},{3,1},{4,6},{6,4},{5,7},{7,5},{8,10},{10,8},{9,1... | collective-permute-start | bytes 3145736 | tf_op jit(solution)/shard_map/ppermute | solution.py:434
  100.4 23.2 %collective-permute-start.19 = (bf16[64,1024]{1,0:T(8,128)(2,1)S(1)}, bf16[64,1024]{1,0:T(8,128)(2,1)S(1)}, u32[]{:S(2)}, u32[]{:S(2)}) collective-permute-start(bf16[64,1024]{1,0:T(8,128)(2,1)S(1)} %split.28), channel_id=1, source_target_pairs={{0,2},{2,0},{1,3},{3,1},{4,6},{6,4},{5,7},{7,5},{8,10},{10,8},{9,1... | collective-permute-start | bytes 393224 | tf_op jit(solution)/shard_map/ppermute | solution.py:434
  123.7 8.4 %collective-permute-start.20 = (bf16[512,512]{1,0:T(8,128)(2,1)S(1)}, bf16[512,512]{1,0:T(8,128)(2,1)S(1)}, u32[]{:S(2)}, u32[]{:S(2)}) collective-permute-start(bf16[512,512]{1,0:T(8,128)(2,1)S(1)} %get-tuple-element.578), channel_id=1, source_target_pairs={{0,1},{1,0},{2,3},{3,2},{4,5},{5,4},{6,7},{7,6},{8,9},{9,8},{10,11... | collective-permute-start | bytes 1572872 | tf_op jit(solution)/shard_map/ppermute | solution.py:437
  123.7 24.9 %collective-permute-start.24 = (bf16[512,1024]{1,0:T(8,128)(2,1)}, bf16[512,1024]{1,0:T(8,128)(2,1)}, u32[]{:S(2)}, u32[]{:S(2)}) collective-permute-start(bf16[512,1024]{1,0:T(8,128)(2,1)} %get-tuple-element.634), channel_id=1, source_target_pairs={{0,4},{5,1},{4,8},{9,5},{8,12},{13,9},{2,6},{7,3},{6,10},{11,7},{1... | collective-permute-start | bytes 3145736 | tf_op jit(solution)/shard_map/ppermute | solution.py:431
  128.5 20.2 %collective-permute-start.25 = (bf16[512,1024]{1,0:T(8,128)(2,1)}, bf16[512,1024]{1,0:T(8,128)(2,1)}, u32[]{:S(2)}, u32[]{:S(2)}) collective-permute-start(bf16[512,1024]{1,0:T(8,128)(2,1)} %shard_map.123.ours), channel_id=1, source_target_pairs={{0,1},{1,0},{2,3},{3,2},{4,5},{5,4},{6,7},{7,6},{8,9},{9,8},{10,11... | collective-permute-start | bytes 3145736 | tf_op jit(solution)/shard_map/ppermute | solution.py:437
  136.5 30.5 %collective-permute-start.27 = (bf16[512,1024]{1,0:T(8,128)(2,1)}, bf16[512,1024]{1,0:T(8,128)(2,1)}, u32[]{:S(2)}, u32[]{:S(2)}) collective-permute-start(bf16[512,1024]{1,0:T(8,128)(2,1)} %get-tuple-element.690), channel_id=1, source_target_pairs={{0,4},{5,1},{4,8},{9,5},{8,12},{13,9},{2,6},{7,3},{6,10},{11,7},{1... | collective-permute-start | bytes 3145736 | tf_op jit(solution)/shard_map/ppermute | solution.py:431
  149.0 25.9 %collective-permute-start.32 = (bf16[512,1024]{1,0:T(8,128)(2,1)S(1)}, bf16[512,1024]{1,0:T(8,128)(2,1)S(1)}, u32[]{:S(2)}, u32[]{:S(2)}) collective-permute-start(bf16[512,1024]{1,0:T(8,128)(2,1)S(1)} %shard_map.127.a), channel_id=1, source_target_pairs={{0,2},{2,0},{1,3},{3,1},{4,6},{6,4},{5,7},{7,5},{8,10},{10,8},{9,1... | collective-permute-start | bytes 3145736 | tf_op jit(solution)/shard_map/ppermute | solution.py:434
  167.1 2.6 %collective-permute-start.31 = (bf16[256,1024]{1,0:T(8,128)(2,1)S(1)}, bf16[256,1024]{1,0:T(8,128)(2,1)S(1)}, u32[]{:S(2)}, u32[]{:S(2)}) collective-permute-start(bf16[256,1024]{1,0:T(8,128)(2,1)S(1)} %get-tuple-element.729), channel_id=1, source_target_pairs={{0,1},{1,0},{2,3},{3,2},{4,5},{5,4},{6,7},{7,6},{8,9},{9,8},{10,11... | collective-permute-start | bytes 1572872 | tf_op jit(solution)/shard_map/ppermute | solution.py:437
  167.4 2.4 %collective-permute-start.30 = (bf16[256,1024]{1,0:T(8,128)(2,1)S(1)}, bf16[256,1024]{1,0:T(8,128)(2,1)S(1)}, u32[]{:S(2)}, u32[]{:S(2)}) collective-permute-start(bf16[256,1024]{1,0:T(8,128)(2,1)S(1)} %get-tuple-element.728), channel_id=1, source_target_pairs={{0,1},{1,0},{2,3},{3,2},{4,5},{5,4},{6,7},{7,6},{8,9},{9,8},{10,11... | collective-permute-start | bytes 1572872 | tf_op jit(solution)/shard_map/ppermute | solution.py:437
  169.4 2.4 %collective-permute-start.28 = (bf16[256,1024]{1,0:T(8,128)(2,1)S(1)}, bf16[256,1024]{1,0:T(8,128)(2,1)S(1)}, u32[]{:S(2)}, u32[]{:S(2)}) collective-permute-start(bf16[256,1024]{1,0:T(8,128)(2,1)S(1)} %get-tuple-element.730), channel_id=1, source_target_pairs={{0,1},{1,0},{2,3},{3,2},{4,5},{5,4},{6,7},{7,6},{8,9},{9,8},{10,11... | collective-permute-start | bytes 1572872 | tf_op jit(solution)/shard_map/ppermute | solution.py:437
  174.9 2.8 %collective-permute-start.34 = (bf16[512,1024]{1,0:T(8,128)(2,1)S(1)}, bf16[512,1024]{1,0:T(8,128)(2,1)}, u32[]{:S(2)}, u32[]{:S(2)}) collective-permute-start(bf16[512,1024]{1,0:T(8,128)(2,1)S(1)} %shard_map.128.ours), channel_id=1, source_target_pairs={{0,1},{1,0},{2,3},{3,2},{4,5},{5,4},{6,7},{7,6},{8,9},{9,8},{10,11... | collective-permute-start | bytes 3145736 | tf_op jit(solution)/shard_map/ppermute | solution.py:437
  176.3 4.6 %collective-permute-start.33 = (bf16[512,1024]{1,0:T(8,128)(2,1)}, bf16[512,1024]{1,0:T(8,128)(2,1)S(1)}, u32[]{:S(2)}, u32[]{:S(2)}) collective-permute-start(bf16[512,1024]{1,0:T(8,128)(2,1)} %shard_map.132.ours), channel_id=1, source_target_pairs={{0,1},{1,0},{2,3},{3,2},{4,5},{5,4},{6,7},{7,6},{8,9},{9,8},{10,11... | collective-permute-start | bytes 3145736 | tf_op jit(solution)/shard_map/ppermute | solution.py:437
  (48 other events, 329.3 us)

commit v3 on v2

--- a/solution.py
+++ b/solution.py
@@ -96,7 +96,7 @@
     return pl.BlockSpec(array.shape, lambda *_: (0,) * array.ndim)
 
 
-def call(body, table, grid, arrays, specs, outs, out_specs, scratch, flops, aliases=None):
+def call(body, table, grid, arrays, specs, outs, out_specs, scratch, flops, aliases=None, limit=48):
     moved = sum(v.size * v.dtype.itemsize for v in arrays)
     return pl.pallas_call(
         body,
@@ -109,13 +109,19 @@
         ),
         out_shape=outs,
         input_output_aliases=aliases or {},
-        compiler_params=pltpu.CompilerParams(vmem_limit_bytes=48 * 1024 * 1024),
+        compiler_params=pltpu.CompilerParams(vmem_limit_bytes=limit * 1024 * 1024),
         cost_estimate=pl.CostEstimate(flops=1, bytes_accessed=1, transcendentals=0),
     )(table, *arrays)
 
 
-def hop_body(table, grads, weight, came, away, goes, share):
-    share[...] = away[...]
+FREE = ()
+HOP_STEPS = 2
+
+
+def hop_body(table, grads, weight, came, goes, share):
+    @pl.when(pl.program_id(0) == table[2])
+    def _():
+        share[...] = came[...]
 
     @pl.when(table[1] == 0)
     def _():
@@ -129,18 +135,17 @@
 
 def hop(table, grads, weight, came):
     rows, width = came.shape
-    half = width // 2
-    cols = pl.BlockSpec((rows, half), lambda j, t: (0, j))
+    half, step = width // 2, width // HOP_STEPS
+    cols = pl.BlockSpec((rows, step), lambda j, t: (0, j))
     return call(
         hop_body,
         table,
-        (2,),
-        [grads, weight, came, came],
+        (HOP_STEPS,),
+        [grads, weight, came],
         [
             whole(grads),
-            pl.BlockSpec((half, width), lambda j, t: (2 * t[0] + j, 0)),
+            pl.BlockSpec((step, width), lambda j, t: (HOP_STEPS * t[0] + j, 0)),
             cols,
-            pl.BlockSpec((rows, half), lambda j, t: (0, t[2])),
         ],
         [jax.ShapeDtypeStruct((rows, width), B16), jax.ShapeDtypeStruct((rows, half), B16)],
         [cols, pl.BlockSpec((rows, half), lambda j, t: (0, 0))],
@@ -149,74 +154,100 @@
     )
 
 
-def copy_chosen(choice, offers, target):
-    if len(offers) == 1:
-        target[...] = offers[0][...]
-        return
+def start_chosen(choice, offers, core, target, done):
+    rows, half = target.shape
     for at, offer in enumerate(offers):
 
         @pl.when(choice == at)
         def _(offer=offer):
-            target[...] = offer[...]
-
-
-def half_spec(array, half, core_at):
-    if array.shape[1] == half:
-        return whole(array)
-    return pl.BlockSpec((array.shape[0], half), lambda j, t: (0, t[core_at]))
-
-
-def piece_body(count, table, *refs):
+            source = offer
+            if offer.shape[1] != half:
+                source = offer.at[:, pl.ds(pl.multiple_of(core * half, half), half)]
+            pltpu.make_async_copy(source, target, done).start()
+
+
+def wait_chosen(target, done):
+    pltpu.make_async_copy(target, target, done).wait()
+
+
+def piece_body(count, extra, table, *refs):
     ours, theirs = refs[:count], refs[count : 2 * count]
-    grads, their_grads, out, a, b = refs[2 * count :]
+    grads, their_grads = refs[2 * count : 2 * count + 2]
+    rest = refs[2 * count + 2 :]
+    out, a, b, done = rest[2 * extra], *rest[-3:]
+    half = a.shape[1]
 
     @pl.when(pl.program_id(0) == 0)
     def _():
-        copy_chosen(table[0], ours, a)
-        copy_chosen(table[0], theirs, b)
-
-    out[...] = (
-        dot(a[...], grads[...], 0, 0) + dot(b[...], their_grads[...], 0, 0)
-    ).astype(B16)
-
-
-def piece(table, ours, theirs, grads, their_grads):
+        start_chosen(table[0], ours, table[1], a, done.at[0])
+        start_chosen(table[0], theirs, table[1], b, done.at[1])
+        wait_chosen(a, done.at[0])
+        wait_chosen(b, done.at[1])
+
+    mix = dot(a[...], grads[...], 0, 0) + dot(b[...], their_grads[...], 0, 0)
+    out[...] = mix.astype(B16)
+    if extra:
+        maps, came, kept, sent = rest[0], rest[1], rest[3], rest[4]
+        split = kept.shape[0]
+        total = maps[...] + came[...].astype(F32)
+        kept[...] = total[:split]
+        sent[...] = total[split:].astype(B16)
+
+
+def piece(table, ours, theirs, grads, their_grads, extra=()):
     rows, width = grads.shape
     half = width // 2
-    cols = pl.BlockSpec((rows, width // 2), lambda j, t: (0, j))
+
+    def cols(count):
+        return pl.BlockSpec((count, width // 2), lambda j, t: (0, j))
+
+    split = extra[0].shape[0] // 2 if extra else 0
+    outs = [jax.ShapeDtypeStruct((half, width), B16)]
+    if extra:
+        outs.append(jax.ShapeDtypeStruct((split, width), F32))
+        outs.append(jax.ShapeDtypeStruct((split, width), B16))
     return call(
-        functools.partial(piece_body, len(ours)),
+        functools.partial(piece_body, len(ours), 1 if extra else 0),
         table,
         (2,),
-        [*ours, *theirs, grads, their_grads],
-        [half_spec(v, half, 1) for v in (*ours, *theirs)] + [cols, cols],
-        jax.ShapeDtypeStruct((half, width), B16),
-        pl.BlockSpec((half, width // 2), lambda j, t: (0, j)),
-        [pltpu.VMEM((rows, half), B16)] * 2,
+        [*ours, *theirs, grads, their_grads, *extra],
+        [pl.BlockSpec(memory_space=pltpu.HBM)] * (2 * len(ours))
+        + [cols(rows), cols(rows)]
+        + [cols(2 * split)] * len(extra),
+        outs,
+        [cols(v.shape[0]) for v in outs],
+        [pltpu.VMEM((rows, half), B16)] * 2 + [pltpu.SemaphoreType.DMA((2,))],
         0,
     )
 
 
 def query_body(groups, n, half, table, *refs):
-    offers, blocks = refs[: -5 - n], refs[-5 - n : -5]
-    own_out, other_out, rows_in, weight_in, _ = refs[-5:]
+    offers, blocks = refs[: -6 - n], refs[-6 - n : -6]
+    own_out, other_out, other_end, rows_in, weight_in, done = refs[-6:]
     rows = own_out.shape[0]
 
     @pl.when(pl.program_id(0) == 0)
     def _():
         at = 0
+        waits = []
         for step, count in enumerate(groups):
             start = pl.multiple_of(table[1 + step] * half, half)
             for side in range(2):
                 here = offers[at : at + count]
                 at += count
                 target = rows_in.at[pl.ds(side * rows, rows), pl.ds(start, half)]
-                copy_chosen(table[1 + n + step], here, target)
+                sem = done.at[2 * step + side]
+                start_chosen(table[1 + n + step], here, table[0], target, sem)
+                waits.append((target, sem))
+        for target, sem in waits:
+            wait_chosen(target, sem)
 
     for chunk in range(n):
         weight_in[pl.ds(chunk * half, half), :] = blocks[chunk][...]
     own_out[...] = dot(rows_in[pl.ds(0, rows), :], weight_in[...], 1, 0)
-    other_out[...] = dot(rows_in[pl.ds(rows, rows), :], weight_in[...], 1, 0).astype(B16)
+    other = dot(rows_in[pl.ds(rows, rows), :], weight_in[...], 1, 0).astype(B16)
+    other_out[...] = other[: rows // 2]
+    other_end[...] = other[rows // 2 :]
 
 
 def query_parts(table, offers, weight):
@@ -229,23 +260,26 @@
         return pl.BlockSpec((half, cols), lambda j, t: (2 * chunk + t[0], j))
 
     out = pl.BlockSpec((rows, cols), lambda j, t: (0, j))
+    part = pl.BlockSpec((rows // 2, cols), lambda j, t: (0, j))
     return call(
         functools.partial(query_body, [len(pair[0]) for pair in offers], n, half),
         table,
         (2,),
         [*flat] + [weight] * n,
-        [half_spec(v, half, 0) for v in flat] + [block(c) for c in range(n)],
+        [pl.BlockSpec(memory_space=pltpu.HBM)] * len(flat) + [block(c) for c in range(n)],
         [
             jax.ShapeDtypeStruct((rows, width), F32),
-            jax.ShapeDtypeStruct((rows, width), B16),
+            jax.ShapeDtypeStruct((rows // 2, width), B16),
+            jax.ShapeDtypeStruct((rows // 2, width), B16),
         ],
-        [out, out],
+        [out, part, part],
         [
             pltpu.VMEM((2 * rows, n * half), B16),
             pltpu.VMEM((n * half, cols), B16),
-            pltpu.VMEM((8, 128), F32),
+            pltpu.SemaphoreType.DMA((2 * n,)),
         ],
         0,
+        limit=28,
     )
 
 
@@ -269,49 +303,46 @@
     )
 
 
-def place_body(table, ours, theirs, *refs):
-    out = refs[-1]
-
-    @pl.when(pl.program_id(0) == 0)
-    def _():
-        out[...] = ours[...]
-
-    @pl.when(pl.program_id(0) == 1)
-    def _():
-        out[...] = theirs[...]
-
-
-def place(table, ours, theirs, target, shape):
-    half, width = ours.shape
-    arrays, specs, aliases = [ours, theirs], [whole(ours), whole(theirs)], {}
+def into_target(value, target, shape, at, body, extra, outs, steps):
+    rows, width = shape[2], shape[1]
+    block = rows // steps
+    spec = pl.BlockSpec((block, width), lambda i, t: (i, 0))
+    arrays, specs, aliases = [value, *extra], [spec] * (1 + len(extra)), {}
     if target is not None:
+        aliases = {1 + len(arrays): 0}
         arrays.append(target)
         specs.append(pl.BlockSpec(memory_space=pl.ANY))
-        aliases = {3: 0}
+    where = pl.BlockSpec((block, width), lambda i, t: (steps * t[0] + i, 0))
     return call(
-        place_body,
-        table,
-        (2,),
+        body,
+        at,
+        (steps,),
         arrays,
         specs,
-        jax.ShapeDtypeStruct(shape, B16),
-        pl.BlockSpec((half, width), lambda i, t: (t[i], 0)),
+        [jax.ShapeDtypeStruct(shape[:2], B16)] + [jax.ShapeDtypeStruct((rows, width), B16)] * outs,
+        [where] + [spec] * outs,
         [],
         0,
         aliases,
     )
 
 
-def add_body(table, a, b, out):
-    out[...] = (a[...].astype(F32) + b[...].astype(F32)).astype(B16)
-
-
-def add(a, b):
-    rows, width = a.shape
-    steps = 2 if rows >= 256 else 1
-    spec = pl.BlockSpec((rows // steps, width), lambda i, t: (i, 0))
-    out = jax.ShapeDtypeStruct(a.shape, B16)
-    return call(add_body, jnp.zeros((1,), jnp.int32), (steps,), [a, b], [spec] * 2, out, spec, [], 0)
+def place_body(table, value, *refs):
+    refs[-1][...] = value[...]
+
+
+def place(at, value, target, shape):
+    return into_target(value, target, (*shape, value.shape[0]), at, place_body, (), 0, 2)[0]
+
+
+def sum_body(table, a, b, *refs):
+    total = (a[...].astype(F32) + b[...].astype(F32)).astype(B16)
+    refs[-2][...] = total
+    refs[-1][...] = total
+
+
+def place_sum(at, a, b, target, shape, rows):
+    return into_target(a, target, (*shape, rows), at, sum_body, (b,), 1, 2)
 
 
 def ranks_body(rank, table, mine, fetched, shared, relative, tokens, grads, down, up, part):
@@ -351,8 +382,12 @@
     return call(body, table, (1,), arrays, specs, outs, [whole(v) for v in outs], [], 0)
 
 
-def maps_body(rank, table, part, came, relative, tokens, grads, low, back, kept, sent):
-    total = (part[...].astype(F32) + came[...].astype(F32)).astype(B16).astype(F32)
+def maps_body(rank, count, table, *refs):
+    relative, tokens, grads, low, back, kept, sent = refs[count:]
+    total = refs[0][...].astype(F32)
+    for part in refs[1:count]:
+        total += part[...].astype(F32)
+    total = total.astype(B16).astype(F32)
     for kind, wide in enumerate((low, back)):
         own = total[kind * rank : (kind + 1) * rank]
         for slot in range(wide.shape[0] // rank):
@@ -370,16 +405,16 @@
             sent[...] = term.astype(B16)
 
 
-def maps_of(table, rank, slots, part, came, relative, tokens, grads):
+def maps_of(table, rank, slots, parts, relative, tokens, grads):
     rows, width = tokens.shape
-    arrays = [part, came, relative, tokens, grads]
+    arrays = [*parts, relative, tokens, grads]
     outs = [
         jax.ShapeDtypeStruct((slots * rank, rows), B16),
         jax.ShapeDtypeStruct((slots * rank, rows), B16),
         jax.ShapeDtypeStruct((slots * rank, width), F32),
         jax.ShapeDtypeStruct((slots * rank, width), B16),
     ]
-    body = functools.partial(maps_body, rank)
+    body = functools.partial(maps_body, rank, len(parts))
     specs = [whole(v) for v in arrays]
     return call(body, table, (1,), arrays, specs, outs, [whole(v) for v in outs], [], 0)
 
@@ -398,19 +433,57 @@
     return call(lora_body, table, (1,), arrays, specs, [out, out], [whole(out)] * 2, [], 0)
 
 
-def finish_body(table, here, there, lora, live, out):
-    total = here[...] + there[...].astype(F32) + lora[...].astype(F32)
-    out[...] = jnp.where(live[...] > 0, total, 0.0).astype(B16)
-
-
-def finish(here, there, lora, live):
+def finish_body(table, here, live, out_lora, term, in_lora, ends, there, there_end, theirs, theirs_end, kept, other, query, token_grad, down, up):
+    for i, (mine, sums) in enumerate(((there, theirs), (there_end, theirs_end))):
+
+        @pl.when(pl.program_id(0) == i)
+        def _(mine=mine, sums=sums):
+            total = here[...] + mine[...].astype(F32) + out_lora[...].astype(F32)
+            query[...] = jnp.where(live[...] > 0, total, 0.0).astype(B16)
+            total = term[...].astype(F32) + in_lora[...].astype(F32) + ends[...].astype(F32)
+            token_grad[...] = (total + sums[...].astype(F32)).astype(B16)
+
+    @pl.when((pl.program_id(0) == 0) & (table[0] == 0))
+    def _():
+        down[...] = kept[...]
+        up[...] = other[...]
+
+    @pl.when((pl.program_id(0) == 0) & (table[0] != 0))
+    def _():
+        down[...] = other[...]
+        up[...] = kept[...]
+
+
+def finish(core, here, live, out_lora, term, in_lora, ends, *rest):
     rows, width = here.shape
+    kept = rest[-1]
     spec = pl.BlockSpec((rows // 2, width), lambda i, t: (i, 0))
     thin = pl.BlockSpec((rows // 2, 1), lambda i, t: (i, 0))
     out = jax.ShapeDtypeStruct((rows, width), B16)
-    arrays = [here, there, lora, live]
+    small = jax.ShapeDtypeStruct(kept.shape, F32)
+    return call(
+        finish_body,
+        core[None],
+        (2,),
+        [here, live, out_lora, term, in_lora, ends, *rest],
+        [spec, thin, spec, spec, spec, spec] + [whole(v) for v in rest],
+        [out, out, small, small],
+        [spec, spec, whole(small), whole(small)],
+        [],
+        0,
+    )
+
+
+def add_body(table, a, b, out):
+    out[...] = (a[...].astype(F32) + b[...].astype(F32)).astype(B16)
+
+
+def add(a, b):
+    rows, width = a.shape
+    spec = pl.BlockSpec((rows // 2, width), lambda i, t: (i, 0))
+    out = jax.ShapeDtypeStruct(a.shape, B16)
     table = jnp.zeros((1,), jnp.int32)
-    return call(finish_body, table, (2,), arrays, [spec] * 3 + [thin], out, spec, [], 0)
+    return call(add_body, table, (2,), [a, b], [spec] * 2, out, spec, [], 0)
 
 
 def shards_line(tokens, weight, down_maps, up_maps, counts, slot_of, cotangent):
@@ -435,9 +508,6 @@
 
     def other_core(value):
         return lax.ppermute(value, "dp", swap)
-
-    def other_core_halves(value):
-        return jnp.concatenate([other_core(v) for v in jnp.split(value, 2)])
 
     def numbers(*values):
         return jnp.stack([v.astype(jnp.int32) for v in values])
@@ -460,7 +530,7 @@
     st = {}
 
     def fence():
-        names = list(st)
+        names = [name for name in st if name not in FREE]
         st.update(zip(names, lax.optimization_barrier([st[name] for name in names])))
 
     def hop_of(k):
@@ -481,19 +551,22 @@
             for s in range(2)
         ]
 
-    def piece_of(step):
+    def piece_of(step, extra=()):
         table = numbers(choice_of[step], core)
-        st["mix", step] = piece(table, *offers_of(step), st["grads"], st["their_grads"])
+        both = st["grads"], st["their_grads"]
+        st["mix", step], *st["kept"] = piece(table, *offers_of(step), *both, extra)
 
     def sum_of(step):
-        st["ours", step] = add(st.pop(("mix", step)), st.pop(("x", step)))
+        at = (2 * chunk_of[step] + core)[None]
+        pair = st.pop(("mix", step)), st.pop(("x", step))
+        shape = n * width, width
+        st["wg"], st["ours", step] = place_sum(at, *pair, st.get("wg"), shape, width // 2)
 
     def place_of(step, theirs):
-        blocks = numbers(2 * chunk_of[step] + core, 2 * chunk_of[step] + 1 - core)
-        into = st.get("wg")
-        st["wg"] = place(blocks, st.pop(("ours", step)), theirs, into, (n * width, width))
-
-    st["weight"], st["tokens"] = weight, tokens
+        at = (2 * chunk_of[step] + 1 - core)[None]
+        st["wg"] = place(at, theirs, st["wg"], (n * width, width))
+
+    st["weight"], st["tokens"], st["z"] = weight, tokens, z
     line = along(tokens)
     st["their_tokens"] = other_core(tokens)
     theirs = other_core(cotangent)
@@ -514,7 +587,6 @@
     piece_of(0)
     swapped = other_tenant(st["mix", 0])
     shared = other_core(st["fetched"])
-    st["term"] = term_of(z[None], st["grads"], st["weight"])
     names = ("relative", "tokens", "grads")
     st["down"], st["up"], st["part"] = ranks_of(
         core[None], rank, st.pop("mine"), st.pop("fetched"), shared, *[st[v] for v in names]
@@ -529,28 +601,26 @@
         last = k == 2 * n
         if not last:
             hop_of(k)
-        if side == 1:
-            st["x", step - 1] = swapped
-        if k in (2, 3):
-            pairs = [(i, i ^ (k - 1)) for i in range(n)]
-            st["came"] = lax.ppermute(st["part"], "tensor", pairs)
-        if k == 4:
-            st["maps"] = st["maps"] + other_core(st.pop("for_sibling")).astype(F32)
-        if k == 6:
-            kept, sent = jnp.split(st.pop("maps"), 2)
-            st["kept"] = kept + other_tenant(sent.astype(B16)).astype(F32)
-        if last:
-            kept = st.pop("kept")
-            other = other_core(kept)
-            down_grad = jnp.where(core == 0, kept, other).reshape(held, rank, width)
-            st["up_grad"] = jnp.where(core == 0, other, kept).reshape(held, rank, width)
-            st["down_grad"] = jnp.swapaxes(down_grad, 1, 2)
+        if k == 2:
+            for d in range(1, n):
+                pairs = [(i, (i + d) % n) for i in range(n)]
+                st["part", d] = lax.ppermute(st["part"], "tensor", pairs)
         fence()
         if not last:
             coming = along(st.pop("sent"))
             st["shared", t - 1, side] = other_core(st.pop("share"))
         if side == 1:
-            piece_of(step)
+            extra = ()
+            if step == 2:
+                extra = st.pop("maps"), st.pop("came")
+            if step == n - 1:
+                kept = st.pop("kept")
+            piece_of(step, extra)
+            if step == n - 1:
+                st["kept"] = kept[:1]
+                st["maps_x"] = other_tenant(kept[1])
+            st["x", step - 1] = swapped
+            fence()
             swapped = other_tenant(st["mix", step])
             sum_of(step - 1)
         elif 4 <= k < 2 * n:
@@ -558,23 +628,23 @@
         if k >= 6 and side == 0:
             place_of(step - 3, st.pop("theirs"))
         if k == 2:
-            st["part"] = add(st["part"], st.pop("came"))
-        if k == 3:
             st["low"], st["back"], st["maps"], st["for_sibling"] = maps_of(
                 core[None],
                 rank,
                 slots,
-                st.pop("part"),
-                st.pop("came"),
+                [st.pop("part")] + [st.pop(("part", d)) for d in range(1, n)],
                 *[st[v] for v in names],
             )
+            st["came"] = other_core(st.pop("for_sibling"))
         if k == 4:
+            st["term"] = term_of(st["z"][None], st["grads"], st["weight"])
+        if k == 6:
             maps = [st.pop(v) for v in ("low", "up", "back", "down")]
             st["lora_out"], st["lora_in"] = lora_of(*maps)
         if last:
             offers = [offers_of(s) for s in range(n)]
             table = numbers(core, *chunk_of, *choice_of)
-            st["query_here"], st["query_there"] = query_parts(table, offers, st["weight"])
+            st["query_here"], *st["query_there"] = query_parts(table, offers, st["weight"])
         st["line", (k - 1) // 2 + 1, 1 - side] = line
         line = coming
         if side == 1 and wg_share is not None:
@@ -582,19 +652,27 @@
             wg_share = None
         fence()
 
-    theirs = other_core_halves(st["line", n, 1])
-    there = other_core_halves(st.pop("query_there"))
-    total = st.pop("term").astype(F32) + st.pop("lora_in").astype(F32)
-    total = total + st["line", n, 0].astype(F32) + theirs.astype(F32)
-    st["token_grad"] = total.astype(B16)
-    st["query"] = finish(st.pop("query_here"), there, st.pop("lora_out"), st.pop("live"))
+    kept = st.pop("kept")[0] + st.pop("maps_x").astype(F32)
+    other = other_core(kept)
+    there = [other_core(v) for v in st.pop("query_there")]
+    theirs = [other_core(v) for v in jnp.split(st["line", n, 1], 2)]
+    sums = [st.pop(v) for v in ("query_here", "live", "lora_out", "term", "lora_in")]
+    ends = st["line", n, 0]
+    done = finish(core, *sums, ends, *there, *theirs, kept, other)
+    st["query"], st["token_grad"], down_grad, up_grad = done
+    st["down_grad"] = jnp.swapaxes(down_grad.reshape(held, rank, width), 1, 2)
+    st["up_grad"] = up_grad.reshape(held, rank, width)
     fence()
     st["x", n - 1] = swapped
     fence()
-    sum_of(n - 1)
-    shares = [other_core(st["ours", step]) for step in (n - 2, n - 1)]
-    for step in (n - 2, n - 1):
-        place_of(step, shares[step - n + 2])
+    st["ours", n - 1] = add(st["mix", n - 1], st["x", n - 1])
+    earlier = other_core(st["ours", n - 2])
+    theirs = other_core(st["ours", n - 1])
+    shape = n * width, width
+    mine_at = (2 * chunk_of[n - 1] + core)[None]
+    st["wg"] = place(mine_at, st["ours", n - 1], st["wg"], shape)
+    place_of(n - 2, earlier)
+    place_of(n - 1, theirs)
     return st["query"], st["token_grad"], st["wg"], st["down_grad"], st["up_grad"]
 
 

time: 185 us -> 168 us (0.908)
  waiting for transfers between devices: 26.5 us -> 15.3 us
  local copies, waits for them, and re-layouts: 15.9 us -> 22.5 us
  starting transfers between devices: 44.8 us -> 39.1 us
  other arithmetic: 14.4 us -> 9.38 us
    ppermute x6, waiting for transfers between devices: 19 us -> 9.11 us  [other_tenant(): return lax.ppermute(value, 'tenant', swap)]
    unnamed x90 -> x86, local copies, waits for them, and re-layouts: 13 us -> 20.8 us
    ppermute x2 -> x3, waiting for transfers between devices: 5.27 us -> 0.01 us  [shards_line(): st['part', d] = lax.ppermute(st['part'], 'tensor', pairs)]
    ppermute x8, starting transfers between devices: 32.2 us -> 27.4 us  [along(): return lax.ppermute(value, ('tensor', 'dp'), line_pairs)]
    ppermute x19, waiting for transfers between devices: 2.18 us -> 6.14 us  [other_core(): return lax.ppermute(value, 'dp', swap)]
    convert_element_type x1 -> x0, other arithmetic: 3.1 us -> none  [shards_line(): st['token_grad'] = total.astype(B16)]
    ppermute x2 -> x3, starting transfers between devices: 1.6 us -> 3.83 us  [shards_line(): st['part', d] = lax.ppermute(st['part'], 'tensor', pairs)]
    ppermute x6, starting transfers between devices: 7.12 us -> 5.25 us  [other_tenant(): return lax.ppermute(value, 'tenant', swap)]
  transfers between devices with their start and end apart: 35 -> 36, of which waited for: 8 -> 9; matrix products, arithmetic and copies ran while one was open for 9% -> 7% of each run, Pallas kernels for 42% -> 47%
where the time goes in v3:
time: 168 us; the launch traced here: 167 us
  Pallas kernels  79.5 us (47%)
  starting transfers between devices  39.1 us (23%)
  local copies, waits for them, and re-layouts  22.5 us (13%)
  waiting for transfers between devices  15.3 us (9%)
  other arithmetic  9.38 us (6%)
    pallas_call x25, Pallas kernels, call(): pl.pallas_call(body, grid_spec=pltpu.PrefetchScalarGridSpec(num_scalar_pr...  79.5 us
    ppermute x8, starting transfers between devices, along(): return lax.ppermute(value, ('tensor', 'dp'), line_pairs)  27.4 us
    unnamed x86, local copies, waits for them, and re-layouts  20.8 us
    ppermute x6, waiting for transfers between devices, other_tenant(): return lax.ppermute(value, 'tenant', swap)  9.11 us
    ppermute x19, waiting for transfers between devices, other_core(): return lax.ppermute(value, 'dp', swap)  6.14 us
    ppermute x6, starting transfers between devices, other_tenant(): return lax.ppermute(value, 'tenant', swap)  5.25 us
    ppermute x3, starting transfers between devices, shards_line(): st['part', d] = lax.ppermute(st['part'], 'tensor', pairs)  3.83 us
  transfers between devices with their start and end apart: 36, of which 9 were waited for; matrix products, arithmetic and copies ran while one was open for 7% of the time, Pallas kernels for 47%

profile of v3, /device:TPU:0, one launch (start us, length us, event | category | flops | bytes accessed | tf_op | source)
XLA Modules:
  0.0 167.0 jit_solution(635595266940371486)
XLA Ops:
  1.1 4.6 %collective-permute-start.4 = (bf16[512,1024]{1,0:T(8,128)(2,1)}, bf16[512,1024]{1,0:T(8,128)(2,1)S(1)}, u32[]{:S(2)}, u32[]{:S(2)}) collective-permute-start(bf16[512,1024]{1,0:T(8,128)(2,1)} %refs_0_.1), channel_id=1, source_target_pairs={{0,4},{5,1},{4,8},{9,5},{8,12},{13,9},{2,6},{7,3},{6,10},{11,7},{1... | collective-permute-start | bytes 3145736 | tf_op jit(solution)/shard_map/ppermute | solution.py:504
  14.8 1.7 %broadcast_select_fusion.refs_3_.grads.refs_5_.refs_9_ = bf16[512,1024]{1,0:T(8,128)(2,1)S(1)} fusion(bf16[512,1024]{1,0:T(8,128)(2,1)} %collective-permute-done.2, pred[512]{0:T(512)(128)(4,1)S(1)} %subtract_compare_fusion.1), kind=kLoop, calls=%fused_computation | loop fusion | flops 524288 | bytes 2097664 | tf_op jit(solution)/shard_map/jit(_where)/select_n | solution.py:583
  16.6 4.4 %collective-permute-start.10 = (bf16[512,1024]{1,0:T(8,128)(2,1)}, bf16[512,1024]{1,0:T(8,128)(2,1)}, u32[]{:S(2)}, u32[]{:S(2)}) collective-permute-start(bf16[512,1024]{1,0:T(8,128)(2,1)} %collective-permute-done.refs_1_), channel_id=1, source_target_pairs={{0,4},{5,1},{4,8},{9,5},{8,12},{13,9},{2,6},{7,3},{6,10},{11,7},{1... | collective-permute-start | bytes 3145736 | tf_op jit(solution)/shard_map/ppermute | solution.py:504
  22.3 4.2 %shard_map.110.a = bf16[512,1024]{1,0:T(8,128)(2,1)} custom-call(s32[2]{0:T(128)S(1)} %pad_add_fusion.table, bf16[512,1024]{1,0:T(8,128)(2,1)S(1)} %copy-done.5, bf16[512,1024]{1,0:T(8,128)(2,1)} %collective-permute-done.refs_1_, bf16[512,1024]{1,0:T(8,128)(2,1)S(1)} %broadcast_select_fusion.1.refs_2_.grads.refs_6_.refs_4_.refs_8_, ...), custom_call_target="tpu_custom_call" | custom-call | flops 1 | bytes 1 | tf_op jit(solution)/shard_map/pallas_call | solution.py:101
  26.5 1.8 %shard_map.111 = (bf16[128,1024]{1,0:T(8,128)(2,1)S(1)}, bf16[128,1024]{1,0:T(8,128)(2,1)S(1)}, bf16[32,512]{1,0:T(8,128)(2,1)S(1)}) custom-call(s32[1]{0:T(128)} %bitcast.9.table, bf16[2,64,1024]{2,1,0:T(8,128)(2,1)S(1)} %pad_maximum_fusion.mine, bf16[64,1024]{1,0:T(8,128)(2,1)S(1)} %collective-permute-done.1.fetched, ...), custom_call_target="tpu_custom_call" | custom-call | flops 1 | bytes 1 | tf_op jit(solution)/shard_map/pallas_call | solution.py:101
  30.4 2.5 %collective-permute-start.6 = (bf16[32,512]{1,0:T(8,128)(2,1)S(1)}, bf16[32,512]{1,0:T(8,128)(2,1)S(1)}, u32[]{:S(2)}, u32[]{:S(2)}) collective-permute-start(bf16[32,512]{1,0:T(8,128)(2,1)S(1)} %get-tuple-element.507.refs_0_), channel_id=1, source_target_pairs={{0,8},{4,12},{8,0},{12,4},{1,9},{5,13},{9,1},{13,5},{2,10},{6,14},... | collective-permute-start | bytes 98312 | tf_op jit(solution)/shard_map/ppermute | solution.py:607
  33.6 4.1 %shard_map.112 = (bf16[512,1024]{1,0:T(8,128)(2,1)}, bf16[512,512]{1,0:T(8,128)(2,1)S(1)}) custom-call(s32[3]{0:T(128)S(1)} %get-tuple-element.912.table, bf16[512,1024]{1,0:T(8,128)(2,1)S(1)} %broadcast_select_fusion.1.refs_2_.grads.refs_6_.refs_4_.refs_8_, bf16[4096,1024]{1,0:T(8,128)(2,1)} %refs_25_, ...), custom_call_target="tpu_custom_call" | custom-call | flops 1 | bytes 1 | tf_op jit(solution)/shard_map/pallas_call | solution.py:101
  38.4 3.2 %collective-permute-start.13 = (bf16[512,1024]{1,0:T(8,128)(2,1)}, bf16[512,1024]{1,0:T(8,128)(2,1)}, u32[]{:S(2)}, u32[]{:S(2)}) collective-permute-start(bf16[512,1024]{1,0:T(8,128)(2,1)} %get-tuple-element.576), channel_id=1, source_target_pairs={{0,4},{5,1},{4,8},{9,5},{8,12},{13,9},{2,6},{7,3},{6,10},{11,7},{1... | collective-permute-start | bytes 3145736 | tf_op jit(solution)/shard_map/ppermute | solution.py:504
  46.2 4.5 %shard_map.114 = (bf16[512,1024]{1,0:T(8,128)(2,1)}, bf16[512,512]{1,0:T(8,128)(2,1)}) custom-call(s32[3]{0:T(128)S(1)} %get-tuple-element.912.table, bf16[512,1024]{1,0:T(8,128)(2,1)S(1)} %broadcast_select_fusion.refs_3_.grads.refs_5_.refs_9_, bf16[4096,1024]{1,0:T(8,128)(2,1)} %refs_25_, bf16[512,1024]{1,0:T(8,128)(2,1)} %collective-permute-done.10.came.refs_3_.refs_5_.refs_11_), custom_call_target="tpu_custom_call" | custom-call | flops 1 | bytes 1 | tf_op jit(solution)/shard_map/pallas_call | solution.py:101
  50.6 2.4 %collective-permute-start.15 = (bf16[512,1024]{1,0:T(8,128)(2,1)}, bf16[512,1024]{1,0:T(8,128)(2,1)}, u32[]{:S(2)}, u32[]{:S(2)}) collective-permute-start(bf16[512,1024]{1,0:T(8,128)(2,1)} %get-tuple-element.622), channel_id=1, source_target_pairs={{0,4},{5,1},{4,8},{9,5},{8,12},{13,9},{2,6},{7,3},{6,10},{11,7},{1... | collective-permute-start | bytes 3145736 | tf_op jit(solution)/shard_map/ppermute | solution.py:504
  54.2 4.0 %shard_map.115.a = bf16[512,1024]{1,0:T(8,128)(2,1)} custom-call(s32[2]{0:T(128)S(1)} %pad_add_fusion.1.table, bf16[512,512]{1,0:T(8,128)(2,1)S(1)} %collective-permute-done.11.refs_0_.refs_2_.refs_6_, bf16[512,1024]{1,0:T(8,128)(2,1)S(1)} %collective-permute-done.4.came.refs_1_.refs_3_.refs_7_, bf16[512,512]{1,0:T(8,128)(2,1)S(1)} %copy-done.11, ...), custom_call_target="tpu_custom_call" | custom-call | flops 1 | bytes 1 | tf_op jit(solution)/shard_map/pallas_call | solution.py:101
  58.2 5.5 %collective-permute-done.12.b = bf16[512,1024]{1,0:T(8,128)(2,1)} collective-permute-done((bf16[512,1024]{1,0:T(8,128)(2,1)}, bf16[512,1024]{1,0:T(8,128)(2,1)}, u32[]{:S(2)}, u32[]{:S(2)}) %collective-permute-start.12) | collective-permute-done | bytes 1048608 | tf_op jit(solution)/shard_map/ppermute | solution.py:507
  63.7 2.6 %shard_map.116 = (bf16[4096,1024]{1,0:T(8,128)(2,1)}, bf16[512,1024]{1,0:T(8,128)(2,1)}) custom-call(s32[1]{0:T(128)} %bitcast.14.table, bf16[512,1024]{1,0:T(8,128)(2,1)} %shard_map.110.a, bf16[512,1024]{1,0:T(8,128)(2,1)} %collective-permute-done.12.b), custom_call_target="tpu_custom_call" | custom-call | flops 1 | bytes 1 | tf_op jit(solution)/shard_map/pallas_call | solution.py:101
  66.3 4.3 %shard_map.117 = (bf16[512,1024]{1,0:T(8,128)(2,1)}, bf16[512,512]{1,0:T(8,128)(2,1)S(1)}) custom-call(s32[3]{0:T(128)S(1)} %get-tuple-element.913.table, bf16[512,1024]{1,0:T(8,128)(2,1)S(1)} %broadcast_select_fusion.1.refs_2_.grads.refs_6_.refs_4_.refs_8_, bf16[4096,1024]{1,0:T(8,128)(2,1)} %refs_25_, ...), custom_call_target="tpu_custom_call" | custom-call | flops 1 | bytes 1 | tf_op jit(solution)/shard_map/pallas_call | solution.py:101
  71.2 3.2 %collective-permute-start.18 = (bf16[512,1024]{1,0:T(8,128)(2,1)}, bf16[512,1024]{1,0:T(8,128)(2,1)}, u32[]{:S(2)}, u32[]{:S(2)}) collective-permute-start(bf16[512,1024]{1,0:T(8,128)(2,1)} %get-tuple-element.700), channel_id=1, source_target_pairs={{0,4},{5,1},{4,8},{9,5},{8,12},{13,9},{2,6},{7,3},{6,10},{11,7},{1... | collective-permute-start | bytes 3145736 | tf_op jit(solution)/shard_map/ppermute | solution.py:504
  74.4 2.8 %shard_map.118.term = bf16[512,1024]{1,0:T(8,128)(2,1)S(1)} custom-call(s32[1]{0:T(128)} %bitcast.17.table, bf16[512,1024]{1,0:T(8,128)(2,1)S(1)} %broadcast_select_fusion.1.refs_2_.grads.refs_6_.refs_4_.refs_8_, bf16[4096,1024]{1,0:T(8,128)(2,1)} %refs_25_), custom_call_target="tpu_custom_call" | custom-call | flops 1 | bytes 1 | tf_op jit(solution)/shard_map/pallas_call | solution.py:101
  78.2 4.4 %shard_map.119 = (bf16[512,1024]{1,0:T(8,128)(2,1)S(1)}, bf16[512,512]{1,0:T(8,128)(2,1)}) custom-call(s32[3]{0:T(128)S(1)} %get-tuple-element.913.table, bf16[512,1024]{1,0:T(8,128)(2,1)S(1)} %copy-done.3, bf16[4096,1024]{1,0:T(8,128)(2,1)} %refs_25_, bf16[512,1024]{1,0:T(8,128)(2,1)} %collective-permute-done.15.came.refs_7_.refs_5_.refs_13_.refs_19_), custom_call_target="tpu_custom_call" | custom-call | flops 1 | bytes 1 | tf_op jit(solution)/shard_map/pallas_call | solution.py:101
  82.6 2.7 %collective-permute-start.21 = (bf16[512,1024]{1,0:T(8,128)(2,1)S(1)}, bf16[512,1024]{1,0:T(8,128)(2,1)S(1)}, u32[]{:S(2)}, u32[]{:S(2)}) collective-permute-start(bf16[512,1024]{1,0:T(8,128)(2,1)S(1)} %get-tuple-element.758), channel_id=1, source_target_pairs={{0,4},{5,1},{4,8},{9,5},{8,12},{13,9},{2,6},{7,3},{6,10},{11,7},{1... | collective-permute-start | bytes 3145736 | tf_op jit(solution)/shard_map/ppermute | solution.py:504
  89.8 5.2 %shard_map.120 = (bf16[512,1024]{1,0:T(8,128)(2,1)}, f32[64,1024]{1,0:T(8,128)S(1)}, bf16[64,1024]{1,0:T(8,128)(2,1)}) custom-call(s32[2]{0:T(128)S(1)} %pad_add_fusion.2.table, bf16[512,512]{1,0:T(8,128)(2,1)S(1)} %copy-done.15, bf16[512,1024]{1,0:T(8,128)(2,1)S(1)} %collective-permute-done.4.came.refs_1_.refs_3_.refs_7_, ...), custom_call_target="tpu_custom_call" | custom-call | flops 1 | bytes 1 | tf_op jit(solution)/shard_map/pallas_call | solution.py:101
  96.5 2.7 %shard_map.121 = (bf16[4096,1024]{1,0:T(8,128)(2,1)}, bf16[512,1024]{1,0:T(8,128)(2,1)}) custom-call(s32[1]{0:T(128)} %bitcast.19.table, bf16[512,1024]{1,0:T(8,128)(2,1)} %shard_map.115.a, bf16[512,1024]{1,0:T(8,128)(2,1)} %collective-permute-done.17.b, bf16[4096,1024]{1,0:T(8,128)(2,1)} %get-tuple-element.691.refs_0_), custom_call_target="tpu_custom_call", output_to_operand_aliasing={{0}: (3, {})} | custom-call | flops 1 | bytes 1 | tf_op jit(solution)/shard_map/pallas_call | solution.py:101
  99.2 4.5 %shard_map.122 = (bf16[512,1024]{1,0:T(8,128)(2,1)}, bf16[512,512]{1,0:T(8,128)(2,1)}) custom-call(s32[3]{0:T(128)S(1)} %add_add_fusion.2.table, bf16[512,1024]{1,0:T(8,128)(2,1)S(1)} %copy-done.1, bf16[4096,1024]{1,0:T(8,128)(2,1)} %refs_25_, bf16[512,1024]{1,0:T(8,128)(2,1)} %collective-permute-done.18.came.refs_3_.refs_17_), custom_call_target="tpu_custom_call" | custom-call | flops 1 | bytes 1 | tf_op jit(solution)/shard_map/pallas_call | solution.py:101
  104.3 3.9 %collective-permute-start.25 = (bf16[512,1024]{1,0:T(8,128)(2,1)}, bf16[512,1024]{1,0:T(8,128)(2,1)}, u32[]{:S(2)}, u32[]{:S(2)}) collective-permute-start(bf16[512,1024]{1,0:T(8,128)(2,1)} %get-tuple-element.837), channel_id=1, source_target_pairs={{0,4},{5,1},{4,8},{9,5},{8,12},{13,9},{2,6},{7,3},{6,10},{11,7},{1... | collective-permute-start | bytes 3145736 | tf_op jit(solution)/shard_map/ppermute | solution.py:504
  108.2 2.2 %shard_map.123.refs_0_ = bf16[4096,1024]{1,0:T(8,128)(2,1)} custom-call(s32[1]{0:T(128)} %bitcast.22.table, bf16[512,1024]{1,0:T(8,128)(2,1)} %collective-permute-done.19.value, bf16[4096,1024]{1,0:T(8,128)(2,1)} %get-tuple-element.742.refs_0_), custom_call_target="tpu_custom_call", output_to_operand_aliasing={{}: (2, {})} | custom-call | flops 1 | bytes 1 | tf_op jit(solution)/shard_map/pallas_call | solution.py:101
  113.2 4.1 %shard_map.125 = (bf16[512,1024]{1,0:T(8,128)(2,1)}, bf16[512,512]{1,0:T(8,128)(2,1)S(1)}) custom-call(s32[3]{0:T(128)S(1)} %add_add_fusion.2.table, bf16[512,1024]{1,0:T(8,128)(2,1)S(1)} %copy-done.4, bf16[4096,1024]{1,0:T(8,128)(2,1)} %refs_25_, bf16[512,1024]{1,0:T(8,128)(2,1)S(1)} %collective-permute-done.21.came.refs_7_.refs_21_), custom_call_target="tpu_custom_call" | custom-call | flops 1 | bytes 1 | tf_op jit(solution)/shard_map/pallas_call | solution.py:101
  117.3 3.0 %collective-permute-start.27 = (bf16[512,1024]{1,0:T(8,128)(2,1)}, bf16[512,1024]{1,0:T(8,128)(2,1)}, u32[]{:S(2)}, u32[]{:S(2)}) collective-permute-start(bf16[512,1024]{1,0:T(8,128)(2,1)} %get-tuple-element.867), channel_id=1, source_target_pairs={{0,4},{5,1},{4,8},{9,5},{8,12},{13,9},{2,6},{7,3},{6,10},{11,7},{1... | collective-permute-start | bytes 3145736 | tf_op jit(solution)/shard_map/ppermute | solution.py:504
  120.4 1.9 %collective-permute-done.22.refs_2_.refs_16_ = bf16[512,512]{1,0:T(8,128)(2,1)S(1)} collective-permute-done((bf16[512,512]{1,0:T(8,128)(2,1)S(1)}, bf16[512,512]{1,0:T(8,128)(2,1)S(1)}, u32[]{:S(2)}, u32[]{:S(2)}) %collective-permute-start.22) | collective-permute-done | bytes 524320 | tf_op jit(solution)/shard_map/ppermute | solution.py:510
  124.9 5.3 %shard_map.126.a = bf16[512,1024]{1,0:T(8,128)(2,1)} custom-call(s32[2]{0:T(128)S(1)} %pad_add_fusion.3.table, bf16[512,512]{1,0:T(8,128)(2,1)} %collective-permute-done.16.refs_2_.refs_0_.refs_8_.refs_14_, bf16[512,1024]{1,0:T(8,128)(2,1)} %collective-permute-done.13.came.refs_3_.refs_1_.refs_9_.refs_15_, ...), custom_call_target="tpu_custom_call" | custom-call | flops 1 | bytes 1 | tf_op jit(solution)/shard_map/pallas_call | solution.py:101
  130.2 2.1 %collective-permute-done.23 = bf16[64,1024]{1,0:T(8,128)(2,1)S(1)} collective-permute-done((bf16[64,1024]{1,0:T(8,128)(2,1)}, bf16[64,1024]{1,0:T(8,128)(2,1)S(1)}, u32[]{:S(2)}, u32[]{:S(2)}) %collective-permute-start.23) | collective-permute-done | bytes 131104 | tf_op jit(solution)/shard_map/ppermute | solution.py:507
  132.9 2.8 %shard_map.127 = (bf16[4096,1024]{1,0:T(8,128)(2,1)}, bf16[512,1024]{1,0:T(8,128)(2,1)}) custom-call(s32[1]{0:T(128)} %bitcast.24.table, bf16[512,1024]{1,0:T(8,128)(2,1)} %get-tuple-element.818.a, bf16[512,1024]{1,0:T(8,128)(2,1)} %collective-permute-done.24.b, bf16[4096,1024]{1,0:T(8,128)(2,1)} %shard_map.123.refs_0_), custom_call_target="tpu_custom_call", output_to_operand_aliasing={{0}: (3, {})} | custom-call | flops 1 | bytes 1 | tf_op jit(solution)/shard_map/pallas_call | solution.py:101
  135.9 2.2 %shard_map.128.refs_0_ = bf16[4096,1024]{1,0:T(8,128)(2,1)} custom-call(s32[1]{0:T(128)} %bitcast.25.table, bf16[512,1024]{1,0:T(8,128)(2,1)} %collective-permute-done.26.value, bf16[4096,1024]{1,0:T(8,128)(2,1)} %get-tuple-element.847.refs_0_), custom_call_target="tpu_custom_call", output_to_operand_aliasing={{}: (2, {})} | custom-call | flops 1 | bytes 1 | tf_op jit(solution)/shard_map/pallas_call | solution.py:101
  140.8 7.4 %shard_map.129 = (f32[512,1024]{1,0:T(8,128)S(1)}, bf16[256,1024]{1,0:T(8,128)(2,1)S(1)}, bf16[256,1024]{1,0:T(8,128)(2,1)S(1)}) custom-call(s32[9]{0:T(128)S(1)} %stack.136.table, bf16[512,1024]{1,0:T(8,128)(2,1)S(1)} %copy-done.7, bf16[512,1024]{1,0:T(8,128)(2,1)} %collective-permute-done.refs_1_, bf16[512,512]{1,0:T(8,128)(2,1)S(1)} %copy-done.16, ...), custom_call_target="tpu_custom_call" | custom-call | flops 1 | bytes 1 | tf_op jit(solution)/shard_map/pallas_call | solution.py:101
  157.0 4.4 %shard_map.130 = (bf16[512,1024]{1,0:T(8,128)(2,1)}, bf16[512,1024]{1,0:T(8,128)(2,1)}, f32[64,1024]{1,0:T(8,128)}, f32[64,1024]{1,0:T(8,128)}) custom-call(s32[1]{0:T(128)} %bitcast.9.table, f32[512,1024]{1,0:T(8,128)} %copy-done.23, f32[512,1]{1,0:T(8,128)S(1)} %copy-done.30, bf16[512,1024]{1,0:T(8,128)(2,1)S(1)} %copy-done.27, ...), custom_call_target="tpu_custom_call" | custom-call | flops 1 | bytes 1 | tf_op jit(solution)/shard_map/pallas_call | solution.py:101
  (181 shorter events, 51.1 us)
Async XLA Ops:
  0.6 15.9 %collective-permute-start = (bf16[512,1024]{1,0:T(8,128)(2,1)}, bf16[512,1024]{1,0:T(8,128)(2,1)}, u32[]{:S(2)}, u32[]{:S(2)}) collective-permute-start(bf16[512,1024]{1,0:T(8,128)(2,1)} %refs_0_.1), channel_id=1, source_target_pairs={{0,1},{1,0},{2,3},{3,2},{4,5},{5,4},{6,7},{7,6},{8,9},{9,8},{10,11... | collective-permute-start | bytes 3145736 | tf_op jit(solution)/shard_map/ppermute | solution.py:510
  1.1 28.5 %collective-permute-start.4 = (bf16[512,1024]{1,0:T(8,128)(2,1)}, bf16[512,1024]{1,0:T(8,128)(2,1)S(1)}, u32[]{:S(2)}, u32[]{:S(2)}) collective-permute-start(bf16[512,1024]{1,0:T(8,128)(2,1)} %refs_0_.1), channel_id=1, source_target_pairs={{0,4},{5,1},{4,8},{9,5},{8,12},{13,9},{2,6},{7,3},{6,10},{11,7},{1... | collective-permute-start | bytes 3145736 | tf_op jit(solution)/shard_map/ppermute | solution.py:504
  7.3 9.2 %collective-permute-start.1 = (bf16[64,1024]{1,0:T(8,128)(2,1)}, bf16[64,1024]{1,0:T(8,128)(2,1)S(1)}, u32[]{:S(2)}, u32[]{:S(2)}) collective-permute-start(bf16[64,1024]{1,0:T(8,128)(2,1)} %fusion.2), channel_id=1, source_target_pairs={{0,2},{2,0},{1,3},{3,1},{4,6},{6,4},{5,7},{7,5},{8,10},{10,8},{9,1... | collective-permute-start | bytes 393224 | tf_op jit(solution)/shard_map/ppermute | solution.py:507
  8.8 5.9 %collective-permute-start.2 = (bf16[512,1024]{1,0:T(8,128)(2,1)}, bf16[512,1024]{1,0:T(8,128)(2,1)}, u32[]{:S(2)}, u32[]{:S(2)}) collective-permute-start(bf16[512,1024]{1,0:T(8,128)(2,1)} %param.13), channel_id=1, source_target_pairs={{0,1},{1,0},{2,3},{3,2},{4,5},{5,4},{6,7},{7,6},{8,9},{9,8},{10,11... | collective-permute-start | bytes 3145736 | tf_op jit(solution)/shard_map/ppermute | solution.py:510
  16.6 29.6 %collective-permute-start.10 = (bf16[512,1024]{1,0:T(8,128)(2,1)}, bf16[512,1024]{1,0:T(8,128)(2,1)}, u32[]{:S(2)}, u32[]{:S(2)}) collective-permute-start(bf16[512,1024]{1,0:T(8,128)(2,1)} %collective-permute-done.refs_1_), channel_id=1, source_target_pairs={{0,4},{5,1},{4,8},{9,5},{8,12},{13,9},{2,6},{7,3},{6,10},{11,7},{1... | collective-permute-start | bytes 3145736 | tf_op jit(solution)/shard_map/ppermute | solution.py:504
  21.0 5.5 %collective-permute-start.3 = (bf16[64,1024]{1,0:T(8,128)(2,1)S(1)}, bf16[64,1024]{1,0:T(8,128)(2,1)}, u32[]{:S(2)}, u32[]{:S(2)}) collective-permute-start(bf16[64,1024]{1,0:T(8,128)(2,1)S(1)} %collective-permute-done.1.fetched), channel_id=1, source_target_pairs={{0,1},{1,0},{2,3},{3,2},{4,5},{5,4},{6,7},{7,6},{8,9},{9,8},{10,11... | collective-permute-start | bytes 393224 | tf_op jit(solution)/shard_map/ppermute | solution.py:510
  29.7 8.0 %collective-permute-start.5 = (bf16[32,512]{1,0:T(8,128)(2,1)S(1)}, bf16[32,512]{1,0:T(8,128)(2,1)S(1)}, u32[]{:S(2)}, u32[]{:S(2)}) collective-permute-start(bf16[32,512]{1,0:T(8,128)(2,1)S(1)} %get-tuple-element.507.refs_0_), channel_id=1, source_target_pairs={{0,4},{4,8},{8,12},{12,0},{1,5},{5,9},{9,13},{13,1},{2,6},{6,10},{... | collective-permute-start | bytes 98312 | tf_op jit(solution)/shard_map/ppermute | solution.py:607
  30.4 7.3 %collective-permute-start.6 = (bf16[32,512]{1,0:T(8,128)(2,1)S(1)}, bf16[32,512]{1,0:T(8,128)(2,1)S(1)}, u32[]{:S(2)}, u32[]{:S(2)}) collective-permute-start(bf16[32,512]{1,0:T(8,128)(2,1)S(1)} %get-tuple-element.507.refs_0_), channel_id=1, source_target_pairs={{0,8},{4,12},{8,0},{12,4},{1,9},{5,13},{9,1},{13,5},{2,10},{6,14},... | collective-permute-start | bytes 98312 | tf_op jit(solution)/shard_map/ppermute | solution.py:607
  32.9 4.8 %collective-permute-start.7 = (bf16[32,512]{1,0:T(8,128)(2,1)S(1)}, bf16[32,512]{1,0:T(8,128)(2,1)S(1)}, u32[]{:S(2)}, u32[]{:S(2)}) collective-permute-start(bf16[32,512]{1,0:T(8,128)(2,1)S(1)} %get-tuple-element.507.refs_0_), channel_id=1, source_target_pairs={{0,12},{4,0},{8,4},{12,8},{1,13},{5,1},{9,5},{13,9},{2,14},{6,2},{... | collective-permute-start | bytes 98312 | tf_op jit(solution)/shard_map/ppermute | solution.py:607
  37.7 7.6 %collective-permute-start.8 = (bf16[512,512]{1,0:T(8,128)(2,1)S(1)}, bf16[512,512]{1,0:T(8,128)(2,1)S(1)}, u32[]{:S(2)}, u32[]{:S(2)}) collective-permute-start(bf16[512,512]{1,0:T(8,128)(2,1)S(1)} %get-tuple-element.506), channel_id=1, source_target_pairs={{0,1},{1,0},{2,3},{3,2},{4,5},{5,4},{6,7},{7,6},{8,9},{9,8},{10,11... | collective-permute-start | bytes 1572872 | tf_op jit(solution)/shard_map/ppermute | solution.py:510
  37.8 25.9 %collective-permute-start.12 = (bf16[512,1024]{1,0:T(8,128)(2,1)}, bf16[512,1024]{1,0:T(8,128)(2,1)}, u32[]{:S(2)}, u32[]{:S(2)}) collective-permute-start(bf16[512,1024]{1,0:T(8,128)(2,1)} %shard_map.110.a), channel_id=1, source_target_pairs={{0,2},{2,0},{1,3},{3,1},{4,6},{6,4},{5,7},{7,5},{8,10},{10,8},{9,1... | collective-permute-start | bytes 3145736 | tf_op jit(solution)/shard_map/ppermute | solution.py:507
  38.4 27.9 %collective-permute-start.13 = (bf16[512,1024]{1,0:T(8,128)(2,1)}, bf16[512,1024]{1,0:T(8,128)(2,1)}, u32[]{:S(2)}, u32[]{:S(2)}) collective-permute-start(bf16[512,1024]{1,0:T(8,128)(2,1)} %get-tuple-element.576), channel_id=1, source_target_pairs={{0,4},{5,1},{4,8},{9,5},{8,12},{13,9},{2,6},{7,3},{6,10},{11,7},{1... | collective-permute-start | bytes 3145736 | tf_op jit(solution)/shard_map/ppermute | solution.py:504
  50.6 2.5 %collective-permute-start.11 = (bf16[512,512]{1,0:T(8,128)(2,1)}, bf16[512,512]{1,0:T(8,128)(2,1)S(1)}, u32[]{:S(2)}, u32[]{:S(2)}) collective-permute-start(bf16[512,512]{1,0:T(8,128)(2,1)} %get-tuple-element.553), channel_id=1, source_target_pairs={{0,1},{1,0},{2,3},{3,2},{4,5},{5,4},{6,7},{7,6},{8,9},{9,8},{10,11... | collective-permute-start | bytes 1572872 | tf_op jit(solution)/shard_map/ppermute | solution.py:510
  50.6 27.6 %collective-permute-start.15 = (bf16[512,1024]{1,0:T(8,128)(2,1)}, bf16[512,1024]{1,0:T(8,128)(2,1)}, u32[]{:S(2)}, u32[]{:S(2)}) collective-permute-start(bf16[512,1024]{1,0:T(8,128)(2,1)} %get-tuple-element.622), channel_id=1, source_target_pairs={{0,4},{5,1},{4,8},{9,5},{8,12},{13,9},{2,6},{7,3},{6,10},{11,7},{1... | collective-permute-start | bytes 3145736 | tf_op jit(solution)/shard_map/ppermute | solution.py:504
  70.6 7.6 %collective-permute-start.14 = (bf16[512,512]{1,0:T(8,128)(2,1)S(1)}, bf16[512,512]{1,0:T(8,128)(2,1)S(1)}, u32[]{:S(2)}, u32[]{:S(2)}) collective-permute-start(bf16[512,512]{1,0:T(8,128)(2,1)S(1)} %get-tuple-element.621), channel_id=1, source_target_pairs={{0,1},{1,0},{2,3},{3,2},{4,5},{5,4},{6,7},{7,6},{8,9},{9,8},{10,11... | collective-permute-start | bytes 1572872 | tf_op jit(solution)/shard_map/ppermute | solution.py:510
  70.6 25.9 %collective-permute-start.17 = (bf16[512,1024]{1,0:T(8,128)(2,1)}, bf16[512,1024]{1,0:T(8,128)(2,1)}, u32[]{:S(2)}, u32[]{:S(2)}) collective-permute-start(bf16[512,1024]{1,0:T(8,128)(2,1)} %shard_map.115.a), channel_id=1, source_target_pairs={{0,2},{2,0},{1,3},{3,1},{4,6},{6,4},{5,7},{7,5},{8,10},{10,8},{9,1... | collective-permute-start | bytes 3145736 | tf_op jit(solution)/shard_map/ppermute | solution.py:507
  71.2 28.0 %collective-permute-start.18 = (bf16[512,1024]{1,0:T(8,128)(2,1)}, bf16[512,1024]{1,0:T(8,128)(2,1)}, u32[]{:S(2)}, u32[]{:S(2)}) collective-permute-start(bf16[512,1024]{1,0:T(8,128)(2,1)} %get-tuple-element.700), channel_id=1, source_target_pairs={{0,4},{5,1},{4,8},{9,5},{8,12},{13,9},{2,6},{7,3},{6,10},{11,7},{1... | collective-permute-start | bytes 3145736 | tf_op jit(solution)/shard_map/ppermute | solution.py:504
  74.4 24.8 %collective-permute-start.19 = (bf16[512,1024]{1,0:T(8,128)(2,1)}, bf16[512,1024]{1,0:T(8,128)(2,1)}, u32[]{:S(2)}, u32[]{:S(2)}) collective-permute-start(bf16[512,1024]{1,0:T(8,128)(2,1)} %get-tuple-element.619), channel_id=1, source_target_pairs={{0,1},{1,0},{2,3},{3,2},{4,5},{5,4},{6,7},{7,6},{8,9},{9,8},{10,11... | collective-permute-start | bytes 3145736 | tf_op jit(solution)/shard_map/ppermute | solution.py:510
  82.6 2.9 %collective-permute-start.16 = (bf16[512,512]{1,0:T(8,128)(2,1)}, bf16[512,512]{1,0:T(8,128)(2,1)}, u32[]{:S(2)}, u32[]{:S(2)}) collective-permute-start(bf16[512,512]{1,0:T(8,128)(2,1)} %get-tuple-element.655), channel_id=1, source_target_pairs={{0,1},{1,0},{2,3},{3,2},{4,5},{5,4},{6,7},{7,6},{8,9},{9,8},{10,11... | collective-permute-start | bytes 1572872 | tf_op jit(solution)/shard_map/ppermute | solution.py:510
  82.6 30.6 %collective-permute-start.21 = (bf16[512,1024]{1,0:T(8,128)(2,1)S(1)}, bf16[512,1024]{1,0:T(8,128)(2,1)S(1)}, u32[]{:S(2)}, u32[]{:S(2)}) collective-permute-start(bf16[512,1024]{1,0:T(8,128)(2,1)S(1)} %get-tuple-element.758), channel_id=1, source_target_pairs={{0,4},{5,1},{4,8},{9,5},{8,12},{13,9},{2,6},{7,3},{6,10},{11,7},{1... | collective-permute-start | bytes 3145736 | tf_op jit(solution)/shard_map/ppermute | solution.py:504
  103.6 9.5 %collective-permute-start.20 = (bf16[512,512]{1,0:T(8,128)(2,1)}, bf16[512,512]{1,0:T(8,128)(2,1)}, u32[]{:S(2)}, u32[]{:S(2)}) collective-permute-start(bf16[512,512]{1,0:T(8,128)(2,1)} %get-tuple-element.751), channel_id=1, source_target_pairs={{0,1},{1,0},{2,3},{3,2},{4,5},{5,4},{6,7},{7,6},{8,9},{9,8},{10,11... | collective-permute-start | bytes 1572872 | tf_op jit(solution)/shard_map/ppermute | solution.py:510
  103.7 28.6 %collective-permute-start.24 = (bf16[512,1024]{1,0:T(8,128)(2,1)}, bf16[512,1024]{1,0:T(8,128)(2,1)}, u32[]{:S(2)}, u32[]{:S(2)}) collective-permute-start(bf16[512,1024]{1,0:T(8,128)(2,1)} %get-tuple-element.818.a), channel_id=1, source_target_pairs={{0,2},{2,0},{1,3},{3,1},{4,6},{6,4},{5,7},{7,5},{8,10},{10,8},{9,1... | collective-permute-start | bytes 3145736 | tf_op jit(solution)/shard_map/ppermute | solution.py:507
  104.3 31.5 %collective-permute-start.25 = (bf16[512,1024]{1,0:T(8,128)(2,1)}, bf16[512,1024]{1,0:T(8,128)(2,1)}, u32[]{:S(2)}, u32[]{:S(2)}) collective-permute-start(bf16[512,1024]{1,0:T(8,128)(2,1)} %get-tuple-element.837), channel_id=1, source_target_pairs={{0,4},{5,1},{4,8},{9,5},{8,12},{13,9},{2,6},{7,3},{6,10},{11,7},{1... | collective-permute-start | bytes 3145736 | tf_op jit(solution)/shard_map/ppermute | solution.py:504
  108.2 27.6 %collective-permute-start.26 = (bf16[512,1024]{1,0:T(8,128)(2,1)}, bf16[512,1024]{1,0:T(8,128)(2,1)}, u32[]{:S(2)}, u32[]{:S(2)}) collective-permute-start(bf16[512,1024]{1,0:T(8,128)(2,1)} %get-tuple-element.749), channel_id=1, source_target_pairs={{0,1},{1,0},{2,3},{3,2},{4,5},{5,4},{6,7},{7,6},{8,9},{9,8},{10,11... | collective-permute-start | bytes 3145736 | tf_op jit(solution)/shard_map/ppermute | solution.py:510
  117.3 32.2 %collective-permute-start.27 = (bf16[512,1024]{1,0:T(8,128)(2,1)}, bf16[512,1024]{1,0:T(8,128)(2,1)}, u32[]{:S(2)}, u32[]{:S(2)}) collective-permute-start(bf16[512,1024]{1,0:T(8,128)(2,1)} %get-tuple-element.867), channel_id=1, source_target_pairs={{0,4},{5,1},{4,8},{9,5},{8,12},{13,9},{2,6},{7,3},{6,10},{11,7},{1... | collective-permute-start | bytes 3145736 | tf_op jit(solution)/shard_map/ppermute | solution.py:504
  122.3 10.0 %collective-permute-start.23 = (bf16[64,1024]{1,0:T(8,128)(2,1)}, bf16[64,1024]{1,0:T(8,128)(2,1)S(1)}, u32[]{:S(2)}, u32[]{:S(2)}) collective-permute-start(bf16[64,1024]{1,0:T(8,128)(2,1)} %get-tuple-element.809), channel_id=1, source_target_pairs={{0,2},{2,0},{1,3},{3,1},{4,6},{6,4},{5,7},{7,5},{8,10},{10,8},{9,1... | collective-permute-start | bytes 393224 | tf_op jit(solution)/shard_map/ppermute | solution.py:507
  132.3 29.0 %collective-permute-start.33 = (bf16[512,1024]{1,0:T(8,128)(2,1)}, bf16[512,1024]{1,0:T(8,128)(2,1)}, u32[]{:S(2)}, u32[]{:S(2)}) collective-permute-start(bf16[512,1024]{1,0:T(8,128)(2,1)} %shard_map.126.a), channel_id=1, source_target_pairs={{0,2},{2,0},{1,3},{3,1},{4,6},{6,4},{5,7},{7,5},{8,10},{10,8},{9,1... | collective-permute-start | bytes 3145736 | tf_op jit(solution)/shard_map/ppermute | solution.py:507
  149.6 3.2 %collective-permute-start.28 = (bf16[256,1024]{1,0:T(8,128)(2,1)S(1)}, bf16[256,1024]{1,0:T(8,128)(2,1)S(1)}, u32[]{:S(2)}, u32[]{:S(2)}) collective-permute-start(bf16[256,1024]{1,0:T(8,128)(2,1)S(1)} %get-tuple-element.878), channel_id=1, source_target_pairs={{0,1},{1,0},{2,3},{3,2},{4,5},{5,4},{6,7},{7,6},{8,9},{9,8},{10,11... | collective-permute-start | bytes 1572872 | tf_op jit(solution)/shard_map/ppermute | solution.py:510
  149.6 3.2 %collective-permute-start.29 = (bf16[256,1024]{1,0:T(8,128)(2,1)S(1)}, bf16[256,1024]{1,0:T(8,128)(2,1)S(1)}, u32[]{:S(2)}, u32[]{:S(2)}) collective-permute-start(bf16[256,1024]{1,0:T(8,128)(2,1)S(1)} %get-tuple-element.879), channel_id=1, source_target_pairs={{0,1},{1,0},{2,3},{3,2},{4,5},{5,4},{6,7},{7,6},{8,9},{9,8},{10,11... | collective-permute-start | bytes 1572872 | tf_op jit(solution)/shard_map/ppermute | solution.py:510
  150.1 2.5 %collective-permute-start.32 = (f32[64,1024]{1,0:T(8,128)S(1)}, f32[64,1024]{1,0:T(8,128)S(1)}, u32[]{:S(2)}, u32[]{:S(2)}) collective-permute-start(f32[64,1024]{1,0:T(8,128)S(1)} %convert_add_fusion.kept), channel_id=1, source_target_pairs={{0,1},{1,0},{2,3},{3,2},{4,5},{5,4},{6,7},{7,6},{8,9},{9,8},{10,11... | collective-permute-start | bytes 786440 | tf_op jit(solution)/shard_map/ppermute | solution.py:510
  161.4 3.3 %collective-permute-start.35 = (bf16[512,1024]{1,0:T(8,128)(2,1)}, bf16[512,1024]{1,0:T(8,128)(2,1)S(1)}, u32[]{:S(2)}, u32[]{:S(2)}) collective-permute-start(bf16[512,1024]{1,0:T(8,128)(2,1)} %get-tuple-element.897), channel_id=1, source_target_pairs={{0,1},{1,0},{2,3},{3,2},{4,5},{5,4},{6,7},{7,6},{8,9},{9,8},{10,11... | collective-permute-start | bytes 3145736 | tf_op jit(solution)/shard_map/ppermute | solution.py:510
  163.3 2.7 %collective-permute-start.34 = (bf16[512,1024]{1,0:T(8,128)(2,1)S(1)}, bf16[512,1024]{1,0:T(8,128)(2,1)S(1)}, u32[]{:S(2)}, u32[]{:S(2)}) collective-permute-start(bf16[512,1024]{1,0:T(8,128)(2,1)S(1)} %shard_map.131.value), channel_id=1, source_target_pairs={{0,1},{1,0},{2,3},{3,2},{4,5},{5,4},{6,7},{7,6},{8,9},{9,8},{10,11... | collective-permute-start | bytes 3145736 | tf_op jit(solution)/shard_map/ppermute | solution.py:510
  (47 other events, 284.6 us)

commit v4 on v3

--- a/solution.py
+++ b/solution.py
@@ -96,8 +96,10 @@
     return pl.BlockSpec(array.shape, lambda *_: (0,) * array.ndim)
 
 
-def call(body, table, grid, arrays, specs, outs, out_specs, scratch, flops, aliases=None, limit=48):
-    moved = sum(v.size * v.dtype.itemsize for v in arrays)
+def call(body, table, grid, arrays, specs, outs, out_specs, scratch, flops, aliases=None, pinned=(), limit=48):
+    arrays = list(arrays)
+    for at in pinned:
+        arrays[at] = pltpu.with_memory_space_constraint(arrays[at], pltpu.HBM)
     return pl.pallas_call(
         body,
         grid_spec=pltpu.PrefetchScalarGridSpec(
@@ -218,6 +220,7 @@
         [cols(v.shape[0]) for v in outs],
         [pltpu.VMEM((rows, half), B16)] * 2 + [pltpu.SemaphoreType.DMA((2,))],
         0,
+        pinned=range(2 * len(ours)),
     )
 
 
@@ -268,7 +271,7 @@
         [*flat] + [weight] * n,
         [pl.BlockSpec(memory_space=pltpu.HBM)] * len(flat) + [block(c) for c in range(n)],
         [
-            jax.ShapeDtypeStruct((rows, width), F32),
+            kept_in_hbm(jax.ShapeDtypeStruct((rows, width), F32)),
             jax.ShapeDtypeStruct((rows // 2, width), B16),
             jax.ShapeDtypeStruct((rows // 2, width), B16),
         ],
@@ -279,6 +282,7 @@
             pltpu.SemaphoreType.DMA((2 * n,)),
         ],
         0,
+        pinned=range(len(flat)),
         limit=28,
     )
 
@@ -296,7 +300,7 @@
         (2,),
         [grads, weight],
         [whole(grads), pl.BlockSpec((half, width), lambda j, t: (2 * t[0] + j, 0))],
-        jax.ShapeDtypeStruct((rows, width), B16),
+        kept_in_hbm(jax.ShapeDtypeStruct((rows, width), B16)),
         pl.BlockSpec((rows, half), lambda j, t: (0, j)),
         [],
         2 * rows * width * width,
@@ -379,7 +383,7 @@
     ]
     body = functools.partial(ranks_body, rank)
     specs = [whole(v) for v in arrays]
-    return call(body, table, (1,), arrays, specs, outs, [whole(v) for v in outs], [], 0)
+    return call(body, table, (1,), arrays, specs, [kept_in_hbm(v) for v in outs], [whole(v) for v in outs], [], 0)
 
 
 def maps_body(rank, count, table, *refs):
@@ -416,7 +420,7 @@
     ]
     body = functools.partial(maps_body, rank, len(parts))
     specs = [whole(v) for v in arrays]
-    return call(body, table, (1,), arrays, specs, outs, [whole(v) for v in outs], [], 0)
+    return call(body, table, (1,), arrays, specs, [kept_in_hbm(v) for v in outs], [whole(v) for v in outs], [], 0)
 
 
 def lora_body(table, low, up, back, down, out, into):
@@ -430,7 +434,7 @@
     out = jax.ShapeDtypeStruct((rows, width), B16)
     specs = [whole(v) for v in arrays]
     table = jnp.zeros((1,), jnp.int32)
-    return call(lora_body, table, (1,), arrays, specs, [out, out], [whole(out)] * 2, [], 0)
+    return call(lora_body, table, (1,), arrays, specs, [kept_in_hbm(out)] * 2, [whole(out)] * 2, [], 0)
 
 
 def finish_body(table, here, live, out_lora, term, in_lora, ends, there, there_end, theirs, theirs_end, kept, other, query, token_grad, down, up):
@@ -486,6 +490,45 @@
     return call(add_body, table, (2,), [a, b], [spec] * 2, out, spec, [], 0)
 
 
+def mask_body(tenants, slots, table, mine, theirs, grads, their_grads, slot_rows, live):
+    blocks = mine.shape[0] // BLOCK_ROWS
+    row = lax.broadcasted_iota(jnp.int32, (BLOCK_ROWS, 1), 0)
+    for side, (rows_in, rows_out) in enumerate(((mine, grads), (theirs, their_grads))):
+        for b in range(blocks):
+            block = table[2 * tenants + side] + b
+            start = jnp.int32(0)
+            left = slot = jnp.int32(0)
+            for t in range(tenants):
+                here = start <= block
+                left = jnp.where(here, table[t] - BLOCK_ROWS * (block - start), left)
+                slot = jnp.where(here, table[tenants + t], slot)
+                start = start + (table[t] + BLOCK_ROWS - 1) // BLOCK_ROWS
+            at = pl.ds(b * BLOCK_ROWS, BLOCK_ROWS)
+            alive = row < left
+            rows_out[at, :] = jnp.where(alive, rows_in[at, :].astype(F32), 0.0).astype(B16)
+            if side == 0:
+                live[at, :] = jnp.where(alive, 1.0, 0.0)
+                placed = lax.rem(slot + table[2 * tenants + 2], slots)
+                slot_rows[:, at] = jnp.full((1, BLOCK_ROWS), placed, jnp.int32)
+
+
+def masked(table, tenants, slots, mine, theirs):
+    rows, width = mine.shape
+    outs = [
+        jax.ShapeDtypeStruct((rows, width), B16),
+        jax.ShapeDtypeStruct((rows, width), B16),
+        jax.ShapeDtypeStruct((1, rows), jnp.int32),
+        jax.ShapeDtypeStruct((rows, 1), F32),
+    ]
+    body = functools.partial(mask_body, tenants, slots)
+    specs = [whole(mine), whole(theirs)]
+    return call(body, table, (1,), [mine, theirs], specs, outs, [whole(v) for v in outs], [], 0)
+
+
+def kept_in_hbm(shape):
+    return pltpu.HBM(shape.shape, shape.dtype)
+
+
 def shards_line(tokens, weight, down_maps, up_maps, counts, slot_of, cotangent):
     rows, width = tokens.shape
     held, _, rank = down_maps.shape
@@ -573,14 +616,14 @@
     mine = jnp.stack([jnp.swapaxes(down_maps, 1, 2), up_maps]).reshape(2, -1, width)
     st["fetched"] = other_tenant(lax.dynamic_index_in_dim(mine, core, 0, keepdims=False))
     st["mine"] = mine
-    row_ids = (owner * 2 + core) * rows + jnp.arange(rows, dtype=jnp.int32)
-    tenant, live = layout(counts, row_ids)
-    relative = lax.rem(lookup(slot_of, tenant) + (2 - owner) * held, slots)
-    st["relative"] = relative[None, :]
-    st["live"] = live.astype(F32)[:, None]
-    their_live = layout(counts, row_ids + (1 - 2 * core) * rows)[1]
-    st["grads"] = jnp.where(live[:, None], cotangent, jnp.zeros_like(cotangent))
-    st["their_grads"] = jnp.where(their_live[:, None], theirs, jnp.zeros_like(cotangent))
+    blocks = rows // BLOCK_ROWS
+    first = (owner * 2 + core) * blocks
+    their_first = (owner * 2 + 1 - core) * blocks
+    places = numbers(first, their_first, (2 - owner) * held)
+    table = jnp.concatenate([counts, slot_of, places])
+    st["grads"], st["their_grads"], st["relative"], st["live"] = masked(
+        table, counts.shape[0], slots, cotangent, theirs
+    )
     fence()
 
     coming = along(st["their_tokens"])
@@ -605,7 +648,13 @@
             for d in range(1, n):
                 pairs = [(i, (i + d) % n) for i in range(n)]
                 st["part", d] = lax.ppermute(st["part"], "tensor", pairs)
+        if k == 3:
+            st["x", 0] = swapped
+        if k == 6:
+            st["maps_x"] = other_tenant(st["kept"].pop())
         fence()
+        if k == 6:
+            swapped = other_tenant(st["mix", 2])
         if not last:
             coming = along(st.pop("sent"))
             st["shared", t - 1, side] = other_core(st.pop("share"))
@@ -618,10 +667,11 @@
             piece_of(step, extra)
             if step == n - 1:
                 st["kept"] = kept[:1]
-                st["maps_x"] = other_tenant(kept[1])
-            st["x", step - 1] = swapped
+            if step > 1:
+                st["x", step - 1] = swapped
             fence()
-            swapped = other_tenant(st["mix", step])
+            if step != 2:
+                swapped = other_tenant(st["mix", step])
             sum_of(step - 1)
         elif 4 <= k < 2 * n:
             wg_share = other_core(st["ours", step - 2])

time: 168 us -> 157 us (0.935)
  local copies, waits for them, and re-layouts: 22.5 us -> 13.1 us
  other arithmetic: 9.38 us -> 3.09 us
  starting transfers between devices: 39.1 us -> 41.9 us
  Pallas kernels: 79.5 us -> 81.8 us
    unnamed x86 -> x52, local copies, waits for them, and re-layouts: 20.8 us -> 11 us
    select_n x3 -> x0, other arithmetic: 3.12 us -> none  [the longest x1 1.74 us: shards_line(): jnp.where(their_live[:, None], theirs, jnp.zeros_like(cotangent))]
    pallas_call x25 -> x26, Pallas kernels: 79.5 us -> 81.8 us  [call(): pl.pallas_call(body, grid_spec=pltpu.PrefetchScalarGridSpec(num_scalar_pr...]
    ppermute x19, waiting for transfers between devices: 6.14 us -> 8.14 us  [other_core(): return lax.ppermute(value, 'dp', swap)]
    ppermute x6, waiting for transfers between devices: 9.11 us -> 7.11 us  [other_tenant(): return lax.ppermute(value, 'tenant', swap)]
  transfers between devices with their start and end apart: 36 -> 36, of which waited for: 9 -> 10; matrix products, arithmetic and copies ran while one was open for 7% -> 3% of each run, Pallas kernels for 47% -> 52%
where the time goes in v4:
time: 157 us; the launch traced here: 156 us
  Pallas kernels  81.8 us (52%)
  starting transfers between devices  41.9 us (27%)
  waiting for transfers between devices  15.3 us (10%)
  local copies, waits for them, and re-layouts  13.1 us (8%)
  other arithmetic  3.09 us (2%)
    pallas_call x26, Pallas kernels, call(): pl.pallas_call(body, grid_spec=pltpu.PrefetchScalarGridSpec(num_scalar_pr...  81.8 us
    ppermute x8, starting transfers between devices, along(): return lax.ppermute(value, ('tensor', 'dp'), line_pairs)  28.7 us
    unnamed x52, local copies, waits for them, and re-layouts  11 us
    ppermute x19, waiting for transfers between devices, other_core(): return lax.ppermute(value, 'dp', swap)  8.14 us
    ppermute x6, waiting for transfers between devices, other_tenant(): return lax.ppermute(value, 'tenant', swap)  7.11 us
    ppermute x6, starting transfers between devices, other_tenant(): return lax.ppermute(value, 'tenant', swap)  6.64 us
    ppermute x3, starting transfers between devices, shards_line(): st['part', d] = lax.ppermute(st['part'], 'tensor', pairs)  3.88 us
  transfers between devices with their start and end apart: 36, of which 10 were waited for; matrix products, arithmetic and copies ran while one was open for 3% of the time, Pallas kernels for 52%

profile of v4, /device:TPU:0, one launch (start us, length us, event | category | flops | bytes accessed | tf_op | source)
XLA Modules:
  0.0 156.2 jit_solution(11183629978055072028)
XLA Ops:
  1.2 5.0 %collective-permute-start.4 = (bf16[512,1024]{1,0:T(8,128)(2,1)}, bf16[512,1024]{1,0:T(8,128)(2,1)S(1)}, u32[]{:S(2)}, u32[]{:S(2)}) collective-permute-start(bf16[512,1024]{1,0:T(8,128)(2,1)} %refs_0_.1), channel_id=1, source_target_pairs={{0,4},{5,1},{4,8},{9,5},{8,12},{13,9},{2,6},{7,3},{6,10},{11,7},{1... | collective-permute-start | bytes 3145736 | tf_op jit(solution)/shard_map/ppermute | solution.py:547
  16.3 4.4 %collective-permute-start.10 = (bf16[512,1024]{1,0:T(8,128)(2,1)}, bf16[512,1024]{1,0:T(8,128)(2,1)}, u32[]{:S(2)}, u32[]{:S(2)}) collective-permute-start(bf16[512,1024]{1,0:T(8,128)(2,1)} %collective-permute-done.refs_1_), channel_id=1, source_target_pairs={{0,4},{5,1},{4,8},{9,5},{8,12},{13,9},{2,6},{7,3},{6,10},{11,7},{1... | collective-permute-start | bytes 3145736 | tf_op jit(solution)/shard_map/ppermute | solution.py:547
  20.8 4.2 %shard_map.111.a = bf16[512,1024]{1,0:T(8,128)(2,1)} custom-call(s32[2]{0:T(128)S(1)} %pad_add_fusion.table, bf16[512,1024]{1,0:T(8,128)(2,1)} %refs_0_.1, bf16[512,1024]{1,0:T(8,128)(2,1)} %collective-permute-done.refs_1_, bf16[512,1024]{1,0:T(8,128)(2,1)S(1)} %get-tuple-element.798.refs_2_.grads.refs_6_.refs_4_.refs_8_, ...), custom_call_target="tpu_custom_call" | custom-call | flops 1 | bytes 1 | tf_op jit(solution)/shard_map/pallas_call | solution.py:103
  28.3 2.4 %shard_map.112 = (bf16[128,1024]{1,0:T(8,128)(2,1)}, bf16[128,1024]{1,0:T(8,128)(2,1)}, bf16[32,512]{1,0:T(8,128)(2,1)}) custom-call(s32[1]{0:T(128)} %bitcast.7.table, bf16[2,64,1024]{2,1,0:T(8,128)(2,1)S(1)} %pad_maximum_fusion.mine, bf16[64,1024]{1,0:T(8,128)(2,1)S(1)} %collective-permute-done.1.fetched, bf16[64,1024]{1,0:T(8,128)(2,1)} %collective-permute-done.3.shared, ...), custom_call_target="tpu_custom_call" | custom-call | flops 1 | bytes 1 | tf_op jit(solution)/shard_map/pallas_call | solution.py:103
  31.3 3.2 %collective-permute-start.7 = (bf16[32,512]{1,0:T(8,128)(2,1)}, bf16[32,512]{1,0:T(8,128)(2,1)S(1)}, u32[]{:S(2)}, u32[]{:S(2)}) collective-permute-start(bf16[32,512]{1,0:T(8,128)(2,1)} %get-tuple-element.516.refs_0_), channel_id=1, source_target_pairs={{0,12},{4,0},{8,4},{12,8},{1,13},{5,1},{9,5},{13,9},{2,14},{6,2},{... | collective-permute-start | bytes 98312 | tf_op jit(solution)/shard_map/ppermute | solution.py:650
  34.6 4.2 %shard_map.113 = (bf16[512,1024]{1,0:T(8,128)(2,1)}, bf16[512,512]{1,0:T(8,128)(2,1)S(1)}) custom-call(s32[3]{0:T(128)S(1)} %get-tuple-element.913.table, bf16[512,1024]{1,0:T(8,128)(2,1)S(1)} %get-tuple-element.798.refs_2_.grads.refs_6_.refs_4_.refs_8_, bf16[4096,1024]{1,0:T(8,128)(2,1)} %refs_25_, ...), custom_call_target="tpu_custom_call" | custom-call | flops 1 | bytes 1 | tf_op jit(solution)/shard_map/pallas_call | solution.py:103
  38.9 3.2 %collective-permute-start.13 = (bf16[512,1024]{1,0:T(8,128)(2,1)}, bf16[512,1024]{1,0:T(8,128)(2,1)}, u32[]{:S(2)}, u32[]{:S(2)}) collective-permute-start(bf16[512,1024]{1,0:T(8,128)(2,1)} %get-tuple-element.586), channel_id=1, source_target_pairs={{0,4},{5,1},{4,8},{9,5},{8,12},{13,9},{2,6},{7,3},{6,10},{11,7},{1... | collective-permute-start | bytes 3145736 | tf_op jit(solution)/shard_map/ppermute | solution.py:547
  46.4 4.4 %shard_map.115 = (bf16[512,1024]{1,0:T(8,128)(2,1)}, bf16[512,512]{1,0:T(8,128)(2,1)}) custom-call(s32[3]{0:T(128)S(1)} %get-tuple-element.913.table, bf16[512,1024]{1,0:T(8,128)(2,1)S(1)} %get-tuple-element.799.refs_3_.grads.refs_5_.refs_9_, bf16[4096,1024]{1,0:T(8,128)(2,1)} %refs_25_, bf16[512,1024]{1,0:T(8,128)(2,1)} %collective-permute-done.10.came.refs_3_.refs_5_.refs_11_), custom_call_target="tpu_custom_call" | custom-call | flops 1 | bytes 1 | tf_op jit(solution)/shard_map/pallas_call | solution.py:103
  51.0 1.8 %collective-permute-start.15 = (bf16[512,1024]{1,0:T(8,128)(2,1)}, bf16[512,1024]{1,0:T(8,128)(2,1)S(1)}, u32[]{:S(2)}, u32[]{:S(2)}) collective-permute-start(bf16[512,1024]{1,0:T(8,128)(2,1)} %get-tuple-element.632), channel_id=1, source_target_pairs={{0,4},{5,1},{4,8},{9,5},{8,12},{13,9},{2,6},{7,3},{6,10},{11,7},{1... | collective-permute-start | bytes 3145736 | tf_op jit(solution)/shard_map/ppermute | solution.py:547
  53.2 4.3 %shard_map.116.a = bf16[512,1024]{1,0:T(8,128)(2,1)} custom-call(s32[2]{0:T(128)S(1)} %pad_add_fusion.1.table, bf16[512,512]{1,0:T(8,128)(2,1)} %collective-permute-done.12.refs_0_.refs_2_.refs_6_, bf16[512,1024]{1,0:T(8,128)(2,1)} %copy-done, bf16[512,512]{1,0:T(8,128)(2,1)} %copy-done.21, ...), custom_call_target="tpu_custom_call" | custom-call | flops 1 | bytes 1 | tf_op jit(solution)/shard_map/pallas_call | solution.py:103
  57.5 2.7 %shard_map.117 = (bf16[4096,1024]{1,0:T(8,128)(2,1)}, bf16[512,1024]{1,0:T(8,128)(2,1)}) custom-call(s32[1]{0:T(128)} %bitcast.12.table, bf16[512,1024]{1,0:T(8,128)(2,1)} %shard_map.111.a, bf16[512,1024]{1,0:T(8,128)(2,1)} %collective-permute-done.11.b), custom_call_target="tpu_custom_call" | custom-call | flops 1 | bytes 1 | tf_op jit(solution)/shard_map/pallas_call | solution.py:103
  60.1 4.3 %shard_map.118 = (bf16[512,1024]{1,0:T(8,128)(2,1)}, bf16[512,512]{1,0:T(8,128)(2,1)S(1)}) custom-call(s32[3]{0:T(128)S(1)} %get-tuple-element.914.table, bf16[512,1024]{1,0:T(8,128)(2,1)S(1)} %get-tuple-element.798.refs_2_.grads.refs_6_.refs_4_.refs_8_, bf16[4096,1024]{1,0:T(8,128)(2,1)} %refs_25_, ...), custom_call_target="tpu_custom_call" | custom-call | flops 1 | bytes 1 | tf_op jit(solution)/shard_map/pallas_call | solution.py:103
  65.9 3.9 %collective-permute-start.18 = (bf16[512,1024]{1,0:T(8,128)(2,1)}, bf16[512,1024]{1,0:T(8,128)(2,1)}, u32[]{:S(2)}, u32[]{:S(2)}) collective-permute-start(bf16[512,1024]{1,0:T(8,128)(2,1)} %get-tuple-element.710), channel_id=1, source_target_pairs={{0,4},{5,1},{4,8},{9,5},{8,12},{13,9},{2,6},{7,3},{6,10},{11,7},{1... | collective-permute-start | bytes 3145736 | tf_op jit(solution)/shard_map/ppermute | solution.py:547
  69.9 3.6 %shard_map.119.term = bf16[512,1024]{1,0:T(8,128)(2,1)} custom-call(s32[1]{0:T(128)} %bitcast.15.table, bf16[512,1024]{1,0:T(8,128)(2,1)S(1)} %get-tuple-element.798.refs_2_.grads.refs_6_.refs_4_.refs_8_, bf16[4096,1024]{1,0:T(8,128)(2,1)} %refs_25_), custom_call_target="tpu_custom_call" | custom-call | flops 1 | bytes 1 | tf_op jit(solution)/shard_map/pallas_call | solution.py:103
  73.5 4.3 %shard_map.120 = (bf16[512,1024]{1,0:T(8,128)(2,1)}, bf16[512,512]{1,0:T(8,128)(2,1)}) custom-call(s32[3]{0:T(128)S(1)} %get-tuple-element.914.table, bf16[512,1024]{1,0:T(8,128)(2,1)S(1)} %get-tuple-element.799.refs_3_.grads.refs_5_.refs_9_, bf16[4096,1024]{1,0:T(8,128)(2,1)} %refs_25_, ...), custom_call_target="tpu_custom_call" | custom-call | flops 1 | bytes 1 | tf_op jit(solution)/shard_map/pallas_call | solution.py:103
  77.8 3.1 %collective-permute-start.22 = (bf16[512,1024]{1,0:T(8,128)(2,1)}, bf16[512,1024]{1,0:T(8,128)(2,1)}, u32[]{:S(2)}, u32[]{:S(2)}) collective-permute-start(bf16[512,1024]{1,0:T(8,128)(2,1)} %get-tuple-element.768), channel_id=1, source_target_pairs={{0,4},{5,1},{4,8},{9,5},{8,12},{13,9},{2,6},{7,3},{6,10},{11,7},{1... | collective-permute-start | bytes 3145736 | tf_op jit(solution)/shard_map/ppermute | solution.py:547
  82.1 4.4 %shard_map.121 = (bf16[512,1024]{1,0:T(8,128)(2,1)}, f32[64,1024]{1,0:T(8,128)S(1)}, bf16[64,1024]{1,0:T(8,128)(2,1)S(1)}) custom-call(s32[2]{0:T(128)S(1)} %pad_add_fusion.2.table, bf16[512,512]{1,0:T(8,128)(2,1)} %collective-permute-done.12.refs_0_.refs_2_.refs_6_, bf16[512,1024]{1,0:T(8,128)(2,1)} %copy-done, ...), custom_call_target="tpu_custom_call" | custom-call | flops 1 | bytes 1 | tf_op jit(solution)/shard_map/pallas_call | solution.py:103
  87.2 3.1 %collective-permute-done.17.b = bf16[512,1024]{1,0:T(8,128)(2,1)} collective-permute-done((bf16[512,1024]{1,0:T(8,128)(2,1)}, bf16[512,1024]{1,0:T(8,128)(2,1)}, u32[]{:S(2)}, u32[]{:S(2)}) %collective-permute-start.17) | collective-permute-done | bytes 1048608 | tf_op jit(solution)/shard_map/ppermute | solution.py:550
  90.3 2.7 %shard_map.122 = (bf16[4096,1024]{1,0:T(8,128)(2,1)}, bf16[512,1024]{1,0:T(8,128)(2,1)}) custom-call(s32[1]{0:T(128)} %bitcast.17.table, bf16[512,1024]{1,0:T(8,128)(2,1)} %shard_map.116.a, bf16[512,1024]{1,0:T(8,128)(2,1)} %collective-permute-done.17.b, bf16[4096,1024]{1,0:T(8,128)(2,1)} %get-tuple-element.701.refs_0_), custom_call_target="tpu_custom_call", output_to_operand_aliasing={{0}: (3, {})} | custom-call | flops 1 | bytes 1 | tf_op jit(solution)/shard_map/pallas_call | solution.py:103
  94.6 4.3 %shard_map.123 = (bf16[512,1024]{1,0:T(8,128)(2,1)}, bf16[512,512]{1,0:T(8,128)(2,1)S(1)}) custom-call(s32[3]{0:T(128)S(1)} %add_add_fusion.2.table, bf16[512,1024]{1,0:T(8,128)(2,1)S(1)} %get-tuple-element.798.refs_2_.grads.refs_6_.refs_4_.refs_8_, bf16[4096,1024]{1,0:T(8,128)(2,1)} %refs_25_, bf16[512,1024]{1,0:T(8,128)(2,1)} %collective-permute-done.18.came.refs_3_.refs_17_), custom_call_target="tpu_custom_call" | custom-call | flops 1 | bytes 1 | tf_op jit(solution)/shard_map/pallas_call | solution.py:103
  99.7 3.2 %collective-permute-start.25 = (bf16[512,1024]{1,0:T(8,128)(2,1)}, bf16[512,1024]{1,0:T(8,128)(2,1)}, u32[]{:S(2)}, u32[]{:S(2)}) collective-permute-start(bf16[512,1024]{1,0:T(8,128)(2,1)} %get-tuple-element.847), channel_id=1, source_target_pairs={{0,4},{5,1},{4,8},{9,5},{8,12},{13,9},{2,6},{7,3},{6,10},{11,7},{1... | collective-permute-start | bytes 3145736 | tf_op jit(solution)/shard_map/ppermute | solution.py:547
  102.9 2.1 %shard_map.124.refs_0_ = bf16[4096,1024]{1,0:T(8,128)(2,1)} custom-call(s32[1]{0:T(128)} %bitcast.20.table, bf16[512,1024]{1,0:T(8,128)(2,1)} %collective-permute-done.19.value, bf16[4096,1024]{1,0:T(8,128)(2,1)} %get-tuple-element.751.refs_0_), custom_call_target="tpu_custom_call", output_to_operand_aliasing={{}: (2, {})} | custom-call | flops 1 | bytes 1 | tf_op jit(solution)/shard_map/pallas_call | solution.py:103
  105.1 1.9 %shard_map.125 = (bf16[512,1024]{1,0:T(8,128)(2,1)}, bf16[512,1024]{1,0:T(8,128)(2,1)}) custom-call(s32[1]{0:T(128)} %constant.35.clone.1.table, bf16[128,512]{1,0:T(8,128)(2,1)S(1)} %copy-done.18, bf16[128,1024]{1,0:T(8,128)(2,1)S(1)} %copy-done.17, bf16[128,512]{1,0:T(8,128)(2,1)S(1)} %copy-done.19, bf16[128,1024]{1,0:T(8,128)(2,1)S(1)} %copy-done.16), custom_call_target="tpu_custom_call" | custom-call | flops 1 | bytes 1 | tf_op jit(solution)/shard_map/pallas_call | solution.py:103
  107.0 4.3 %shard_map.126 = (bf16[512,1024]{1,0:T(8,128)(2,1)}, bf16[512,512]{1,0:T(8,128)(2,1)S(1)}) custom-call(s32[3]{0:T(128)S(1)} %add_add_fusion.2.table, bf16[512,1024]{1,0:T(8,128)(2,1)S(1)} %get-tuple-element.799.refs_3_.grads.refs_5_.refs_9_, bf16[4096,1024]{1,0:T(8,128)(2,1)} %refs_25_, bf16[512,1024]{1,0:T(8,128)(2,1)} %collective-permute-done.22.came.refs_7_.refs_21_), custom_call_target="tpu_custom_call" | custom-call | flops 1 | bytes 1 | tf_op jit(solution)/shard_map/pallas_call | solution.py:103
  111.3 4.0 %collective-permute-start.27 = (bf16[512,1024]{1,0:T(8,128)(2,1)}, bf16[512,1024]{1,0:T(8,128)(2,1)}, u32[]{:S(2)}, u32[]{:S(2)}) collective-permute-start(bf16[512,1024]{1,0:T(8,128)(2,1)} %get-tuple-element.877), channel_id=1, source_target_pairs={{0,4},{5,1},{4,8},{9,5},{8,12},{13,9},{2,6},{7,3},{6,10},{11,7},{1... | collective-permute-start | bytes 3145736 | tf_op jit(solution)/shard_map/ppermute | solution.py:547
  115.4 2.0 %collective-permute-done.23.refs_2_.refs_16_ = bf16[512,512]{1,0:T(8,128)(2,1)} collective-permute-done((bf16[512,512]{1,0:T(8,128)(2,1)S(1)}, bf16[512,512]{1,0:T(8,128)(2,1)}, u32[]{:S(2)}, u32[]{:S(2)}) %collective-permute-start.23) | collective-permute-done | bytes 524320 | tf_op jit(solution)/shard_map/ppermute | solution.py:553
  117.3 3.5 %shard_map.127.a = bf16[512,1024]{1,0:T(8,128)(2,1)S(1)} custom-call(s32[2]{0:T(128)S(1)} %pad_add_fusion.3.table, bf16[512,512]{1,0:T(8,128)(2,1)} %collective-permute-done.16.refs_2_.refs_0_.refs_8_.refs_14_, bf16[512,1024]{1,0:T(8,128)(2,1)} %collective-permute-done.13.came.refs_3_.refs_1_.refs_9_.refs_15_, ...), custom_call_target="tpu_custom_call" | custom-call | flops 1 | bytes 1 | tf_op jit(solution)/shard_map/pallas_call | solution.py:103
  120.8 4.0 %collective-permute-done.24.b = bf16[512,1024]{1,0:T(8,128)(2,1)} collective-permute-done((bf16[512,1024]{1,0:T(8,128)(2,1)}, bf16[512,1024]{1,0:T(8,128)(2,1)}, u32[]{:S(2)}, u32[]{:S(2)}) %collective-permute-start.24) | collective-permute-done | bytes 1048608 | tf_op jit(solution)/shard_map/ppermute | solution.py:550
  125.7 2.8 %shard_map.128 = (bf16[4096,1024]{1,0:T(8,128)(2,1)}, bf16[512,1024]{1,0:T(8,128)(2,1)}) custom-call(s32[1]{0:T(128)} %bitcast.22.table, bf16[512,1024]{1,0:T(8,128)(2,1)} %get-tuple-element.828.a, bf16[512,1024]{1,0:T(8,128)(2,1)} %collective-permute-done.24.b, bf16[4096,1024]{1,0:T(8,128)(2,1)} %shard_map.124.refs_0_), custom_call_target="tpu_custom_call", output_to_operand_aliasing={{0}: (3, {})} | custom-call | flops 1 | bytes 1 | tf_op jit(solution)/shard_map/pallas_call | solution.py:103
  128.5 2.2 %shard_map.129.refs_0_ = bf16[4096,1024]{1,0:T(8,128)(2,1)} custom-call(s32[1]{0:T(128)} %bitcast.23.table, bf16[512,1024]{1,0:T(8,128)(2,1)} %collective-permute-done.26.value, bf16[4096,1024]{1,0:T(8,128)(2,1)} %get-tuple-element.857.refs_0_), custom_call_target="tpu_custom_call", output_to_operand_aliasing={{}: (2, {})} | custom-call | flops 1 | bytes 1 | tf_op jit(solution)/shard_map/pallas_call | solution.py:103
  131.6 8.7 %shard_map.130 = (f32[512,1024]{1,0:T(8,128)}, bf16[256,1024]{1,0:T(8,128)(2,1)S(1)}, bf16[256,1024]{1,0:T(8,128)(2,1)S(1)}) custom-call(s32[9]{0:T(128)S(1)} %stack.148.table, bf16[512,1024]{1,0:T(8,128)(2,1)} %refs_0_.1, bf16[512,1024]{1,0:T(8,128)(2,1)} %collective-permute-done.refs_1_, bf16[512,512]{1,0:T(8,128)(2,1)} %collective-permute-done.12.refs_0_.refs_2_.refs_6_, ...), custom_call_target="tpu_custom_call" | custom-call | flops 1 | bytes 1 | tf_op jit(solution)/shard_map/pallas_call | solution.py:103
  145.3 4.4 %shard_map.131 = (bf16[512,1024]{1,0:T(8,128)(2,1)}, bf16[512,1024]{1,0:T(8,128)(2,1)}, f32[64,1024]{1,0:T(8,128)}, f32[64,1024]{1,0:T(8,128)}) custom-call(s32[1]{0:T(128)} %bitcast.7.table, f32[512,1024]{1,0:T(8,128)} %get-tuple-element.883.here, f32[512,1]{1,0:T(8,128)S(1)} %copy-done.13, bf16[512,1024]{1,0:T(8,128)(2,1)S(1)} %copy-done.4, ...), custom_call_target="tpu_custom_call" | custom-call | flops 1 | bytes 1 | tf_op jit(solution)/shard_map/pallas_call | solution.py:103
  (131 shorter events, 38.5 us)
Async XLA Ops:
  0.6 10.4 %collective-permute-start.2 = (bf16[512,1024]{1,0:T(8,128)(2,1)}, bf16[512,1024]{1,0:T(8,128)(2,1)S(1)}, u32[]{:S(2)}, u32[]{:S(2)}) collective-permute-start(bf16[512,1024]{1,0:T(8,128)(2,1)} %mine.1), channel_id=1, source_target_pairs={{0,1},{1,0},{2,3},{3,2},{4,5},{5,4},{6,7},{7,6},{8,9},{9,8},{10,11... | collective-permute-start | bytes 3145736 | tf_op jit(solution)/shard_map/ppermute | solution.py:553
  1.1 15.1 %collective-permute-start = (bf16[512,1024]{1,0:T(8,128)(2,1)}, bf16[512,1024]{1,0:T(8,128)(2,1)}, u32[]{:S(2)}, u32[]{:S(2)}) collective-permute-start(bf16[512,1024]{1,0:T(8,128)(2,1)} %refs_0_.1), channel_id=1, source_target_pairs={{0,1},{1,0},{2,3},{3,2},{4,5},{5,4},{6,7},{7,6},{8,9},{9,8},{10,11... | collective-permute-start | bytes 3145736 | tf_op jit(solution)/shard_map/ppermute | solution.py:553
  1.2 29.5 %collective-permute-start.4 = (bf16[512,1024]{1,0:T(8,128)(2,1)}, bf16[512,1024]{1,0:T(8,128)(2,1)S(1)}, u32[]{:S(2)}, u32[]{:S(2)}) collective-permute-start(bf16[512,1024]{1,0:T(8,128)(2,1)} %refs_0_.1), channel_id=1, source_target_pairs={{0,4},{5,1},{4,8},{9,5},{8,12},{13,9},{2,6},{7,3},{6,10},{11,7},{1... | collective-permute-start | bytes 3145736 | tf_op jit(solution)/shard_map/ppermute | solution.py:547
  7.8 8.5 %collective-permute-start.1 = (bf16[64,1024]{1,0:T(8,128)(2,1)}, bf16[64,1024]{1,0:T(8,128)(2,1)S(1)}, u32[]{:S(2)}, u32[]{:S(2)}) collective-permute-start(bf16[64,1024]{1,0:T(8,128)(2,1)} %fusion.1), channel_id=1, source_target_pairs={{0,2},{2,0},{1,3},{3,1},{4,6},{6,4},{5,7},{7,5},{8,10},{10,8},{9,1... | collective-permute-start | bytes 393224 | tf_op jit(solution)/shard_map/ppermute | solution.py:550
  16.3 30.1 %collective-permute-start.10 = (bf16[512,1024]{1,0:T(8,128)(2,1)}, bf16[512,1024]{1,0:T(8,128)(2,1)}, u32[]{:S(2)}, u32[]{:S(2)}) collective-permute-start(bf16[512,1024]{1,0:T(8,128)(2,1)} %collective-permute-done.refs_1_), channel_id=1, source_target_pairs={{0,4},{5,1},{4,8},{9,5},{8,12},{13,9},{2,6},{7,3},{6,10},{11,7},{1... | collective-permute-start | bytes 3145736 | tf_op jit(solution)/shard_map/ppermute | solution.py:547
  25.0 25.9 %collective-permute-start.11 = (bf16[512,1024]{1,0:T(8,128)(2,1)}, bf16[512,1024]{1,0:T(8,128)(2,1)}, u32[]{:S(2)}, u32[]{:S(2)}) collective-permute-start(bf16[512,1024]{1,0:T(8,128)(2,1)} %shard_map.111.a), channel_id=1, source_target_pairs={{0,2},{2,0},{1,3},{3,1},{4,6},{6,4},{5,7},{7,5},{8,10},{10,8},{9,1... | collective-permute-start | bytes 3145736 | tf_op jit(solution)/shard_map/ppermute | solution.py:550
  30.7 8.2 %collective-permute-start.5 = (bf16[32,512]{1,0:T(8,128)(2,1)}, bf16[32,512]{1,0:T(8,128)(2,1)S(1)}, u32[]{:S(2)}, u32[]{:S(2)}) collective-permute-start(bf16[32,512]{1,0:T(8,128)(2,1)} %get-tuple-element.516.refs_0_), channel_id=1, source_target_pairs={{0,4},{4,8},{8,12},{12,0},{1,5},{5,9},{9,13},{13,1},{2,6},{6,10},{... | collective-permute-start | bytes 98312 | tf_op jit(solution)/shard_map/ppermute | solution.py:650
  31.3 7.5 %collective-permute-start.6 = (bf16[32,512]{1,0:T(8,128)(2,1)}, bf16[32,512]{1,0:T(8,128)(2,1)S(1)}, u32[]{:S(2)}, u32[]{:S(2)}) collective-permute-start(bf16[32,512]{1,0:T(8,128)(2,1)} %get-tuple-element.516.refs_0_), channel_id=1, source_target_pairs={{0,8},{4,12},{8,0},{12,4},{1,9},{5,13},{9,1},{13,5},{2,10},{6,14},... | collective-permute-start | bytes 98312 | tf_op jit(solution)/shard_map/ppermute | solution.py:650
  31.3 7.5 %collective-permute-start.7 = (bf16[32,512]{1,0:T(8,128)(2,1)}, bf16[32,512]{1,0:T(8,128)(2,1)S(1)}, u32[]{:S(2)}, u32[]{:S(2)}) collective-permute-start(bf16[32,512]{1,0:T(8,128)(2,1)} %get-tuple-element.516.refs_0_), channel_id=1, source_target_pairs={{0,12},{4,0},{8,4},{12,8},{1,13},{5,1},{9,5},{13,9},{2,14},{6,2},{... | collective-permute-start | bytes 98312 | tf_op jit(solution)/shard_map/ppermute | solution.py:650
  38.9 6.7 %collective-permute-start.8 = (bf16[512,512]{1,0:T(8,128)(2,1)S(1)}, bf16[512,512]{1,0:T(8,128)(2,1)S(1)}, u32[]{:S(2)}, u32[]{:S(2)}) collective-permute-start(bf16[512,512]{1,0:T(8,128)(2,1)S(1)} %get-tuple-element.515), channel_id=1, source_target_pairs={{0,1},{1,0},{2,3},{3,2},{4,5},{5,4},{6,7},{7,6},{8,9},{9,8},{10,11... | collective-permute-start | bytes 1572872 | tf_op jit(solution)/shard_map/ppermute | solution.py:553
  38.9 21.2 %collective-permute-start.13 = (bf16[512,1024]{1,0:T(8,128)(2,1)}, bf16[512,1024]{1,0:T(8,128)(2,1)}, u32[]{:S(2)}, u32[]{:S(2)}) collective-permute-start(bf16[512,1024]{1,0:T(8,128)(2,1)} %get-tuple-element.586), channel_id=1, source_target_pairs={{0,4},{5,1},{4,8},{9,5},{8,12},{13,9},{2,6},{7,3},{6,10},{11,7},{1... | collective-permute-start | bytes 3145736 | tf_op jit(solution)/shard_map/ppermute | solution.py:547
  50.9 2.3 %collective-permute-start.12 = (bf16[512,512]{1,0:T(8,128)(2,1)}, bf16[512,512]{1,0:T(8,128)(2,1)}, u32[]{:S(2)}, u32[]{:S(2)}) collective-permute-start(bf16[512,512]{1,0:T(8,128)(2,1)} %get-tuple-element.563), channel_id=1, source_target_pairs={{0,1},{1,0},{2,3},{3,2},{4,5},{5,4},{6,7},{7,6},{8,9},{9,8},{10,11... | collective-permute-start | bytes 1572872 | tf_op jit(solution)/shard_map/ppermute | solution.py:553
  51.0 22.5 %collective-permute-start.15 = (bf16[512,1024]{1,0:T(8,128)(2,1)}, bf16[512,1024]{1,0:T(8,128)(2,1)S(1)}, u32[]{:S(2)}, u32[]{:S(2)}) collective-permute-start(bf16[512,1024]{1,0:T(8,128)(2,1)} %get-tuple-element.632), channel_id=1, source_target_pairs={{0,4},{5,1},{4,8},{9,5},{8,12},{13,9},{2,6},{7,3},{6,10},{11,7},{1... | collective-permute-start | bytes 3145736 | tf_op jit(solution)/shard_map/ppermute | solution.py:547
  64.4 9.0 %collective-permute-start.14 = (bf16[512,512]{1,0:T(8,128)(2,1)S(1)}, bf16[512,512]{1,0:T(8,128)(2,1)S(1)}, u32[]{:S(2)}, u32[]{:S(2)}) collective-permute-start(bf16[512,512]{1,0:T(8,128)(2,1)S(1)} %get-tuple-element.631), channel_id=1, source_target_pairs={{0,1},{1,0},{2,3},{3,2},{4,5},{5,4},{6,7},{7,6},{8,9},{9,8},{10,11... | collective-permute-start | bytes 1572872 | tf_op jit(solution)/shard_map/ppermute | solution.py:553
  64.4 25.9 %collective-permute-start.17 = (bf16[512,1024]{1,0:T(8,128)(2,1)}, bf16[512,1024]{1,0:T(8,128)(2,1)}, u32[]{:S(2)}, u32[]{:S(2)}) collective-permute-start(bf16[512,1024]{1,0:T(8,128)(2,1)} %shard_map.116.a), channel_id=1, source_target_pairs={{0,2},{2,0},{1,3},{3,1},{4,6},{6,4},{5,7},{7,5},{8,10},{10,8},{9,1... | collective-permute-start | bytes 3145736 | tf_op jit(solution)/shard_map/ppermute | solution.py:550
  65.9 27.1 %collective-permute-start.18 = (bf16[512,1024]{1,0:T(8,128)(2,1)}, bf16[512,1024]{1,0:T(8,128)(2,1)}, u32[]{:S(2)}, u32[]{:S(2)}) collective-permute-start(bf16[512,1024]{1,0:T(8,128)(2,1)} %get-tuple-element.710), channel_id=1, source_target_pairs={{0,4},{5,1},{4,8},{9,5},{8,12},{13,9},{2,6},{7,3},{6,10},{11,7},{1... | collective-permute-start | bytes 3145736 | tf_op jit(solution)/shard_map/ppermute | solution.py:547
  69.9 23.1 %collective-permute-start.19 = (bf16[512,1024]{1,0:T(8,128)(2,1)}, bf16[512,1024]{1,0:T(8,128)(2,1)}, u32[]{:S(2)}, u32[]{:S(2)}) collective-permute-start(bf16[512,1024]{1,0:T(8,128)(2,1)} %get-tuple-element.629), channel_id=1, source_target_pairs={{0,1},{1,0},{2,3},{3,2},{4,5},{5,4},{6,7},{7,6},{8,9},{9,8},{10,11... | collective-permute-start | bytes 3145736 | tf_op jit(solution)/shard_map/ppermute | solution.py:553
  77.8 3.2 %collective-permute-start.16 = (bf16[512,512]{1,0:T(8,128)(2,1)}, bf16[512,512]{1,0:T(8,128)(2,1)}, u32[]{:S(2)}, u32[]{:S(2)}) collective-permute-start(bf16[512,512]{1,0:T(8,128)(2,1)} %get-tuple-element.665), channel_id=1, source_target_pairs={{0,1},{1,0},{2,3},{3,2},{4,5},{5,4},{6,7},{7,6},{8,9},{9,8},{10,11... | collective-permute-start | bytes 1572872 | tf_op jit(solution)/shard_map/ppermute | solution.py:553
  77.8 29.2 %collective-permute-start.22 = (bf16[512,1024]{1,0:T(8,128)(2,1)}, bf16[512,1024]{1,0:T(8,128)(2,1)}, u32[]{:S(2)}, u32[]{:S(2)}) collective-permute-start(bf16[512,1024]{1,0:T(8,128)(2,1)} %get-tuple-element.768), channel_id=1, source_target_pairs={{0,4},{5,1},{4,8},{9,5},{8,12},{13,9},{2,6},{7,3},{6,10},{11,7},{1... | collective-permute-start | bytes 3145736 | tf_op jit(solution)/shard_map/ppermute | solution.py:547
  93.0 5.9 %collective-permute-start.20 = (bf16[64,1024]{1,0:T(8,128)(2,1)S(1)}, bf16[64,1024]{1,0:T(8,128)(2,1)S(1)}, u32[]{:S(2)}, u32[]{:S(2)}) collective-permute-start(bf16[64,1024]{1,0:T(8,128)(2,1)S(1)} %get-tuple-element.738), channel_id=1, source_target_pairs={{0,2},{2,0},{1,3},{3,1},{4,6},{6,4},{5,7},{7,5},{8,10},{10,8},{9,1... | collective-permute-start | bytes 393224 | tf_op jit(solution)/shard_map/ppermute | solution.py:550
  98.9 8.1 %collective-permute-start.21 = (bf16[512,512]{1,0:T(8,128)(2,1)S(1)}, bf16[512,512]{1,0:T(8,128)(2,1)S(1)}, u32[]{:S(2)}, u32[]{:S(2)}) collective-permute-start(bf16[512,512]{1,0:T(8,128)(2,1)S(1)} %get-tuple-element.761), channel_id=1, source_target_pairs={{0,1},{1,0},{2,3},{3,2},{4,5},{5,4},{6,7},{7,6},{8,9},{9,8},{10,11... | collective-permute-start | bytes 1572872 | tf_op jit(solution)/shard_map/ppermute | solution.py:553
  98.9 25.9 %collective-permute-start.24 = (bf16[512,1024]{1,0:T(8,128)(2,1)}, bf16[512,1024]{1,0:T(8,128)(2,1)}, u32[]{:S(2)}, u32[]{:S(2)}) collective-permute-start(bf16[512,1024]{1,0:T(8,128)(2,1)} %get-tuple-element.828.a), channel_id=1, source_target_pairs={{0,2},{2,0},{1,3},{3,1},{4,6},{6,4},{5,7},{7,5},{8,10},{10,8},{9,1... | collective-permute-start | bytes 3145736 | tf_op jit(solution)/shard_map/ppermute | solution.py:550
  99.7 28.8 %collective-permute-start.25 = (bf16[512,1024]{1,0:T(8,128)(2,1)}, bf16[512,1024]{1,0:T(8,128)(2,1)}, u32[]{:S(2)}, u32[]{:S(2)}) collective-permute-start(bf16[512,1024]{1,0:T(8,128)(2,1)} %get-tuple-element.847), channel_id=1, source_target_pairs={{0,4},{5,1},{4,8},{9,5},{8,12},{13,9},{2,6},{7,3},{6,10},{11,7},{1... | collective-permute-start | bytes 3145736 | tf_op jit(solution)/shard_map/ppermute | solution.py:547
  102.9 25.6 %collective-permute-start.26 = (bf16[512,1024]{1,0:T(8,128)(2,1)}, bf16[512,1024]{1,0:T(8,128)(2,1)}, u32[]{:S(2)}, u32[]{:S(2)}) collective-permute-start(bf16[512,1024]{1,0:T(8,128)(2,1)} %get-tuple-element.758), channel_id=1, source_target_pairs={{0,1},{1,0},{2,3},{3,2},{4,5},{5,4},{6,7},{7,6},{8,9},{9,8},{10,11... | collective-permute-start | bytes 3145736 | tf_op jit(solution)/shard_map/ppermute | solution.py:553
  111.3 29.0 %collective-permute-start.27 = (bf16[512,1024]{1,0:T(8,128)(2,1)}, bf16[512,1024]{1,0:T(8,128)(2,1)}, u32[]{:S(2)}, u32[]{:S(2)}) collective-permute-start(bf16[512,1024]{1,0:T(8,128)(2,1)} %get-tuple-element.877), channel_id=1, source_target_pairs={{0,4},{5,1},{4,8},{9,5},{8,12},{13,9},{2,6},{7,3},{6,10},{11,7},{1... | collective-permute-start | bytes 3145736 | tf_op jit(solution)/shard_map/ppermute | solution.py:547
  115.3 2.0 %collective-permute-start.23 = (bf16[512,512]{1,0:T(8,128)(2,1)S(1)}, bf16[512,512]{1,0:T(8,128)(2,1)}, u32[]{:S(2)}, u32[]{:S(2)}) collective-permute-start(bf16[512,512]{1,0:T(8,128)(2,1)S(1)} %get-tuple-element.818), channel_id=1, source_target_pairs={{0,1},{1,0},{2,3},{3,2},{4,5},{5,4},{6,7},{7,6},{8,9},{9,8},{10,11... | collective-permute-start | bytes 1572872 | tf_op jit(solution)/shard_map/ppermute | solution.py:553
  124.8 24.9 %collective-permute-start.33 = (bf16[512,1024]{1,0:T(8,128)(2,1)S(1)}, bf16[512,1024]{1,0:T(8,128)(2,1)S(1)}, u32[]{:S(2)}, u32[]{:S(2)}) collective-permute-start(bf16[512,1024]{1,0:T(8,128)(2,1)S(1)} %shard_map.127.a), channel_id=1, source_target_pairs={{0,2},{2,0},{1,3},{3,1},{4,6},{6,4},{5,7},{7,5},{8,10},{10,8},{9,1... | collective-permute-start | bytes 3145736 | tf_op jit(solution)/shard_map/ppermute | solution.py:550
  140.3 3.2 %collective-permute-start.28 = (bf16[256,1024]{1,0:T(8,128)(2,1)S(1)}, bf16[256,1024]{1,0:T(8,128)(2,1)S(1)}, u32[]{:S(2)}, u32[]{:S(2)}) collective-permute-start(bf16[256,1024]{1,0:T(8,128)(2,1)S(1)} %get-tuple-element.888), channel_id=1, source_target_pairs={{0,1},{1,0},{2,3},{3,2},{4,5},{5,4},{6,7},{7,6},{8,9},{9,8},{10,11... | collective-permute-start | bytes 1572872 | tf_op jit(solution)/shard_map/ppermute | solution.py:553
  140.4 3.2 %collective-permute-start.29 = (bf16[256,1024]{1,0:T(8,128)(2,1)S(1)}, bf16[256,1024]{1,0:T(8,128)(2,1)S(1)}, u32[]{:S(2)}, u32[]{:S(2)}) collective-permute-start(bf16[256,1024]{1,0:T(8,128)(2,1)S(1)} %get-tuple-element.889), channel_id=1, source_target_pairs={{0,1},{1,0},{2,3},{3,2},{4,5},{5,4},{6,7},{7,6},{8,9},{9,8},{10,11... | collective-permute-start | bytes 1572872 | tf_op jit(solution)/shard_map/ppermute | solution.py:553
  140.9 2.5 %collective-permute-start.32 = (f32[64,1024]{1,0:T(8,128)S(1)}, f32[64,1024]{1,0:T(8,128)S(1)}, u32[]{:S(2)}, u32[]{:S(2)}) collective-permute-start(f32[64,1024]{1,0:T(8,128)S(1)} %convert_add_fusion.kept), channel_id=1, source_target_pairs={{0,1},{1,0},{2,3},{3,2},{4,5},{5,4},{6,7},{7,6},{8,9},{9,8},{10,11... | collective-permute-start | bytes 786440 | tf_op jit(solution)/shard_map/ppermute | solution.py:553
  150.8 3.1 %collective-permute-start.35 = (bf16[512,1024]{1,0:T(8,128)(2,1)}, bf16[512,1024]{1,0:T(8,128)(2,1)S(1)}, u32[]{:S(2)}, u32[]{:S(2)}) collective-permute-start(bf16[512,1024]{1,0:T(8,128)(2,1)} %get-tuple-element.907), channel_id=1, source_target_pairs={{0,1},{1,0},{2,3},{3,2},{4,5},{5,4},{6,7},{7,6},{8,9},{9,8},{10,11... | collective-permute-start | bytes 3145736 | tf_op jit(solution)/shard_map/ppermute | solution.py:553
  152.4 2.7 %collective-permute-start.34 = (bf16[512,1024]{1,0:T(8,128)(2,1)S(1)}, bf16[512,1024]{1,0:T(8,128)(2,1)S(1)}, u32[]{:S(2)}, u32[]{:S(2)}) collective-permute-start(bf16[512,1024]{1,0:T(8,128)(2,1)S(1)} %shard_map.132.value), channel_id=1, source_target_pairs={{0,1},{1,0},{2,3},{3,2},{4,5},{5,4},{6,7},{7,6},{8,9},{9,8},{10,11... | collective-permute-start | bytes 3145736 | tf_op jit(solution)/shard_map/ppermute | solution.py:553
  (30 other events, 150.3 us)

commit v5 on v4

--- a/solution.py
+++ b/solution.py
@@ -206,7 +206,7 @@
     split = extra[0].shape[0] // 2 if extra else 0
     outs = [jax.ShapeDtypeStruct((half, width), B16)]
     if extra:
-        outs.append(jax.ShapeDtypeStruct((split, width), F32))
+        outs.append(kept_in_hbm(jax.ShapeDtypeStruct((split, width), F32)))
         outs.append(jax.ShapeDtypeStruct((split, width), B16))
     return call(
         functools.partial(piece_body, len(ours), 1 if extra else 0),
@@ -220,7 +220,7 @@
         [cols(v.shape[0]) for v in outs],
         [pltpu.VMEM((rows, half), B16)] * 2 + [pltpu.SemaphoreType.DMA((2,))],
         0,
-        pinned=range(2 * len(ours)),
+        pinned=[*range(2 * len(ours))] + [2 * len(ours) + 2] * (1 if extra else 0),
     )
 
 
@@ -383,7 +383,7 @@
     ]
     body = functools.partial(ranks_body, rank)
     specs = [whole(v) for v in arrays]
-    return call(body, table, (1,), arrays, specs, [kept_in_hbm(v) for v in outs], [whole(v) for v in outs], [], 0)
+    return call(body, table, (1,), arrays, specs, [kept_in_hbm(v) for v in outs], [whole(v) for v in outs], [], 0, pinned=(4,))
 
 
 def maps_body(rank, count, table, *refs):
@@ -420,7 +420,7 @@
     ]
     body = functools.partial(maps_body, rank, len(parts))
     specs = [whole(v) for v in arrays]
-    return call(body, table, (1,), arrays, specs, [kept_in_hbm(v) for v in outs], [whole(v) for v in outs], [], 0)
+    return call(body, table, (1,), arrays, specs, [kept_in_hbm(v) for v in outs], [whole(v) for v in outs], [], 0, pinned=(len(parts) + 1,))
 
 
 def lora_body(table, low, up, back, down, out, into):
@@ -487,7 +487,7 @@
     spec = pl.BlockSpec((rows // 2, width), lambda i, t: (i, 0))
     out = jax.ShapeDtypeStruct(a.shape, B16)
     table = jnp.zeros((1,), jnp.int32)
-    return call(add_body, table, (2,), [a, b], [spec] * 2, out, spec, [], 0)
+    return call(add_body, table, (2,), [a, b], [spec] * 2, out, spec, [], 0, pinned=(0, 1))
 
 
 def mask_body(tenants, slots, table, mine, theirs, grads, their_grads, slot_rows, live):
@@ -522,7 +522,7 @@
     ]
     body = functools.partial(mask_body, tenants, slots)
     specs = [whole(mine), whole(theirs)]
-    return call(body, table, (1,), [mine, theirs], specs, outs, [whole(v) for v in outs], [], 0)
+    return call(body, table, (1,), [mine, theirs], specs, [*outs[:3], kept_in_hbm(outs[3])], [whole(v) for v in outs], [], 0, pinned=(0, 1))
 
 
 def kept_in_hbm(shape):

time: 157 us -> 154 us (0.981)
  local copies, waits for them, and re-layouts: 13.1 us -> 3.01 us
  Pallas kernels: 81.8 us -> 87.6 us
    unnamed x52 -> x36, local copies, waits for them, and re-layouts: 11 us -> 0.91 us
    pallas_call x26, Pallas kernels: 81.8 us -> 87.6 us  [call(): pl.pallas_call(body, grid_spec=pltpu.PrefetchScalarGridSpec(num_scalar_pr...]
  transfers between devices with their start and end apart: 36 -> 36, of which waited for: 10 -> 10; matrix products, arithmetic and copies ran while one was open for 3% -> 3% of each run, Pallas kernels for 52% -> 57%
where the time goes in v5:
time: 154 us; the launch traced here: 153 us
  Pallas kernels  87.6 us (57%)
  starting transfers between devices  41.8 us (27%)
  waiting for transfers between devices  16.3 us (11%)
  other arithmetic  3.1 us (2%)
  local copies, waits for them, and re-layouts  3.01 us (2%)
    pallas_call x26, Pallas kernels, call(): pl.pallas_call(body, grid_spec=pltpu.PrefetchScalarGridSpec(num_scalar_pr...  87.6 us
    ppermute x8, starting transfers between devices, along(): return lax.ppermute(value, ('tensor', 'dp'), line_pairs)  28.6 us
    ppermute x6, waiting for transfers between devices, other_tenant(): return lax.ppermute(value, 'tenant', swap)  8.18 us
    ppermute x19, waiting for transfers between devices, other_core(): return lax.ppermute(value, 'dp', swap)  8.13 us
    ppermute x6, starting transfers between devices, other_tenant(): return lax.ppermute(value, 'tenant', swap)  6.57 us
    ppermute x3, starting transfers between devices, shards_line(): st['part', d] = lax.ppermute(st['part'], 'tensor', pairs)  3.88 us
  transfers between devices with their start and end apart: 36, of which 10 were waited for; matrix products, arithmetic and copies ran while one was open for 3% of the time, Pallas kernels for 57%

profile of v5, /device:TPU:0, one launch (start us, length us, event | category | flops | bytes accessed | tf_op | source)
XLA Modules:
  0.0 152.9 jit_solution(12184142395608287317)
XLA Ops:
  1.2 5.0 %collective-permute-start.4 = (bf16[512,1024]{1,0:T(8,128)(2,1)}, bf16[512,1024]{1,0:T(8,128)(2,1)S(1)}, u32[]{:S(2)}, u32[]{:S(2)}) collective-permute-start(bf16[512,1024]{1,0:T(8,128)(2,1)} %refs_0_.1), channel_id=1, source_target_pairs={{0,4},{5,1},{4,8},{9,5},{8,12},{13,9},{2,6},{7,3},{6,10},{11,7},{1... | collective-permute-start | bytes 3145736 | tf_op jit(solution)/shard_map/ppermute | solution.py:547
  11.1 3.1 %shard_map.110 = (bf16[512,1024]{1,0:T(8,128)(2,1)S(1)}, bf16[512,1024]{1,0:T(8,128)(2,1)S(1)}, s32[1,512]{1,0:T(1,128)S(1)}, f32[512,1]{1,0:T(8,128)}) custom-call(s32[19]{0:T(128)S(1)} %concatenate.4.table, bf16[512,1024]{1,0:T(8,128)(2,1)} %mine.1, bf16[512,1024]{1,0:T(8,128)(2,1)} %collective-permute-done.2.theirs), custom_call_target="tpu_custom_call" | custom-call | flops 1 | bytes 1 | tf_op jit(solution)/shard_map/pallas_call | solution.py:103
  14.2 4.4 %collective-permute-start.10 = (bf16[512,1024]{1,0:T(8,128)(2,1)}, bf16[512,1024]{1,0:T(8,128)(2,1)}, u32[]{:S(2)}, u32[]{:S(2)}) collective-permute-start(bf16[512,1024]{1,0:T(8,128)(2,1)} %collective-permute-done.refs_1_), channel_id=1, source_target_pairs={{0,4},{5,1},{4,8},{9,5},{8,12},{13,9},{2,6},{7,3},{6,10},{11,7},{1... | collective-permute-start | bytes 3145736 | tf_op jit(solution)/shard_map/ppermute | solution.py:547
  18.7 4.2 %shard_map.111.a = bf16[512,1024]{1,0:T(8,128)(2,1)} custom-call(s32[2]{0:T(128)S(1)} %pad_add_fusion.table, bf16[512,1024]{1,0:T(8,128)(2,1)} %refs_0_.1, bf16[512,1024]{1,0:T(8,128)(2,1)} %collective-permute-done.refs_1_, bf16[512,1024]{1,0:T(8,128)(2,1)S(1)} %get-tuple-element.798.refs_2_.grads.refs_6_.refs_4_.refs_8_, ...), custom_call_target="tpu_custom_call" | custom-call | flops 1 | bytes 1 | tf_op jit(solution)/shard_map/pallas_call | solution.py:103
  25.0 2.8 %shard_map.112 = (bf16[128,1024]{1,0:T(8,128)(2,1)}, bf16[128,1024]{1,0:T(8,128)(2,1)}, bf16[32,512]{1,0:T(8,128)(2,1)}) custom-call(s32[1]{0:T(128)} %bitcast.7.table, bf16[2,64,1024]{2,1,0:T(8,128)(2,1)S(1)} %pad_maximum_fusion.mine, bf16[64,1024]{1,0:T(8,128)(2,1)S(1)} %collective-permute-done.1.fetched, bf16[64,1024]{1,0:T(8,128)(2,1)} %collective-permute-done.3.shared, ...), custom_call_target="tpu_custom_call" | custom-call | flops 1 | bytes 1 | tf_op jit(solution)/shard_map/pallas_call | solution.py:103
  28.5 3.2 %collective-permute-start.7 = (bf16[32,512]{1,0:T(8,128)(2,1)}, bf16[32,512]{1,0:T(8,128)(2,1)S(1)}, u32[]{:S(2)}, u32[]{:S(2)}) collective-permute-start(bf16[32,512]{1,0:T(8,128)(2,1)} %get-tuple-element.516.refs_0_), channel_id=1, source_target_pairs={{0,12},{4,0},{8,4},{12,8},{1,13},{5,1},{9,5},{13,9},{2,14},{6,2},{... | collective-permute-start | bytes 98312 | tf_op jit(solution)/shard_map/ppermute | solution.py:650
  31.7 4.2 %shard_map.113 = (bf16[512,1024]{1,0:T(8,128)(2,1)}, bf16[512,512]{1,0:T(8,128)(2,1)S(1)}) custom-call(s32[3]{0:T(128)S(1)} %get-tuple-element.913.table, bf16[512,1024]{1,0:T(8,128)(2,1)S(1)} %get-tuple-element.798.refs_2_.grads.refs_6_.refs_4_.refs_8_, bf16[4096,1024]{1,0:T(8,128)(2,1)} %refs_25_, ...), custom_call_target="tpu_custom_call" | custom-call | flops 1 | bytes 1 | tf_op jit(solution)/shard_map/pallas_call | solution.py:103
  36.0 3.2 %collective-permute-start.13 = (bf16[512,1024]{1,0:T(8,128)(2,1)}, bf16[512,1024]{1,0:T(8,128)(2,1)}, u32[]{:S(2)}, u32[]{:S(2)}) collective-permute-start(bf16[512,1024]{1,0:T(8,128)(2,1)} %get-tuple-element.586), channel_id=1, source_target_pairs={{0,4},{5,1},{4,8},{9,5},{8,12},{13,9},{2,6},{7,3},{6,10},{11,7},{1... | collective-permute-start | bytes 3145736 | tf_op jit(solution)/shard_map/ppermute | solution.py:547
  39.3 2.9 %shard_map.114 = (bf16[128,512]{1,0:T(8,128)(2,1)}, bf16[128,512]{1,0:T(8,128)(2,1)}, f32[128,1024]{1,0:T(8,128)}, bf16[128,1024]{1,0:T(8,128)(2,1)}) custom-call(s32[1]{0:T(128)} %bitcast.7.table, bf16[32,512]{1,0:T(8,128)(2,1)S(1)} %copy-done.11, bf16[32,512]{1,0:T(8,128)(2,1)S(1)} %collective-permute-done.5.refs_1_, ...), custom_call_target="tpu_custom_call" | custom-call | flops 1 | bytes 1 | tf_op jit(solution)/shard_map/pallas_call | solution.py:103
  43.9 4.5 %shard_map.115 = (bf16[512,1024]{1,0:T(8,128)(2,1)}, bf16[512,512]{1,0:T(8,128)(2,1)}) custom-call(s32[3]{0:T(128)S(1)} %get-tuple-element.913.table, bf16[512,1024]{1,0:T(8,128)(2,1)S(1)} %get-tuple-element.799.refs_3_.grads.refs_5_.refs_9_, bf16[4096,1024]{1,0:T(8,128)(2,1)} %refs_25_, bf16[512,1024]{1,0:T(8,128)(2,1)} %collective-permute-done.10.came.refs_3_.refs_5_.refs_11_), custom_call_target="tpu_custom_call" | custom-call | flops 1 | bytes 1 | tf_op jit(solution)/shard_map/pallas_call | solution.py:103
  50.7 4.3 %shard_map.116.a = bf16[512,1024]{1,0:T(8,128)(2,1)} custom-call(s32[2]{0:T(128)S(1)} %pad_add_fusion.1.table, bf16[512,512]{1,0:T(8,128)(2,1)} %collective-permute-done.12.refs_0_.refs_2_.refs_6_, bf16[512,1024]{1,0:T(8,128)(2,1)} %copy-done, bf16[512,512]{1,0:T(8,128)(2,1)} %copy-done.12, ...), custom_call_target="tpu_custom_call" | custom-call | flops 1 | bytes 1 | tf_op jit(solution)/shard_map/pallas_call | solution.py:103
  55.0 2.6 %shard_map.117 = (bf16[4096,1024]{1,0:T(8,128)(2,1)}, bf16[512,1024]{1,0:T(8,128)(2,1)}) custom-call(s32[1]{0:T(128)} %bitcast.12.table, bf16[512,1024]{1,0:T(8,128)(2,1)} %shard_map.111.a, bf16[512,1024]{1,0:T(8,128)(2,1)} %collective-permute-done.11.b), custom_call_target="tpu_custom_call" | custom-call | flops 1 | bytes 1 | tf_op jit(solution)/shard_map/pallas_call | solution.py:103
  57.7 4.3 %shard_map.118 = (bf16[512,1024]{1,0:T(8,128)(2,1)}, bf16[512,512]{1,0:T(8,128)(2,1)S(1)}) custom-call(s32[3]{0:T(128)S(1)} %get-tuple-element.914.table, bf16[512,1024]{1,0:T(8,128)(2,1)S(1)} %get-tuple-element.798.refs_2_.grads.refs_6_.refs_4_.refs_8_, bf16[4096,1024]{1,0:T(8,128)(2,1)} %refs_25_, ...), custom_call_target="tpu_custom_call" | custom-call | flops 1 | bytes 1 | tf_op jit(solution)/shard_map/pallas_call | solution.py:103
  63.5 3.9 %collective-permute-start.18 = (bf16[512,1024]{1,0:T(8,128)(2,1)}, bf16[512,1024]{1,0:T(8,128)(2,1)}, u32[]{:S(2)}, u32[]{:S(2)}) collective-permute-start(bf16[512,1024]{1,0:T(8,128)(2,1)} %get-tuple-element.710), channel_id=1, source_target_pairs={{0,4},{5,1},{4,8},{9,5},{8,12},{13,9},{2,6},{7,3},{6,10},{11,7},{1... | collective-permute-start | bytes 3145736 | tf_op jit(solution)/shard_map/ppermute | solution.py:547
  67.4 3.6 %shard_map.119.term = bf16[512,1024]{1,0:T(8,128)(2,1)} custom-call(s32[1]{0:T(128)} %bitcast.15.table, bf16[512,1024]{1,0:T(8,128)(2,1)S(1)} %get-tuple-element.798.refs_2_.grads.refs_6_.refs_4_.refs_8_, bf16[4096,1024]{1,0:T(8,128)(2,1)} %refs_25_), custom_call_target="tpu_custom_call" | custom-call | flops 1 | bytes 1 | tf_op jit(solution)/shard_map/pallas_call | solution.py:103
  70.9 4.3 %shard_map.120 = (bf16[512,1024]{1,0:T(8,128)(2,1)}, bf16[512,512]{1,0:T(8,128)(2,1)}) custom-call(s32[3]{0:T(128)S(1)} %get-tuple-element.914.table, bf16[512,1024]{1,0:T(8,128)(2,1)S(1)} %get-tuple-element.799.refs_3_.grads.refs_5_.refs_9_, bf16[4096,1024]{1,0:T(8,128)(2,1)} %refs_25_, ...), custom_call_target="tpu_custom_call" | custom-call | flops 1 | bytes 1 | tf_op jit(solution)/shard_map/pallas_call | solution.py:103
  75.3 3.1 %collective-permute-start.22 = (bf16[512,1024]{1,0:T(8,128)(2,1)}, bf16[512,1024]{1,0:T(8,128)(2,1)}, u32[]{:S(2)}, u32[]{:S(2)}) collective-permute-start(bf16[512,1024]{1,0:T(8,128)(2,1)} %get-tuple-element.768), channel_id=1, source_target_pairs={{0,4},{5,1},{4,8},{9,5},{8,12},{13,9},{2,6},{7,3},{6,10},{11,7},{1... | collective-permute-start | bytes 3145736 | tf_op jit(solution)/shard_map/ppermute | solution.py:547
  78.5 5.2 %shard_map.121 = (bf16[512,1024]{1,0:T(8,128)(2,1)}, f32[64,1024]{1,0:T(8,128)}, bf16[64,1024]{1,0:T(8,128)(2,1)S(1)}) custom-call(s32[2]{0:T(128)S(1)} %pad_add_fusion.2.table, bf16[512,512]{1,0:T(8,128)(2,1)} %collective-permute-done.12.refs_0_.refs_2_.refs_6_, bf16[512,1024]{1,0:T(8,128)(2,1)} %copy-done, ...), custom_call_target="tpu_custom_call" | custom-call | flops 1 | bytes 1 | tf_op jit(solution)/shard_map/pallas_call | solution.py:103
  83.7 4.1 %collective-permute-done.17.b = bf16[512,1024]{1,0:T(8,128)(2,1)} collective-permute-done((bf16[512,1024]{1,0:T(8,128)(2,1)}, bf16[512,1024]{1,0:T(8,128)(2,1)}, u32[]{:S(2)}, u32[]{:S(2)}) %collective-permute-start.17) | collective-permute-done | bytes 1048608 | tf_op jit(solution)/shard_map/ppermute | solution.py:550
  87.8 2.6 %shard_map.122 = (bf16[4096,1024]{1,0:T(8,128)(2,1)}, bf16[512,1024]{1,0:T(8,128)(2,1)}) custom-call(s32[1]{0:T(128)} %bitcast.17.table, bf16[512,1024]{1,0:T(8,128)(2,1)} %shard_map.116.a, bf16[512,1024]{1,0:T(8,128)(2,1)} %collective-permute-done.17.b, bf16[4096,1024]{1,0:T(8,128)(2,1)} %get-tuple-element.701.refs_0_), custom_call_target="tpu_custom_call", output_to_operand_aliasing={{0}: (3, {})} | custom-call | flops 1 | bytes 1 | tf_op jit(solution)/shard_map/pallas_call | solution.py:103
  92.1 4.3 %shard_map.123 = (bf16[512,1024]{1,0:T(8,128)(2,1)}, bf16[512,512]{1,0:T(8,128)(2,1)S(1)}) custom-call(s32[3]{0:T(128)S(1)} %add_add_fusion.2.table, bf16[512,1024]{1,0:T(8,128)(2,1)S(1)} %get-tuple-element.798.refs_2_.grads.refs_6_.refs_4_.refs_8_, bf16[4096,1024]{1,0:T(8,128)(2,1)} %refs_25_, bf16[512,1024]{1,0:T(8,128)(2,1)} %collective-permute-done.18.came.refs_3_.refs_17_), custom_call_target="tpu_custom_call" | custom-call | flops 1 | bytes 1 | tf_op jit(solution)/shard_map/pallas_call | solution.py:103
  97.2 3.2 %collective-permute-start.25 = (bf16[512,1024]{1,0:T(8,128)(2,1)}, bf16[512,1024]{1,0:T(8,128)(2,1)}, u32[]{:S(2)}, u32[]{:S(2)}) collective-permute-start(bf16[512,1024]{1,0:T(8,128)(2,1)} %get-tuple-element.847), channel_id=1, source_target_pairs={{0,4},{5,1},{4,8},{9,5},{8,12},{13,9},{2,6},{7,3},{6,10},{11,7},{1... | collective-permute-start | bytes 3145736 | tf_op jit(solution)/shard_map/ppermute | solution.py:547
  100.4 2.1 %shard_map.124.refs_0_ = bf16[4096,1024]{1,0:T(8,128)(2,1)} custom-call(s32[1]{0:T(128)} %bitcast.20.table, bf16[512,1024]{1,0:T(8,128)(2,1)} %collective-permute-done.19.value, bf16[4096,1024]{1,0:T(8,128)(2,1)} %get-tuple-element.751.refs_0_), custom_call_target="tpu_custom_call", output_to_operand_aliasing={{}: (2, {})} | custom-call | flops 1 | bytes 1 | tf_op jit(solution)/shard_map/pallas_call | solution.py:103
  104.5 4.3 %shard_map.126 = (bf16[512,1024]{1,0:T(8,128)(2,1)}, bf16[512,512]{1,0:T(8,128)(2,1)S(1)}) custom-call(s32[3]{0:T(128)S(1)} %add_add_fusion.2.table, bf16[512,1024]{1,0:T(8,128)(2,1)S(1)} %get-tuple-element.799.refs_3_.grads.refs_5_.refs_9_, bf16[4096,1024]{1,0:T(8,128)(2,1)} %refs_25_, bf16[512,1024]{1,0:T(8,128)(2,1)} %collective-permute-done.22.came.refs_7_.refs_21_), custom_call_target="tpu_custom_call" | custom-call | flops 1 | bytes 1 | tf_op jit(solution)/shard_map/pallas_call | solution.py:103
  108.8 4.0 %collective-permute-start.27 = (bf16[512,1024]{1,0:T(8,128)(2,1)}, bf16[512,1024]{1,0:T(8,128)(2,1)}, u32[]{:S(2)}, u32[]{:S(2)}) collective-permute-start(bf16[512,1024]{1,0:T(8,128)(2,1)} %get-tuple-element.877), channel_id=1, source_target_pairs={{0,4},{5,1},{4,8},{9,5},{8,12},{13,9},{2,6},{7,3},{6,10},{11,7},{1... | collective-permute-start | bytes 3145736 | tf_op jit(solution)/shard_map/ppermute | solution.py:547
  112.8 2.0 %collective-permute-done.23.refs_2_.refs_16_ = bf16[512,512]{1,0:T(8,128)(2,1)} collective-permute-done((bf16[512,512]{1,0:T(8,128)(2,1)S(1)}, bf16[512,512]{1,0:T(8,128)(2,1)}, u32[]{:S(2)}, u32[]{:S(2)}) %collective-permute-start.23) | collective-permute-done | bytes 524320 | tf_op jit(solution)/shard_map/ppermute | solution.py:553
  114.8 3.5 %shard_map.127.a = bf16[512,1024]{1,0:T(8,128)(2,1)S(1)} custom-call(s32[2]{0:T(128)S(1)} %pad_add_fusion.3.table, bf16[512,512]{1,0:T(8,128)(2,1)} %collective-permute-done.16.refs_2_.refs_0_.refs_8_.refs_14_, bf16[512,1024]{1,0:T(8,128)(2,1)} %collective-permute-done.13.came.refs_3_.refs_1_.refs_9_.refs_15_, ...), custom_call_target="tpu_custom_call" | custom-call | flops 1 | bytes 1 | tf_op jit(solution)/shard_map/pallas_call | solution.py:103
  118.3 4.1 %collective-permute-done.24.b = bf16[512,1024]{1,0:T(8,128)(2,1)} collective-permute-done((bf16[512,1024]{1,0:T(8,128)(2,1)}, bf16[512,1024]{1,0:T(8,128)(2,1)}, u32[]{:S(2)}, u32[]{:S(2)}) %collective-permute-start.24) | collective-permute-done | bytes 1048608 | tf_op jit(solution)/shard_map/ppermute | solution.py:550
  123.2 2.8 %shard_map.128 = (bf16[4096,1024]{1,0:T(8,128)(2,1)}, bf16[512,1024]{1,0:T(8,128)(2,1)}) custom-call(s32[1]{0:T(128)} %bitcast.22.table, bf16[512,1024]{1,0:T(8,128)(2,1)} %get-tuple-element.828.a, bf16[512,1024]{1,0:T(8,128)(2,1)} %collective-permute-done.24.b, bf16[4096,1024]{1,0:T(8,128)(2,1)} %shard_map.124.refs_0_), custom_call_target="tpu_custom_call", output_to_operand_aliasing={{0}: (3, {})} | custom-call | flops 1 | bytes 1 | tf_op jit(solution)/shard_map/pallas_call | solution.py:103
  126.0 2.2 %shard_map.129.refs_0_ = bf16[4096,1024]{1,0:T(8,128)(2,1)} custom-call(s32[1]{0:T(128)} %bitcast.23.table, bf16[512,1024]{1,0:T(8,128)(2,1)} %collective-permute-done.26.value, bf16[4096,1024]{1,0:T(8,128)(2,1)} %get-tuple-element.857.refs_0_), custom_call_target="tpu_custom_call", output_to_operand_aliasing={{}: (2, {})} | custom-call | flops 1 | bytes 1 | tf_op jit(solution)/shard_map/pallas_call | solution.py:103
  129.1 8.7 %shard_map.130 = (f32[512,1024]{1,0:T(8,128)}, bf16[256,1024]{1,0:T(8,128)(2,1)S(1)}, bf16[256,1024]{1,0:T(8,128)(2,1)S(1)}) custom-call(s32[9]{0:T(128)S(1)} %stack.148.table, bf16[512,1024]{1,0:T(8,128)(2,1)} %refs_0_.1, bf16[512,1024]{1,0:T(8,128)(2,1)} %collective-permute-done.refs_1_, bf16[512,512]{1,0:T(8,128)(2,1)} %collective-permute-done.12.refs_0_.refs_2_.refs_6_, ...), custom_call_target="tpu_custom_call" | custom-call | flops 1 | bytes 1 | tf_op jit(solution)/shard_map/pallas_call | solution.py:103
  142.8 4.4 %shard_map.131 = (bf16[512,1024]{1,0:T(8,128)(2,1)}, bf16[512,1024]{1,0:T(8,128)(2,1)}, f32[64,1024]{1,0:T(8,128)}, f32[64,1024]{1,0:T(8,128)}) custom-call(s32[1]{0:T(128)} %bitcast.7.table, f32[512,1024]{1,0:T(8,128)} %get-tuple-element.883.here, f32[512,1]{1,0:T(8,128)S(1)} %copy-done.6, bf16[512,1024]{1,0:T(8,128)(2,1)S(1)} %copy-done.4, ...), custom_call_target="tpu_custom_call" | custom-call | flops 1 | bytes 1 | tf_op jit(solution)/shard_map/pallas_call | solution.py:103
  (115 shorter events, 30.7 us)
Async XLA Ops:
  0.6 10.4 %collective-permute-start.2 = (bf16[512,1024]{1,0:T(8,128)(2,1)}, bf16[512,1024]{1,0:T(8,128)(2,1)}, u32[]{:S(2)}, u32[]{:S(2)}) collective-permute-start(bf16[512,1024]{1,0:T(8,128)(2,1)} %mine.1), channel_id=1, source_target_pairs={{0,1},{1,0},{2,3},{3,2},{4,5},{5,4},{6,7},{7,6},{8,9},{9,8},{10,11... | collective-permute-start | bytes 3145736 | tf_op jit(solution)/shard_map/ppermute | solution.py:553
  1.1 13.1 %collective-permute-start = (bf16[512,1024]{1,0:T(8,128)(2,1)}, bf16[512,1024]{1,0:T(8,128)(2,1)}, u32[]{:S(2)}, u32[]{:S(2)}) collective-permute-start(bf16[512,1024]{1,0:T(8,128)(2,1)} %refs_0_.1), channel_id=1, source_target_pairs={{0,1},{1,0},{2,3},{3,2},{4,5},{5,4},{6,7},{7,6},{8,9},{9,8},{10,11... | collective-permute-start | bytes 3145736 | tf_op jit(solution)/shard_map/ppermute | solution.py:553
  1.2 26.5 %collective-permute-start.4 = (bf16[512,1024]{1,0:T(8,128)(2,1)}, bf16[512,1024]{1,0:T(8,128)(2,1)S(1)}, u32[]{:S(2)}, u32[]{:S(2)}) collective-permute-start(bf16[512,1024]{1,0:T(8,128)(2,1)} %refs_0_.1), channel_id=1, source_target_pairs={{0,4},{5,1},{4,8},{9,5},{8,12},{13,9},{2,6},{7,3},{6,10},{11,7},{1... | collective-permute-start | bytes 3145736 | tf_op jit(solution)/shard_map/ppermute | solution.py:547
  7.8 6.4 %collective-permute-start.1 = (bf16[64,1024]{1,0:T(8,128)(2,1)}, bf16[64,1024]{1,0:T(8,128)(2,1)S(1)}, u32[]{:S(2)}, u32[]{:S(2)}) collective-permute-start(bf16[64,1024]{1,0:T(8,128)(2,1)} %fusion.1), channel_id=1, source_target_pairs={{0,2},{2,0},{1,3},{3,1},{4,6},{6,4},{5,7},{7,5},{8,10},{10,8},{9,1... | collective-permute-start | bytes 393224 | tf_op jit(solution)/shard_map/ppermute | solution.py:550
  14.2 29.7 %collective-permute-start.10 = (bf16[512,1024]{1,0:T(8,128)(2,1)}, bf16[512,1024]{1,0:T(8,128)(2,1)}, u32[]{:S(2)}, u32[]{:S(2)}) collective-permute-start(bf16[512,1024]{1,0:T(8,128)(2,1)} %collective-permute-done.refs_1_), channel_id=1, source_target_pairs={{0,4},{5,1},{4,8},{9,5},{8,12},{13,9},{2,6},{7,3},{6,10},{11,7},{1... | collective-permute-start | bytes 3145736 | tf_op jit(solution)/shard_map/ppermute | solution.py:547
  22.9 25.5 %collective-permute-start.11 = (bf16[512,1024]{1,0:T(8,128)(2,1)}, bf16[512,1024]{1,0:T(8,128)(2,1)}, u32[]{:S(2)}, u32[]{:S(2)}) collective-permute-start(bf16[512,1024]{1,0:T(8,128)(2,1)} %shard_map.111.a), channel_id=1, source_target_pairs={{0,2},{2,0},{1,3},{3,1},{4,6},{6,4},{5,7},{7,5},{8,10},{10,8},{9,1... | collective-permute-start | bytes 3145736 | tf_op jit(solution)/shard_map/ppermute | solution.py:550
  27.8 8.2 %collective-permute-start.5 = (bf16[32,512]{1,0:T(8,128)(2,1)}, bf16[32,512]{1,0:T(8,128)(2,1)S(1)}, u32[]{:S(2)}, u32[]{:S(2)}) collective-permute-start(bf16[32,512]{1,0:T(8,128)(2,1)} %get-tuple-element.516.refs_0_), channel_id=1, source_target_pairs={{0,4},{4,8},{8,12},{12,0},{1,5},{5,9},{9,13},{13,1},{2,6},{6,10},{... | collective-permute-start | bytes 98312 | tf_op jit(solution)/shard_map/ppermute | solution.py:650
  28.5 7.5 %collective-permute-start.6 = (bf16[32,512]{1,0:T(8,128)(2,1)}, bf16[32,512]{1,0:T(8,128)(2,1)S(1)}, u32[]{:S(2)}, u32[]{:S(2)}) collective-permute-start(bf16[32,512]{1,0:T(8,128)(2,1)} %get-tuple-element.516.refs_0_), channel_id=1, source_target_pairs={{0,8},{4,12},{8,0},{12,4},{1,9},{5,13},{9,1},{13,5},{2,10},{6,14},... | collective-permute-start | bytes 98312 | tf_op jit(solution)/shard_map/ppermute | solution.py:650
  28.5 7.5 %collective-permute-start.7 = (bf16[32,512]{1,0:T(8,128)(2,1)}, bf16[32,512]{1,0:T(8,128)(2,1)S(1)}, u32[]{:S(2)}, u32[]{:S(2)}) collective-permute-start(bf16[32,512]{1,0:T(8,128)(2,1)} %get-tuple-element.516.refs_0_), channel_id=1, source_target_pairs={{0,12},{4,0},{8,4},{12,8},{1,13},{5,1},{9,5},{13,9},{2,14},{6,2},{... | collective-permute-start | bytes 98312 | tf_op jit(solution)/shard_map/ppermute | solution.py:650
  36.0 8.0 %collective-permute-start.8 = (bf16[512,512]{1,0:T(8,128)(2,1)S(1)}, bf16[512,512]{1,0:T(8,128)(2,1)S(1)}, u32[]{:S(2)}, u32[]{:S(2)}) collective-permute-start(bf16[512,512]{1,0:T(8,128)(2,1)S(1)} %get-tuple-element.515), channel_id=1, source_target_pairs={{0,1},{1,0},{2,3},{3,2},{4,5},{5,4},{6,7},{7,6},{8,9},{9,8},{10,11... | collective-permute-start | bytes 1572872 | tf_op jit(solution)/shard_map/ppermute | solution.py:553
  36.0 21.6 %collective-permute-start.13 = (bf16[512,1024]{1,0:T(8,128)(2,1)}, bf16[512,1024]{1,0:T(8,128)(2,1)}, u32[]{:S(2)}, u32[]{:S(2)}) collective-permute-start(bf16[512,1024]{1,0:T(8,128)(2,1)} %get-tuple-element.586), channel_id=1, source_target_pairs={{0,4},{5,1},{4,8},{9,5},{8,12},{13,9},{2,6},{7,3},{6,10},{11,7},{1... | collective-permute-start | bytes 3145736 | tf_op jit(solution)/shard_map/ppermute | solution.py:547
  48.4 2.3 %collective-permute-start.12 = (bf16[512,512]{1,0:T(8,128)(2,1)}, bf16[512,512]{1,0:T(8,128)(2,1)}, u32[]{:S(2)}, u32[]{:S(2)}) collective-permute-start(bf16[512,512]{1,0:T(8,128)(2,1)} %get-tuple-element.563), channel_id=1, source_target_pairs={{0,1},{1,0},{2,3},{3,2},{4,5},{5,4},{6,7},{7,6},{8,9},{9,8},{10,11... | collective-permute-start | bytes 1572872 | tf_op jit(solution)/shard_map/ppermute | solution.py:553
  48.5 22.4 %collective-permute-start.15 = (bf16[512,1024]{1,0:T(8,128)(2,1)}, bf16[512,1024]{1,0:T(8,128)(2,1)S(1)}, u32[]{:S(2)}, u32[]{:S(2)}) collective-permute-start(bf16[512,1024]{1,0:T(8,128)(2,1)} %get-tuple-element.632), channel_id=1, source_target_pairs={{0,4},{5,1},{4,8},{9,5},{8,12},{13,9},{2,6},{7,3},{6,10},{11,7},{1... | collective-permute-start | bytes 3145736 | tf_op jit(solution)/shard_map/ppermute | solution.py:547
  62.0 9.0 %collective-permute-start.14 = (bf16[512,512]{1,0:T(8,128)(2,1)S(1)}, bf16[512,512]{1,0:T(8,128)(2,1)S(1)}, u32[]{:S(2)}, u32[]{:S(2)}) collective-permute-start(bf16[512,512]{1,0:T(8,128)(2,1)S(1)} %get-tuple-element.631), channel_id=1, source_target_pairs={{0,1},{1,0},{2,3},{3,2},{4,5},{5,4},{6,7},{7,6},{8,9},{9,8},{10,11... | collective-permute-start | bytes 1572872 | tf_op jit(solution)/shard_map/ppermute | solution.py:553
  62.0 25.9 %collective-permute-start.17 = (bf16[512,1024]{1,0:T(8,128)(2,1)}, bf16[512,1024]{1,0:T(8,128)(2,1)}, u32[]{:S(2)}, u32[]{:S(2)}) collective-permute-start(bf16[512,1024]{1,0:T(8,128)(2,1)} %shard_map.116.a), channel_id=1, source_target_pairs={{0,2},{2,0},{1,3},{3,1},{4,6},{6,4},{5,7},{7,5},{8,10},{10,8},{9,1... | collective-permute-start | bytes 3145736 | tf_op jit(solution)/shard_map/ppermute | solution.py:550
  63.5 27.0 %collective-permute-start.18 = (bf16[512,1024]{1,0:T(8,128)(2,1)}, bf16[512,1024]{1,0:T(8,128)(2,1)}, u32[]{:S(2)}, u32[]{:S(2)}) collective-permute-start(bf16[512,1024]{1,0:T(8,128)(2,1)} %get-tuple-element.710), channel_id=1, source_target_pairs={{0,4},{5,1},{4,8},{9,5},{8,12},{13,9},{2,6},{7,3},{6,10},{11,7},{1... | collective-permute-start | bytes 3145736 | tf_op jit(solution)/shard_map/ppermute | solution.py:547
  67.4 23.1 %collective-permute-start.19 = (bf16[512,1024]{1,0:T(8,128)(2,1)}, bf16[512,1024]{1,0:T(8,128)(2,1)}, u32[]{:S(2)}, u32[]{:S(2)}) collective-permute-start(bf16[512,1024]{1,0:T(8,128)(2,1)} %get-tuple-element.629), channel_id=1, source_target_pairs={{0,1},{1,0},{2,3},{3,2},{4,5},{5,4},{6,7},{7,6},{8,9},{9,8},{10,11... | collective-permute-start | bytes 3145736 | tf_op jit(solution)/shard_map/ppermute | solution.py:553
  75.3 3.2 %collective-permute-start.16 = (bf16[512,512]{1,0:T(8,128)(2,1)}, bf16[512,512]{1,0:T(8,128)(2,1)}, u32[]{:S(2)}, u32[]{:S(2)}) collective-permute-start(bf16[512,512]{1,0:T(8,128)(2,1)} %get-tuple-element.665), channel_id=1, source_target_pairs={{0,1},{1,0},{2,3},{3,2},{4,5},{5,4},{6,7},{7,6},{8,9},{9,8},{10,11... | collective-permute-start | bytes 1572872 | tf_op jit(solution)/shard_map/ppermute | solution.py:553
  75.3 29.2 %collective-permute-start.22 = (bf16[512,1024]{1,0:T(8,128)(2,1)}, bf16[512,1024]{1,0:T(8,128)(2,1)}, u32[]{:S(2)}, u32[]{:S(2)}) collective-permute-start(bf16[512,1024]{1,0:T(8,128)(2,1)} %get-tuple-element.768), channel_id=1, source_target_pairs={{0,4},{5,1},{4,8},{9,5},{8,12},{13,9},{2,6},{7,3},{6,10},{11,7},{1... | collective-permute-start | bytes 3145736 | tf_op jit(solution)/shard_map/ppermute | solution.py:547
  90.5 6.0 %collective-permute-start.20 = (bf16[64,1024]{1,0:T(8,128)(2,1)S(1)}, bf16[64,1024]{1,0:T(8,128)(2,1)S(1)}, u32[]{:S(2)}, u32[]{:S(2)}) collective-permute-start(bf16[64,1024]{1,0:T(8,128)(2,1)S(1)} %get-tuple-element.738), channel_id=1, source_target_pairs={{0,2},{2,0},{1,3},{3,1},{4,6},{6,4},{5,7},{7,5},{8,10},{10,8},{9,1... | collective-permute-start | bytes 393224 | tf_op jit(solution)/shard_map/ppermute | solution.py:550
  96.5 8.0 %collective-permute-start.21 = (bf16[512,512]{1,0:T(8,128)(2,1)S(1)}, bf16[512,512]{1,0:T(8,128)(2,1)S(1)}, u32[]{:S(2)}, u32[]{:S(2)}) collective-permute-start(bf16[512,512]{1,0:T(8,128)(2,1)S(1)} %get-tuple-element.761), channel_id=1, source_target_pairs={{0,1},{1,0},{2,3},{3,2},{4,5},{5,4},{6,7},{7,6},{8,9},{9,8},{10,11... | collective-permute-start | bytes 1572872 | tf_op jit(solution)/shard_map/ppermute | solution.py:553
  96.5 25.9 %collective-permute-start.24 = (bf16[512,1024]{1,0:T(8,128)(2,1)}, bf16[512,1024]{1,0:T(8,128)(2,1)}, u32[]{:S(2)}, u32[]{:S(2)}) collective-permute-start(bf16[512,1024]{1,0:T(8,128)(2,1)} %get-tuple-element.828.a), channel_id=1, source_target_pairs={{0,2},{2,0},{1,3},{3,1},{4,6},{6,4},{5,7},{7,5},{8,10},{10,8},{9,1... | collective-permute-start | bytes 3145736 | tf_op jit(solution)/shard_map/ppermute | solution.py:550
  97.2 28.8 %collective-permute-start.25 = (bf16[512,1024]{1,0:T(8,128)(2,1)}, bf16[512,1024]{1,0:T(8,128)(2,1)}, u32[]{:S(2)}, u32[]{:S(2)}) collective-permute-start(bf16[512,1024]{1,0:T(8,128)(2,1)} %get-tuple-element.847), channel_id=1, source_target_pairs={{0,4},{5,1},{4,8},{9,5},{8,12},{13,9},{2,6},{7,3},{6,10},{11,7},{1... | collective-permute-start | bytes 3145736 | tf_op jit(solution)/shard_map/ppermute | solution.py:547
  100.4 25.6 %collective-permute-start.26 = (bf16[512,1024]{1,0:T(8,128)(2,1)}, bf16[512,1024]{1,0:T(8,128)(2,1)}, u32[]{:S(2)}, u32[]{:S(2)}) collective-permute-start(bf16[512,1024]{1,0:T(8,128)(2,1)} %get-tuple-element.758), channel_id=1, source_target_pairs={{0,1},{1,0},{2,3},{3,2},{4,5},{5,4},{6,7},{7,6},{8,9},{9,8},{10,11... | collective-permute-start | bytes 3145736 | tf_op jit(solution)/shard_map/ppermute | solution.py:553
  108.8 29.0 %collective-permute-start.27 = (bf16[512,1024]{1,0:T(8,128)(2,1)}, bf16[512,1024]{1,0:T(8,128)(2,1)}, u32[]{:S(2)}, u32[]{:S(2)}) collective-permute-start(bf16[512,1024]{1,0:T(8,128)(2,1)} %get-tuple-element.877), channel_id=1, source_target_pairs={{0,4},{5,1},{4,8},{9,5},{8,12},{13,9},{2,6},{7,3},{6,10},{11,7},{1... | collective-permute-start | bytes 3145736 | tf_op jit(solution)/shard_map/ppermute | solution.py:547
  112.7 2.0 %collective-permute-start.23 = (bf16[512,512]{1,0:T(8,128)(2,1)S(1)}, bf16[512,512]{1,0:T(8,128)(2,1)}, u32[]{:S(2)}, u32[]{:S(2)}) collective-permute-start(bf16[512,512]{1,0:T(8,128)(2,1)S(1)} %get-tuple-element.818), channel_id=1, source_target_pairs={{0,1},{1,0},{2,3},{3,2},{4,5},{5,4},{6,7},{7,6},{8,9},{9,8},{10,11... | collective-permute-start | bytes 1572872 | tf_op jit(solution)/shard_map/ppermute | solution.py:553
  122.4 24.9 %collective-permute-start.33 = (bf16[512,1024]{1,0:T(8,128)(2,1)S(1)}, bf16[512,1024]{1,0:T(8,128)(2,1)}, u32[]{:S(2)}, u32[]{:S(2)}) collective-permute-start(bf16[512,1024]{1,0:T(8,128)(2,1)S(1)} %shard_map.127.a), channel_id=1, source_target_pairs={{0,2},{2,0},{1,3},{3,1},{4,6},{6,4},{5,7},{7,5},{8,10},{10,8},{9,1... | collective-permute-start | bytes 3145736 | tf_op jit(solution)/shard_map/ppermute | solution.py:550
  137.8 3.2 %collective-permute-start.28 = (bf16[256,1024]{1,0:T(8,128)(2,1)S(1)}, bf16[256,1024]{1,0:T(8,128)(2,1)S(1)}, u32[]{:S(2)}, u32[]{:S(2)}) collective-permute-start(bf16[256,1024]{1,0:T(8,128)(2,1)S(1)} %get-tuple-element.888), channel_id=1, source_target_pairs={{0,1},{1,0},{2,3},{3,2},{4,5},{5,4},{6,7},{7,6},{8,9},{9,8},{10,11... | collective-permute-start | bytes 1572872 | tf_op jit(solution)/shard_map/ppermute | solution.py:553
  137.9 3.2 %collective-permute-start.29 = (bf16[256,1024]{1,0:T(8,128)(2,1)S(1)}, bf16[256,1024]{1,0:T(8,128)(2,1)S(1)}, u32[]{:S(2)}, u32[]{:S(2)}) collective-permute-start(bf16[256,1024]{1,0:T(8,128)(2,1)S(1)} %get-tuple-element.889), channel_id=1, source_target_pairs={{0,1},{1,0},{2,3},{3,2},{4,5},{5,4},{6,7},{7,6},{8,9},{9,8},{10,11... | collective-permute-start | bytes 1572872 | tf_op jit(solution)/shard_map/ppermute | solution.py:553
  138.4 2.5 %collective-permute-start.32 = (f32[64,1024]{1,0:T(8,128)S(1)}, f32[64,1024]{1,0:T(8,128)S(1)}, u32[]{:S(2)}, u32[]{:S(2)}) collective-permute-start(f32[64,1024]{1,0:T(8,128)S(1)} %convert_add_fusion.kept), channel_id=1, source_target_pairs={{0,1},{1,0},{2,3},{3,2},{4,5},{5,4},{6,7},{7,6},{8,9},{9,8},{10,11... | collective-permute-start | bytes 786440 | tf_op jit(solution)/shard_map/ppermute | solution.py:553
  147.2 3.3 %collective-permute-start.35 = (bf16[512,1024]{1,0:T(8,128)(2,1)}, bf16[512,1024]{1,0:T(8,128)(2,1)S(1)}, u32[]{:S(2)}, u32[]{:S(2)}) collective-permute-start(bf16[512,1024]{1,0:T(8,128)(2,1)} %get-tuple-element.907), channel_id=1, source_target_pairs={{0,1},{1,0},{2,3},{3,2},{4,5},{5,4},{6,7},{7,6},{8,9},{9,8},{10,11... | collective-permute-start | bytes 3145736 | tf_op jit(solution)/shard_map/ppermute | solution.py:553
  149.2 2.7 %collective-permute-start.34 = (bf16[512,1024]{1,0:T(8,128)(2,1)S(1)}, bf16[512,1024]{1,0:T(8,128)(2,1)S(1)}, u32[]{:S(2)}, u32[]{:S(2)}) collective-permute-start(bf16[512,1024]{1,0:T(8,128)(2,1)S(1)} %shard_map.132.value), channel_id=1, source_target_pairs={{0,1},{1,0},{2,3},{3,2},{4,5},{5,4},{6,7},{7,6},{8,9},{9,8},{10,11... | collective-permute-start | bytes 3145736 | tf_op jit(solution)/shard_map/ppermute | solution.py:553
  (22 other events, 154.9 us)

commit v6 on v5

--- a/solution.py
+++ b/solution.py
@@ -650,6 +650,7 @@
                 st["part", d] = lax.ppermute(st["part"], "tensor", pairs)
         if k == 3:
             st["x", 0] = swapped
+            st["came"] = other_core(st.pop("for_sibling"))
         if k == 6:
             st["maps_x"] = other_tenant(st["kept"].pop())
         fence()
@@ -672,8 +673,9 @@
             fence()
             if step != 2:
                 swapped = other_tenant(st["mix", step])
-            sum_of(step - 1)
-        elif 4 <= k < 2 * n:
+        elif k >= 4:
+            sum_of(step - 2)
+        if side == 0 and 4 <= k < 2 * n:
             wg_share = other_core(st["ours", step - 2])
         if k >= 6 and side == 0:
             place_of(step - 3, st.pop("theirs"))
@@ -685,7 +687,6 @@
                 [st.pop("part")] + [st.pop(("part", d)) for d in range(1, n)],
                 *[st[v] for v in names],
             )
-            st["came"] = other_core(st.pop("for_sibling"))
         if k == 4:
             st["term"] = term_of(st["z"][None], st["grads"], st["weight"])
         if k == 6:

time: 154 us -> 149 us (0.968)
  waiting for transfers between devices: 16.3 us -> 9.85 us
  local copies, waits for them, and re-layouts: 3.01 us -> 4.79 us
    ppermute x6, waiting for transfers between devices: 8.18 us -> 3.44 us  [other_tenant(): return lax.ppermute(value, 'tenant', swap)]
    unnamed x36, local copies, waits for them, and re-layouts: 0.91 us -> 2.69 us
    ppermute x19, waiting for transfers between devices: 8.13 us -> 6.39 us  [other_core(): return lax.ppermute(value, 'dp', swap)]
  transfers between devices with their start and end apart: 36 -> 36, of which waited for: 10 -> 9; matrix products, arithmetic and copies ran while one was open for 3% -> 4% of each run, Pallas kernels for 57% -> 59%
where the time goes in v6:
time: 149 us; the launch traced here: 148 us
  Pallas kernels  87.7 us (59%)
  starting transfers between devices  41.3 us (28%)
  waiting for transfers between devices  9.85 us (7%)
  local copies, waits for them, and re-layouts  4.79 us (3%)
  other arithmetic  3.1 us (2%)
    pallas_call x26, Pallas kernels, call(): pl.pallas_call(body, grid_spec=pltpu.PrefetchScalarGridSpec(num_scalar_pr...  87.7 us
    ppermute x8, starting transfers between devices, along(): return lax.ppermute(value, ('tensor', 'dp'), line_pairs)  28.2 us
    ppermute x6, starting transfers between devices, other_tenant(): return lax.ppermute(value, 'tenant', swap)  6.49 us
    ppermute x19, waiting for transfers between devices, other_core(): return lax.ppermute(value, 'dp', swap)  6.39 us
    ppermute x3, starting transfers between devices, shards_line(): st['part', d] = lax.ppermute(st['part'], 'tensor', pairs)  3.88 us
    ppermute x6, waiting for transfers between devices, other_tenant(): return lax.ppermute(value, 'tenant', swap)  3.44 us
  transfers between devices with their start and end apart: 36, of which 9 were waited for; matrix products, arithmetic and copies ran while one was open for 4% of the time, Pallas kernels for 59%

profile of v6, /device:TPU:0, one launch (start us, length us, event | category | flops | bytes accessed | tf_op | source)
XLA Modules:
  0.0 147.7 jit_solution(5165225271863464579)
XLA Ops:
  1.2 5.0 %collective-permute-start.4 = (bf16[512,1024]{1,0:T(8,128)(2,1)}, bf16[512,1024]{1,0:T(8,128)(2,1)S(1)}, u32[]{:S(2)}, u32[]{:S(2)}) collective-permute-start(bf16[512,1024]{1,0:T(8,128)(2,1)} %refs_0_.1), channel_id=1, source_target_pairs={{0,4},{5,1},{4,8},{9,5},{8,12},{13,9},{2,6},{7,3},{6,10},{11,7},{1... | collective-permute-start | bytes 3145736 | tf_op jit(solution)/shard_map/ppermute | solution.py:547
  11.1 3.1 %shard_map.110 = (bf16[512,1024]{1,0:T(8,128)(2,1)S(1)}, bf16[512,1024]{1,0:T(8,128)(2,1)S(1)}, s32[1,512]{1,0:T(1,128)S(1)}, f32[512,1]{1,0:T(8,128)}) custom-call(s32[19]{0:T(128)S(1)} %concatenate.4.table, bf16[512,1024]{1,0:T(8,128)(2,1)} %mine.1, bf16[512,1024]{1,0:T(8,128)(2,1)} %collective-permute-done.2.theirs), custom_call_target="tpu_custom_call" | custom-call | flops 1 | bytes 1 | tf_op jit(solution)/shard_map/pallas_call | solution.py:103
  14.2 4.4 %collective-permute-start.9 = (bf16[512,1024]{1,0:T(8,128)(2,1)}, bf16[512,1024]{1,0:T(8,128)(2,1)}, u32[]{:S(2)}, u32[]{:S(2)}) collective-permute-start(bf16[512,1024]{1,0:T(8,128)(2,1)} %collective-permute-done.refs_1_), channel_id=1, source_target_pairs={{0,4},{5,1},{4,8},{9,5},{8,12},{13,9},{2,6},{7,3},{6,10},{11,7},{1... | collective-permute-start | bytes 3145736 | tf_op jit(solution)/shard_map/ppermute | solution.py:547
  18.7 4.3 %shard_map.111.a = bf16[512,1024]{1,0:T(8,128)(2,1)} custom-call(s32[2]{0:T(128)S(1)} %pad_add_fusion.table, bf16[512,1024]{1,0:T(8,128)(2,1)} %refs_0_.1, bf16[512,1024]{1,0:T(8,128)(2,1)} %collective-permute-done.refs_1_, bf16[512,1024]{1,0:T(8,128)(2,1)S(1)} %get-tuple-element.804.refs_2_.grads.refs_6_.refs_4_.refs_8_, ...), custom_call_target="tpu_custom_call" | custom-call | flops 1 | bytes 1 | tf_op jit(solution)/shard_map/pallas_call | solution.py:103
  25.0 2.8 %shard_map.112 = (bf16[128,1024]{1,0:T(8,128)(2,1)}, bf16[128,1024]{1,0:T(8,128)(2,1)}, bf16[32,512]{1,0:T(8,128)(2,1)}) custom-call(s32[1]{0:T(128)} %bitcast.7.table, bf16[2,64,1024]{2,1,0:T(8,128)(2,1)S(1)} %pad_maximum_fusion.mine, bf16[64,1024]{1,0:T(8,128)(2,1)S(1)} %collective-permute-done.1.fetched, bf16[64,1024]{1,0:T(8,128)(2,1)} %collective-permute-done.3.shared, ...), custom_call_target="tpu_custom_call" | custom-call | flops 1 | bytes 1 | tf_op jit(solution)/shard_map/pallas_call | solution.py:103
  28.5 3.2 %collective-permute-start.7 = (bf16[32,512]{1,0:T(8,128)(2,1)}, bf16[32,512]{1,0:T(8,128)(2,1)S(1)}, u32[]{:S(2)}, u32[]{:S(2)}) collective-permute-start(bf16[32,512]{1,0:T(8,128)(2,1)} %get-tuple-element.520.refs_0_), channel_id=1, source_target_pairs={{0,12},{4,0},{8,4},{12,8},{1,13},{5,1},{9,5},{13,9},{2,14},{6,2},{... | collective-permute-start | bytes 98312 | tf_op jit(solution)/shard_map/ppermute | solution.py:650
  31.8 4.1 %shard_map.113 = (bf16[512,1024]{1,0:T(8,128)(2,1)}, bf16[512,512]{1,0:T(8,128)(2,1)S(1)}) custom-call(s32[3]{0:T(128)S(1)} %get-tuple-element.920.table, bf16[512,1024]{1,0:T(8,128)(2,1)S(1)} %get-tuple-element.804.refs_2_.grads.refs_6_.refs_4_.refs_8_, bf16[4096,1024]{1,0:T(8,128)(2,1)} %refs_25_, ...), custom_call_target="tpu_custom_call" | custom-call | flops 1 | bytes 1 | tf_op jit(solution)/shard_map/pallas_call | solution.py:103
  36.0 3.3 %collective-permute-start.13 = (bf16[512,1024]{1,0:T(8,128)(2,1)}, bf16[512,1024]{1,0:T(8,128)(2,1)}, u32[]{:S(2)}, u32[]{:S(2)}) collective-permute-start(bf16[512,1024]{1,0:T(8,128)(2,1)} %get-tuple-element.588), channel_id=1, source_target_pairs={{0,4},{5,1},{4,8},{9,5},{8,12},{13,9},{2,6},{7,3},{6,10},{11,7},{1... | collective-permute-start | bytes 3145736 | tf_op jit(solution)/shard_map/ppermute | solution.py:547
  39.3 2.9 %shard_map.114 = (bf16[128,512]{1,0:T(8,128)(2,1)}, bf16[128,512]{1,0:T(8,128)(2,1)}, f32[128,1024]{1,0:T(8,128)}, bf16[128,1024]{1,0:T(8,128)(2,1)}) custom-call(s32[1]{0:T(128)} %bitcast.7.table, bf16[32,512]{1,0:T(8,128)(2,1)S(1)} %copy-done.11, bf16[32,512]{1,0:T(8,128)(2,1)S(1)} %collective-permute-done.5.refs_1_, ...), custom_call_target="tpu_custom_call" | custom-call | flops 1 | bytes 1 | tf_op jit(solution)/shard_map/pallas_call | solution.py:103
  43.0 4.5 %shard_map.115 = (bf16[512,1024]{1,0:T(8,128)(2,1)}, bf16[512,512]{1,0:T(8,128)(2,1)}) custom-call(s32[3]{0:T(128)S(1)} %get-tuple-element.920.table, bf16[512,1024]{1,0:T(8,128)(2,1)S(1)} %get-tuple-element.805.refs_3_.grads.refs_5_.refs_9_, bf16[4096,1024]{1,0:T(8,128)(2,1)} %refs_25_, bf16[512,1024]{1,0:T(8,128)(2,1)} %collective-permute-done.9.came.refs_3_.refs_5_.refs_11_), custom_call_target="tpu_custom_call" | custom-call | flops 1 | bytes 1 | tf_op jit(solution)/shard_map/pallas_call | solution.py:103
  47.6 1.8 %collective-permute-start.15 = (bf16[512,1024]{1,0:T(8,128)(2,1)}, bf16[512,1024]{1,0:T(8,128)(2,1)S(1)}, u32[]{:S(2)}, u32[]{:S(2)}) collective-permute-start(bf16[512,1024]{1,0:T(8,128)(2,1)} %get-tuple-element.636), channel_id=1, source_target_pairs={{0,4},{5,1},{4,8},{9,5},{8,12},{13,9},{2,6},{7,3},{6,10},{11,7},{1... | collective-permute-start | bytes 3145736 | tf_op jit(solution)/shard_map/ppermute | solution.py:547
  49.8 4.3 %shard_map.116.a = bf16[512,1024]{1,0:T(8,128)(2,1)} custom-call(s32[2]{0:T(128)S(1)} %pad_add_fusion.1.table, bf16[512,512]{1,0:T(8,128)(2,1)} %collective-permute-done.12.refs_0_.refs_2_.refs_6_, bf16[512,1024]{1,0:T(8,128)(2,1)} %copy-done, bf16[512,512]{1,0:T(8,128)(2,1)} %copy-done.13, ...), custom_call_target="tpu_custom_call" | custom-call | flops 1 | bytes 1 | tf_op jit(solution)/shard_map/pallas_call | solution.py:103
  54.1 4.4 %shard_map.117 = (bf16[512,1024]{1,0:T(8,128)(2,1)S(1)}, bf16[512,512]{1,0:T(8,128)(2,1)}) custom-call(s32[3]{0:T(128)S(1)} %get-tuple-element.921.table, bf16[512,1024]{1,0:T(8,128)(2,1)S(1)} %get-tuple-element.804.refs_2_.grads.refs_6_.refs_4_.refs_8_, bf16[4096,1024]{1,0:T(8,128)(2,1)} %refs_25_, ...), custom_call_target="tpu_custom_call" | custom-call | flops 1 | bytes 1 | tf_op jit(solution)/shard_map/pallas_call | solution.py:103
  61.0 3.9 %collective-permute-start.18 = (bf16[512,1024]{1,0:T(8,128)(2,1)}, bf16[512,1024]{1,0:T(8,128)(2,1)}, u32[]{:S(2)}, u32[]{:S(2)}) collective-permute-start(bf16[512,1024]{1,0:T(8,128)(2,1)} %copy-done.12), channel_id=1, source_target_pairs={{0,4},{5,1},{4,8},{9,5},{8,12},{13,9},{2,6},{7,3},{6,10},{11,7},{1... | collective-permute-start | bytes 3145736 | tf_op jit(solution)/shard_map/ppermute | solution.py:547
  64.9 2.6 %shard_map.118 = (bf16[4096,1024]{1,0:T(8,128)(2,1)}, bf16[512,1024]{1,0:T(8,128)(2,1)}) custom-call(s32[1]{0:T(128)} %bitcast.14.table, bf16[512,1024]{1,0:T(8,128)(2,1)} %shard_map.111.a, bf16[512,1024]{1,0:T(8,128)(2,1)} %collective-permute-done.10.b), custom_call_target="tpu_custom_call" | custom-call | flops 1 | bytes 1 | tf_op jit(solution)/shard_map/pallas_call | solution.py:103
  67.5 3.6 %shard_map.119.term = bf16[512,1024]{1,0:T(8,128)(2,1)} custom-call(s32[1]{0:T(128)} %bitcast.15.table, bf16[512,1024]{1,0:T(8,128)(2,1)S(1)} %get-tuple-element.804.refs_2_.grads.refs_6_.refs_4_.refs_8_, bf16[4096,1024]{1,0:T(8,128)(2,1)} %refs_25_), custom_call_target="tpu_custom_call" | custom-call | flops 1 | bytes 1 | tf_op jit(solution)/shard_map/pallas_call | solution.py:103
  71.1 4.3 %shard_map.120 = (bf16[512,1024]{1,0:T(8,128)(2,1)}, bf16[512,512]{1,0:T(8,128)(2,1)}) custom-call(s32[3]{0:T(128)S(1)} %get-tuple-element.921.table, bf16[512,1024]{1,0:T(8,128)(2,1)S(1)} %get-tuple-element.805.refs_3_.grads.refs_5_.refs_9_, bf16[4096,1024]{1,0:T(8,128)(2,1)} %refs_25_, ...), custom_call_target="tpu_custom_call" | custom-call | flops 1 | bytes 1 | tf_op jit(solution)/shard_map/pallas_call | solution.py:103
  75.4 3.0 %collective-permute-start.22 = (bf16[512,1024]{1,0:T(8,128)(2,1)}, bf16[512,1024]{1,0:T(8,128)(2,1)}, u32[]{:S(2)}, u32[]{:S(2)}) collective-permute-start(bf16[512,1024]{1,0:T(8,128)(2,1)} %get-tuple-element.774), channel_id=1, source_target_pairs={{0,4},{5,1},{4,8},{9,5},{8,12},{13,9},{2,6},{7,3},{6,10},{11,7},{1... | collective-permute-start | bytes 3145736 | tf_op jit(solution)/shard_map/ppermute | solution.py:547
  78.5 5.2 %shard_map.121 = (bf16[512,1024]{1,0:T(8,128)(2,1)}, f32[64,1024]{1,0:T(8,128)}, bf16[64,1024]{1,0:T(8,128)(2,1)S(1)}) custom-call(s32[2]{0:T(128)S(1)} %pad_add_fusion.2.table, bf16[512,512]{1,0:T(8,128)(2,1)} %collective-permute-done.12.refs_0_.refs_2_.refs_6_, bf16[512,1024]{1,0:T(8,128)(2,1)} %copy-done, ...), custom_call_target="tpu_custom_call" | custom-call | flops 1 | bytes 1 | tf_op jit(solution)/shard_map/pallas_call | solution.py:103
  87.0 4.3 %shard_map.122 = (bf16[512,1024]{1,0:T(8,128)(2,1)}, bf16[512,512]{1,0:T(8,128)(2,1)S(1)}) custom-call(s32[3]{0:T(128)S(1)} %add_add_fusion.2.table, bf16[512,1024]{1,0:T(8,128)(2,1)S(1)} %get-tuple-element.804.refs_2_.grads.refs_6_.refs_4_.refs_8_, bf16[4096,1024]{1,0:T(8,128)(2,1)} %refs_25_, bf16[512,1024]{1,0:T(8,128)(2,1)} %collective-permute-done.18.came.refs_3_.refs_17_), custom_call_target="tpu_custom_call" | custom-call | flops 1 | bytes 1 | tf_op jit(solution)/shard_map/pallas_call | solution.py:103
  92.0 3.4 %collective-permute-start.25 = (bf16[512,1024]{1,0:T(8,128)(2,1)}, bf16[512,1024]{1,0:T(8,128)(2,1)}, u32[]{:S(2)}, u32[]{:S(2)}) collective-permute-start(bf16[512,1024]{1,0:T(8,128)(2,1)} %get-tuple-element.851), channel_id=1, source_target_pairs={{0,4},{5,1},{4,8},{9,5},{8,12},{13,9},{2,6},{7,3},{6,10},{11,7},{1... | collective-permute-start | bytes 3145736 | tf_op jit(solution)/shard_map/ppermute | solution.py:547
  95.5 2.6 %shard_map.123 = (bf16[4096,1024]{1,0:T(8,128)(2,1)}, bf16[512,1024]{1,0:T(8,128)(2,1)}) custom-call(s32[1]{0:T(128)} %bitcast.20.table, bf16[512,1024]{1,0:T(8,128)(2,1)} %shard_map.116.a, bf16[512,1024]{1,0:T(8,128)(2,1)} %collective-permute-done.17.b, bf16[4096,1024]{1,0:T(8,128)(2,1)} %get-tuple-element.758.refs_0_), custom_call_target="tpu_custom_call", output_to_operand_aliasing={{0}: (3, {})} | custom-call | flops 1 | bytes 1 | tf_op jit(solution)/shard_map/pallas_call | solution.py:103
  98.1 2.1 %shard_map.124.refs_0_ = bf16[4096,1024]{1,0:T(8,128)(2,1)} custom-call(s32[1]{0:T(128)} %bitcast.19.table, bf16[512,1024]{1,0:T(8,128)(2,1)} %collective-permute-done.19.value, bf16[4096,1024]{1,0:T(8,128)(2,1)} %get-tuple-element.759.refs_0_), custom_call_target="tpu_custom_call", output_to_operand_aliasing={{}: (2, {})} | custom-call | flops 1 | bytes 1 | tf_op jit(solution)/shard_map/pallas_call | solution.py:103
  100.3 1.9 %shard_map.125 = (bf16[512,1024]{1,0:T(8,128)(2,1)}, bf16[512,1024]{1,0:T(8,128)(2,1)}) custom-call(s32[1]{0:T(128)} %constant.35.clone.1.table, bf16[128,512]{1,0:T(8,128)(2,1)S(1)} %copy-done.9, bf16[128,1024]{1,0:T(8,128)(2,1)S(1)} %copy-done.8, bf16[128,512]{1,0:T(8,128)(2,1)S(1)} %copy-done.10, bf16[128,1024]{1,0:T(8,128)(2,1)S(1)} %copy-done.7), custom_call_target="tpu_custom_call" | custom-call | flops 1 | bytes 1 | tf_op jit(solution)/shard_map/pallas_call | solution.py:103
  102.2 4.3 %shard_map.126 = (bf16[512,1024]{1,0:T(8,128)(2,1)}, bf16[512,512]{1,0:T(8,128)(2,1)S(1)}) custom-call(s32[3]{0:T(128)S(1)} %add_add_fusion.2.table, bf16[512,1024]{1,0:T(8,128)(2,1)S(1)} %get-tuple-element.805.refs_3_.grads.refs_5_.refs_9_, bf16[4096,1024]{1,0:T(8,128)(2,1)} %refs_25_, bf16[512,1024]{1,0:T(8,128)(2,1)} %collective-permute-done.22.came.refs_7_.refs_21_), custom_call_target="tpu_custom_call" | custom-call | flops 1 | bytes 1 | tf_op jit(solution)/shard_map/pallas_call | solution.py:103
  106.4 3.5 %collective-permute-start.27 = (bf16[512,1024]{1,0:T(8,128)(2,1)}, bf16[512,1024]{1,0:T(8,128)(2,1)}, u32[]{:S(2)}, u32[]{:S(2)}) collective-permute-start(bf16[512,1024]{1,0:T(8,128)(2,1)} %get-tuple-element.884), channel_id=1, source_target_pairs={{0,4},{5,1},{4,8},{9,5},{8,12},{13,9},{2,6},{7,3},{6,10},{11,7},{1... | collective-permute-start | bytes 3145736 | tf_op jit(solution)/shard_map/ppermute | solution.py:547
  110.0 2.0 %collective-permute-done.23.refs_2_.refs_16_ = bf16[512,512]{1,0:T(8,128)(2,1)} collective-permute-done((bf16[512,512]{1,0:T(8,128)(2,1)S(1)}, bf16[512,512]{1,0:T(8,128)(2,1)}, u32[]{:S(2)}, u32[]{:S(2)}) %collective-permute-start.23) | collective-permute-done | bytes 524320 | tf_op jit(solution)/shard_map/ppermute | solution.py:553
  111.9 3.5 %shard_map.127.a = bf16[512,1024]{1,0:T(8,128)(2,1)S(1)} custom-call(s32[2]{0:T(128)S(1)} %pad_add_fusion.3.table, bf16[512,512]{1,0:T(8,128)(2,1)} %collective-permute-done.16.refs_2_.refs_0_.refs_8_.refs_14_, bf16[512,1024]{1,0:T(8,128)(2,1)} %collective-permute-done.13.came.refs_3_.refs_1_.refs_9_.refs_15_, ...), custom_call_target="tpu_custom_call" | custom-call | flops 1 | bytes 1 | tf_op jit(solution)/shard_map/pallas_call | solution.py:103
  118.0 2.8 %shard_map.128 = (bf16[4096,1024]{1,0:T(8,128)(2,1)}, bf16[512,1024]{1,0:T(8,128)(2,1)}) custom-call(s32[1]{0:T(128)} %bitcast.23.table, bf16[512,1024]{1,0:T(8,128)(2,1)} %get-tuple-element.863.a, bf16[512,1024]{1,0:T(8,128)(2,1)} %collective-permute-done.24.b, bf16[4096,1024]{1,0:T(8,128)(2,1)} %shard_map.124.refs_0_), custom_call_target="tpu_custom_call", output_to_operand_aliasing={{0}: (3, {})} | custom-call | flops 1 | bytes 1 | tf_op jit(solution)/shard_map/pallas_call | solution.py:103
  120.8 2.2 %shard_map.129.refs_0_ = bf16[4096,1024]{1,0:T(8,128)(2,1)} custom-call(s32[1]{0:T(128)} %bitcast.22.table, bf16[512,1024]{1,0:T(8,128)(2,1)} %collective-permute-done.26.value, bf16[4096,1024]{1,0:T(8,128)(2,1)} %get-tuple-element.866.refs_0_), custom_call_target="tpu_custom_call", output_to_operand_aliasing={{}: (2, {})} | custom-call | flops 1 | bytes 1 | tf_op jit(solution)/shard_map/pallas_call | solution.py:103
  123.9 8.7 %shard_map.130 = (f32[512,1024]{1,0:T(8,128)}, bf16[256,1024]{1,0:T(8,128)(2,1)S(1)}, bf16[256,1024]{1,0:T(8,128)(2,1)S(1)}) custom-call(s32[9]{0:T(128)S(1)} %stack.148.table, bf16[512,1024]{1,0:T(8,128)(2,1)} %refs_0_.1, bf16[512,1024]{1,0:T(8,128)(2,1)} %collective-permute-done.refs_1_, bf16[512,512]{1,0:T(8,128)(2,1)} %collective-permute-done.12.refs_0_.refs_2_.refs_6_, ...), custom_call_target="tpu_custom_call" | custom-call | flops 1 | bytes 1 | tf_op jit(solution)/shard_map/pallas_call | solution.py:103
  137.7 4.4 %shard_map.131 = (bf16[512,1024]{1,0:T(8,128)(2,1)}, bf16[512,1024]{1,0:T(8,128)(2,1)}, f32[64,1024]{1,0:T(8,128)}, f32[64,1024]{1,0:T(8,128)}) custom-call(s32[1]{0:T(128)} %bitcast.7.table, f32[512,1024]{1,0:T(8,128)} %get-tuple-element.890.here, f32[512,1]{1,0:T(8,128)S(1)} %copy-done.6, bf16[512,1024]{1,0:T(8,128)(2,1)S(1)} %copy-done.4, ...), custom_call_target="tpu_custom_call" | custom-call | flops 1 | bytes 1 | tf_op jit(solution)/shard_map/pallas_call | solution.py:103
  (115 shorter events, 30.4 us)
Async XLA Ops:
  0.6 10.4 %collective-permute-start.2 = (bf16[512,1024]{1,0:T(8,128)(2,1)}, bf16[512,1024]{1,0:T(8,128)(2,1)}, u32[]{:S(2)}, u32[]{:S(2)}) collective-permute-start(bf16[512,1024]{1,0:T(8,128)(2,1)} %mine.1), channel_id=1, source_target_pairs={{0,1},{1,0},{2,3},{3,2},{4,5},{5,4},{6,7},{7,6},{8,9},{9,8},{10,11... | collective-permute-start | bytes 3145736 | tf_op jit(solution)/shard_map/ppermute | solution.py:553
  1.1 13.1 %collective-permute-start = (bf16[512,1024]{1,0:T(8,128)(2,1)}, bf16[512,1024]{1,0:T(8,128)(2,1)}, u32[]{:S(2)}, u32[]{:S(2)}) collective-permute-start(bf16[512,1024]{1,0:T(8,128)(2,1)} %refs_0_.1), channel_id=1, source_target_pairs={{0,1},{1,0},{2,3},{3,2},{4,5},{5,4},{6,7},{7,6},{8,9},{9,8},{10,11... | collective-permute-start | bytes 3145736 | tf_op jit(solution)/shard_map/ppermute | solution.py:553
  1.2 26.6 %collective-permute-start.4 = (bf16[512,1024]{1,0:T(8,128)(2,1)}, bf16[512,1024]{1,0:T(8,128)(2,1)S(1)}, u32[]{:S(2)}, u32[]{:S(2)}) collective-permute-start(bf16[512,1024]{1,0:T(8,128)(2,1)} %refs_0_.1), channel_id=1, source_target_pairs={{0,4},{5,1},{4,8},{9,5},{8,12},{13,9},{2,6},{7,3},{6,10},{11,7},{1... | collective-permute-start | bytes 3145736 | tf_op jit(solution)/shard_map/ppermute | solution.py:547
  7.8 6.4 %collective-permute-start.1 = (bf16[64,1024]{1,0:T(8,128)(2,1)}, bf16[64,1024]{1,0:T(8,128)(2,1)S(1)}, u32[]{:S(2)}, u32[]{:S(2)}) collective-permute-start(bf16[64,1024]{1,0:T(8,128)(2,1)} %fusion.1), channel_id=1, source_target_pairs={{0,2},{2,0},{1,3},{3,1},{4,6},{6,4},{5,7},{7,5},{8,10},{10,8},{9,1... | collective-permute-start | bytes 393224 | tf_op jit(solution)/shard_map/ppermute | solution.py:550
  14.2 28.0 %collective-permute-start.9 = (bf16[512,1024]{1,0:T(8,128)(2,1)}, bf16[512,1024]{1,0:T(8,128)(2,1)}, u32[]{:S(2)}, u32[]{:S(2)}) collective-permute-start(bf16[512,1024]{1,0:T(8,128)(2,1)} %collective-permute-done.refs_1_), channel_id=1, source_target_pairs={{0,4},{5,1},{4,8},{9,5},{8,12},{13,9},{2,6},{7,3},{6,10},{11,7},{1... | collective-permute-start | bytes 3145736 | tf_op jit(solution)/shard_map/ppermute | solution.py:547
  23.0 24.5 %collective-permute-start.10 = (bf16[512,1024]{1,0:T(8,128)(2,1)}, bf16[512,1024]{1,0:T(8,128)(2,1)}, u32[]{:S(2)}, u32[]{:S(2)}) collective-permute-start(bf16[512,1024]{1,0:T(8,128)(2,1)} %shard_map.111.a), channel_id=1, source_target_pairs={{0,2},{2,0},{1,3},{3,1},{4,6},{6,4},{5,7},{7,5},{8,10},{10,8},{9,1... | collective-permute-start | bytes 3145736 | tf_op jit(solution)/shard_map/ppermute | solution.py:550
  27.8 8.1 %collective-permute-start.5 = (bf16[32,512]{1,0:T(8,128)(2,1)}, bf16[32,512]{1,0:T(8,128)(2,1)S(1)}, u32[]{:S(2)}, u32[]{:S(2)}) collective-permute-start(bf16[32,512]{1,0:T(8,128)(2,1)} %get-tuple-element.520.refs_0_), channel_id=1, source_target_pairs={{0,4},{4,8},{8,12},{12,0},{1,5},{5,9},{9,13},{13,1},{2,6},{6,10},{... | collective-permute-start | bytes 98312 | tf_op jit(solution)/shard_map/ppermute | solution.py:650
  28.5 7.4 %collective-permute-start.6 = (bf16[32,512]{1,0:T(8,128)(2,1)}, bf16[32,512]{1,0:T(8,128)(2,1)S(1)}, u32[]{:S(2)}, u32[]{:S(2)}) collective-permute-start(bf16[32,512]{1,0:T(8,128)(2,1)} %get-tuple-element.520.refs_0_), channel_id=1, source_target_pairs={{0,8},{4,12},{8,0},{12,4},{1,9},{5,13},{9,1},{13,5},{2,10},{6,14},... | collective-permute-start | bytes 98312 | tf_op jit(solution)/shard_map/ppermute | solution.py:650
  28.5 7.4 %collective-permute-start.7 = (bf16[32,512]{1,0:T(8,128)(2,1)}, bf16[32,512]{1,0:T(8,128)(2,1)S(1)}, u32[]{:S(2)}, u32[]{:S(2)}) collective-permute-start(bf16[32,512]{1,0:T(8,128)(2,1)} %get-tuple-element.520.refs_0_), channel_id=1, source_target_pairs={{0,12},{4,0},{8,4},{12,8},{1,13},{5,1},{9,5},{13,9},{2,14},{6,2},{... | collective-permute-start | bytes 98312 | tf_op jit(solution)/shard_map/ppermute | solution.py:650
  35.9 6.3 %collective-permute-start.8 = (bf16[512,512]{1,0:T(8,128)(2,1)S(1)}, bf16[512,512]{1,0:T(8,128)(2,1)S(1)}, u32[]{:S(2)}, u32[]{:S(2)}) collective-permute-start(bf16[512,512]{1,0:T(8,128)(2,1)S(1)} %get-tuple-element.519), channel_id=1, source_target_pairs={{0,1},{1,0},{2,3},{3,2},{4,5},{5,4},{6,7},{7,6},{8,9},{9,8},{10,11... | collective-permute-start | bytes 1572872 | tf_op jit(solution)/shard_map/ppermute | solution.py:553
  36.0 18.1 %collective-permute-start.13 = (bf16[512,1024]{1,0:T(8,128)(2,1)}, bf16[512,1024]{1,0:T(8,128)(2,1)}, u32[]{:S(2)}, u32[]{:S(2)}) collective-permute-start(bf16[512,1024]{1,0:T(8,128)(2,1)} %get-tuple-element.588), channel_id=1, source_target_pairs={{0,4},{5,1},{4,8},{9,5},{8,12},{13,9},{2,6},{7,3},{6,10},{11,7},{1... | collective-permute-start | bytes 3145736 | tf_op jit(solution)/shard_map/ppermute | solution.py:547
  43.0 4.5 %collective-permute-start.11 = (bf16[128,1024]{1,0:T(8,128)(2,1)}, bf16[128,1024]{1,0:T(8,128)(2,1)S(1)}, u32[]{:S(2)}, u32[]{:S(2)}) collective-permute-start(bf16[128,1024]{1,0:T(8,128)(2,1)} %get-tuple-element.547), channel_id=1, source_target_pairs={{0,1},{1,0},{2,3},{3,2},{4,5},{5,4},{6,7},{7,6},{8,9},{9,8},{10,11... | collective-permute-start | bytes 786440 | tf_op jit(solution)/shard_map/ppermute | solution.py:553
  47.5 2.3 %collective-permute-start.12 = (bf16[512,512]{1,0:T(8,128)(2,1)}, bf16[512,512]{1,0:T(8,128)(2,1)}, u32[]{:S(2)}, u32[]{:S(2)}) collective-permute-start(bf16[512,512]{1,0:T(8,128)(2,1)} %get-tuple-element.567), channel_id=1, source_target_pairs={{0,1},{1,0},{2,3},{3,2},{4,5},{5,4},{6,7},{7,6},{8,9},{9,8},{10,11... | collective-permute-start | bytes 1572872 | tf_op jit(solution)/shard_map/ppermute | solution.py:553
  47.6 23.5 %collective-permute-start.15 = (bf16[512,1024]{1,0:T(8,128)(2,1)}, bf16[512,1024]{1,0:T(8,128)(2,1)S(1)}, u32[]{:S(2)}, u32[]{:S(2)}) collective-permute-start(bf16[512,1024]{1,0:T(8,128)(2,1)} %get-tuple-element.636), channel_id=1, source_target_pairs={{0,4},{5,1},{4,8},{9,5},{8,12},{13,9},{2,6},{7,3},{6,10},{11,7},{1... | collective-permute-start | bytes 3145736 | tf_op jit(solution)/shard_map/ppermute | solution.py:547
  59.5 11.6 %collective-permute-start.14 = (bf16[512,512]{1,0:T(8,128)(2,1)}, bf16[512,512]{1,0:T(8,128)(2,1)}, u32[]{:S(2)}, u32[]{:S(2)}) collective-permute-start(bf16[512,512]{1,0:T(8,128)(2,1)} %get-tuple-element.631), channel_id=1, source_target_pairs={{0,1},{1,0},{2,3},{3,2},{4,5},{5,4},{6,7},{7,6},{8,9},{9,8},{10,11... | collective-permute-start | bytes 1572872 | tf_op jit(solution)/shard_map/ppermute | solution.py:553
  59.5 25.9 %collective-permute-start.17 = (bf16[512,1024]{1,0:T(8,128)(2,1)}, bf16[512,1024]{1,0:T(8,128)(2,1)}, u32[]{:S(2)}, u32[]{:S(2)}) collective-permute-start(bf16[512,1024]{1,0:T(8,128)(2,1)} %shard_map.116.a), channel_id=1, source_target_pairs={{0,2},{2,0},{1,3},{3,1},{4,6},{6,4},{5,7},{7,5},{8,10},{10,8},{9,1... | collective-permute-start | bytes 3145736 | tf_op jit(solution)/shard_map/ppermute | solution.py:550
  61.0 24.4 %collective-permute-start.18 = (bf16[512,1024]{1,0:T(8,128)(2,1)}, bf16[512,1024]{1,0:T(8,128)(2,1)}, u32[]{:S(2)}, u32[]{:S(2)}) collective-permute-start(bf16[512,1024]{1,0:T(8,128)(2,1)} %copy-done.12), channel_id=1, source_target_pairs={{0,4},{5,1},{4,8},{9,5},{8,12},{13,9},{2,6},{7,3},{6,10},{11,7},{1... | collective-permute-start | bytes 3145736 | tf_op jit(solution)/shard_map/ppermute | solution.py:547
  67.5 17.9 %collective-permute-start.19 = (bf16[512,1024]{1,0:T(8,128)(2,1)}, bf16[512,1024]{1,0:T(8,128)(2,1)}, u32[]{:S(2)}, u32[]{:S(2)}) collective-permute-start(bf16[512,1024]{1,0:T(8,128)(2,1)} %get-tuple-element.635), channel_id=1, source_target_pairs={{0,1},{1,0},{2,3},{3,2},{4,5},{5,4},{6,7},{7,6},{8,9},{9,8},{10,11... | collective-permute-start | bytes 3145736 | tf_op jit(solution)/shard_map/ppermute | solution.py:553
  75.4 3.1 %collective-permute-start.16 = (bf16[512,512]{1,0:T(8,128)(2,1)}, bf16[512,512]{1,0:T(8,128)(2,1)}, u32[]{:S(2)}, u32[]{:S(2)}) collective-permute-start(bf16[512,512]{1,0:T(8,128)(2,1)} %get-tuple-element.669), channel_id=1, source_target_pairs={{0,1},{1,0},{2,3},{3,2},{4,5},{5,4},{6,7},{7,6},{8,9},{9,8},{10,11... | collective-permute-start | bytes 1572872 | tf_op jit(solution)/shard_map/ppermute | solution.py:553
  75.4 26.7 %collective-permute-start.22 = (bf16[512,1024]{1,0:T(8,128)(2,1)}, bf16[512,1024]{1,0:T(8,128)(2,1)}, u32[]{:S(2)}, u32[]{:S(2)}) collective-permute-start(bf16[512,1024]{1,0:T(8,128)(2,1)} %get-tuple-element.774), channel_id=1, source_target_pairs={{0,4},{5,1},{4,8},{9,5},{8,12},{13,9},{2,6},{7,3},{6,10},{11,7},{1... | collective-permute-start | bytes 3145736 | tf_op jit(solution)/shard_map/ppermute | solution.py:547
  85.4 5.9 %collective-permute-start.20 = (bf16[64,1024]{1,0:T(8,128)(2,1)S(1)}, bf16[64,1024]{1,0:T(8,128)(2,1)S(1)}, u32[]{:S(2)}, u32[]{:S(2)}) collective-permute-start(bf16[64,1024]{1,0:T(8,128)(2,1)S(1)} %get-tuple-element.741), channel_id=1, source_target_pairs={{0,2},{2,0},{1,3},{3,1},{4,6},{6,4},{5,7},{7,5},{8,10},{10,8},{9,1... | collective-permute-start | bytes 393224 | tf_op jit(solution)/shard_map/ppermute | solution.py:550
  91.3 10.8 %collective-permute-start.21 = (bf16[512,512]{1,0:T(8,128)(2,1)S(1)}, bf16[512,512]{1,0:T(8,128)(2,1)S(1)}, u32[]{:S(2)}, u32[]{:S(2)}) collective-permute-start(bf16[512,512]{1,0:T(8,128)(2,1)S(1)} %get-tuple-element.766), channel_id=1, source_target_pairs={{0,1},{1,0},{2,3},{3,2},{4,5},{5,4},{6,7},{7,6},{8,9},{9,8},{10,11... | collective-permute-start | bytes 1572872 | tf_op jit(solution)/shard_map/ppermute | solution.py:553
  91.3 25.9 %collective-permute-start.24 = (bf16[512,1024]{1,0:T(8,128)(2,1)}, bf16[512,1024]{1,0:T(8,128)(2,1)}, u32[]{:S(2)}, u32[]{:S(2)}) collective-permute-start(bf16[512,1024]{1,0:T(8,128)(2,1)} %get-tuple-element.863.a), channel_id=1, source_target_pairs={{0,2},{2,0},{1,3},{3,1},{4,6},{6,4},{5,7},{7,5},{8,10},{10,8},{9,1... | collective-permute-start | bytes 3145736 | tf_op jit(solution)/shard_map/ppermute | solution.py:550
  92.0 26.0 %collective-permute-start.25 = (bf16[512,1024]{1,0:T(8,128)(2,1)}, bf16[512,1024]{1,0:T(8,128)(2,1)}, u32[]{:S(2)}, u32[]{:S(2)}) collective-permute-start(bf16[512,1024]{1,0:T(8,128)(2,1)} %get-tuple-element.851), channel_id=1, source_target_pairs={{0,4},{5,1},{4,8},{9,5},{8,12},{13,9},{2,6},{7,3},{6,10},{11,7},{1... | collective-permute-start | bytes 3145736 | tf_op jit(solution)/shard_map/ppermute | solution.py:547
  98.1 19.9 %collective-permute-start.26 = (bf16[512,1024]{1,0:T(8,128)(2,1)}, bf16[512,1024]{1,0:T(8,128)(2,1)}, u32[]{:S(2)}, u32[]{:S(2)}) collective-permute-start(bf16[512,1024]{1,0:T(8,128)(2,1)} %get-tuple-element.767), channel_id=1, source_target_pairs={{0,1},{1,0},{2,3},{3,2},{4,5},{5,4},{6,7},{7,6},{8,9},{9,8},{10,11... | collective-permute-start | bytes 3145736 | tf_op jit(solution)/shard_map/ppermute | solution.py:553
  106.4 26.2 %collective-permute-start.27 = (bf16[512,1024]{1,0:T(8,128)(2,1)}, bf16[512,1024]{1,0:T(8,128)(2,1)}, u32[]{:S(2)}, u32[]{:S(2)}) collective-permute-start(bf16[512,1024]{1,0:T(8,128)(2,1)} %get-tuple-element.884), channel_id=1, source_target_pairs={{0,4},{5,1},{4,8},{9,5},{8,12},{13,9},{2,6},{7,3},{6,10},{11,7},{1... | collective-permute-start | bytes 3145736 | tf_op jit(solution)/shard_map/ppermute | solution.py:547
  117.2 24.8 %collective-permute-start.33 = (bf16[512,1024]{1,0:T(8,128)(2,1)S(1)}, bf16[512,1024]{1,0:T(8,128)(2,1)}, u32[]{:S(2)}, u32[]{:S(2)}) collective-permute-start(bf16[512,1024]{1,0:T(8,128)(2,1)S(1)} %shard_map.127.a), channel_id=1, source_target_pairs={{0,2},{2,0},{1,3},{3,1},{4,6},{6,4},{5,7},{7,5},{8,10},{10,8},{9,1... | collective-permute-start | bytes 3145736 | tf_op jit(solution)/shard_map/ppermute | solution.py:550
  132.6 3.2 %collective-permute-start.28 = (bf16[256,1024]{1,0:T(8,128)(2,1)S(1)}, bf16[256,1024]{1,0:T(8,128)(2,1)S(1)}, u32[]{:S(2)}, u32[]{:S(2)}) collective-permute-start(bf16[256,1024]{1,0:T(8,128)(2,1)S(1)} %get-tuple-element.895), channel_id=1, source_target_pairs={{0,1},{1,0},{2,3},{3,2},{4,5},{5,4},{6,7},{7,6},{8,9},{9,8},{10,11... | collective-permute-start | bytes 1572872 | tf_op jit(solution)/shard_map/ppermute | solution.py:553
  132.7 3.2 %collective-permute-start.29 = (bf16[256,1024]{1,0:T(8,128)(2,1)S(1)}, bf16[256,1024]{1,0:T(8,128)(2,1)S(1)}, u32[]{:S(2)}, u32[]{:S(2)}) collective-permute-start(bf16[256,1024]{1,0:T(8,128)(2,1)S(1)} %get-tuple-element.896), channel_id=1, source_target_pairs={{0,1},{1,0},{2,3},{3,2},{4,5},{5,4},{6,7},{7,6},{8,9},{9,8},{10,11... | collective-permute-start | bytes 1572872 | tf_op jit(solution)/shard_map/ppermute | solution.py:553
  133.3 2.5 %collective-permute-start.32 = (f32[64,1024]{1,0:T(8,128)S(1)}, f32[64,1024]{1,0:T(8,128)S(1)}, u32[]{:S(2)}, u32[]{:S(2)}) collective-permute-start(f32[64,1024]{1,0:T(8,128)S(1)} %convert_add_fusion.kept), channel_id=1, source_target_pairs={{0,1},{1,0},{2,3},{3,2},{4,5},{5,4},{6,7},{7,6},{8,9},{9,8},{10,11... | collective-permute-start | bytes 786440 | tf_op jit(solution)/shard_map/ppermute | solution.py:553
  142.1 3.3 %collective-permute-start.35 = (bf16[512,1024]{1,0:T(8,128)(2,1)}, bf16[512,1024]{1,0:T(8,128)(2,1)S(1)}, u32[]{:S(2)}, u32[]{:S(2)}) collective-permute-start(bf16[512,1024]{1,0:T(8,128)(2,1)} %get-tuple-element.914), channel_id=1, source_target_pairs={{0,1},{1,0},{2,3},{3,2},{4,5},{5,4},{6,7},{7,6},{8,9},{9,8},{10,11... | collective-permute-start | bytes 3145736 | tf_op jit(solution)/shard_map/ppermute | solution.py:553
  144.0 2.7 %collective-permute-start.34 = (bf16[512,1024]{1,0:T(8,128)(2,1)S(1)}, bf16[512,1024]{1,0:T(8,128)(2,1)S(1)}, u32[]{:S(2)}, u32[]{:S(2)}) collective-permute-start(bf16[512,1024]{1,0:T(8,128)(2,1)S(1)} %shard_map.132.value), channel_id=1, source_target_pairs={{0,1},{1,0},{2,3},{3,2},{4,5},{5,4},{6,7},{7,6},{8,9},{9,8},{10,11... | collective-permute-start | bytes 3145736 | tf_op jit(solution)/shard_map/ppermute | solution.py:553
  (22 other events, 144.2 us)

commit v7 on v6

--- a/solution.py
+++ b/solution.py
@@ -206,7 +206,7 @@
     split = extra[0].shape[0] // 2 if extra else 0
     outs = [jax.ShapeDtypeStruct((half, width), B16)]
     if extra:
-        outs.append(kept_in_hbm(jax.ShapeDtypeStruct((split, width), F32)))
+        outs.append(jax.ShapeDtypeStruct((split, width), F32))
         outs.append(jax.ShapeDtypeStruct((split, width), B16))
     return call(
         functools.partial(piece_body, len(ours), 1 if extra else 0),
@@ -220,7 +220,7 @@
         [cols(v.shape[0]) for v in outs],
         [pltpu.VMEM((rows, half), B16)] * 2 + [pltpu.SemaphoreType.DMA((2,))],
         0,
-        pinned=[*range(2 * len(ours))] + [2 * len(ours) + 2] * (1 if extra else 0),
+        pinned=range(2 * len(ours)),
     )
 
 

time: 149 us -> 148 us (level)
    unnamed x36 -> x40, local copies, waits for them, and re-layouts: 2.69 us -> 3.65 us
  transfers between devices with their start and end apart: 36 -> 36, of which waited for: 9 -> 9; matrix products, arithmetic and copies ran while one was open for 4% -> 4% of each run, Pallas kernels for 59% -> 58%
where the time goes in v7:
time: 148 us; the launch traced here: 147 us
  Pallas kernels  86.9 us (59%)
  starting transfers between devices  41.5 us (28%)
  waiting for transfers between devices  8.73 us (6%)
  local copies, waits for them, and re-layouts  5.75 us (4%)
  other arithmetic  3.1 us (2%)
    pallas_call x26, Pallas kernels, call(): pl.pallas_call(body, grid_spec=pltpu.PrefetchScalarGridSpec(num_scalar_pr...  86.9 us
    ppermute x8, starting transfers between devices, along(): return lax.ppermute(value, ('tensor', 'dp'), line_pairs)  28.3 us
    ppermute x6, starting transfers between devices, other_tenant(): return lax.ppermute(value, 'tenant', swap)  6.53 us
    ppermute x19, waiting for transfers between devices, other_core(): return lax.ppermute(value, 'dp', swap)  6.4 us
    ppermute x3, starting transfers between devices, shards_line(): st['part', d] = lax.ppermute(st['part'], 'tensor', pairs)  3.88 us
    unnamed x40, local copies, waits for them, and re-layouts  3.65 us
  transfers between devices with their start and end apart: 36, of which 9 were waited for; matrix products, arithmetic and copies ran while one was open for 4% of the time, Pallas kernels for 58%

profile of v7, /device:TPU:0, one launch (start us, length us, event | category | flops | bytes accessed | tf_op | source)
XLA Modules:
  0.0 147.0 jit_solution(8440793164582127146)
XLA Ops:
  1.2 5.0 %collective-permute-start.4 = (bf16[512,1024]{1,0:T(8,128)(2,1)}, bf16[512,1024]{1,0:T(8,128)(2,1)S(1)}, u32[]{:S(2)}, u32[]{:S(2)}) collective-permute-start(bf16[512,1024]{1,0:T(8,128)(2,1)} %refs_0_.1), channel_id=1, source_target_pairs={{0,4},{5,1},{4,8},{9,5},{8,12},{13,9},{2,6},{7,3},{6,10},{11,7},{1... | collective-permute-start | bytes 3145736 | tf_op jit(solution)/shard_map/ppermute | solution.py:547
  11.1 3.1 %shard_map.110 = (bf16[512,1024]{1,0:T(8,128)(2,1)S(1)}, bf16[512,1024]{1,0:T(8,128)(2,1)S(1)}, s32[1,512]{1,0:T(1,128)S(1)}, f32[512,1]{1,0:T(8,128)}) custom-call(s32[19]{0:T(128)S(1)} %concatenate.4.table, bf16[512,1024]{1,0:T(8,128)(2,1)} %mine.1, bf16[512,1024]{1,0:T(8,128)(2,1)} %collective-permute-done.2.theirs), custom_call_target="tpu_custom_call" | custom-call | flops 1 | bytes 1 | tf_op jit(solution)/shard_map/pallas_call | solution.py:103
  14.2 4.4 %collective-permute-start.9 = (bf16[512,1024]{1,0:T(8,128)(2,1)}, bf16[512,1024]{1,0:T(8,128)(2,1)}, u32[]{:S(2)}, u32[]{:S(2)}) collective-permute-start(bf16[512,1024]{1,0:T(8,128)(2,1)} %collective-permute-done.refs_1_), channel_id=1, source_target_pairs={{0,4},{5,1},{4,8},{9,5},{8,12},{13,9},{2,6},{7,3},{6,10},{11,7},{1... | collective-permute-start | bytes 3145736 | tf_op jit(solution)/shard_map/ppermute | solution.py:547
  18.7 4.3 %shard_map.111.a = bf16[512,1024]{1,0:T(8,128)(2,1)} custom-call(s32[2]{0:T(128)S(1)} %pad_add_fusion.table, bf16[512,1024]{1,0:T(8,128)(2,1)} %refs_0_.1, bf16[512,1024]{1,0:T(8,128)(2,1)} %collective-permute-done.refs_1_, bf16[512,1024]{1,0:T(8,128)(2,1)S(1)} %get-tuple-element.804.refs_2_.grads.refs_6_.refs_4_.refs_8_, ...), custom_call_target="tpu_custom_call" | custom-call | flops 1 | bytes 1 | tf_op jit(solution)/shard_map/pallas_call | solution.py:103
  25.0 2.8 %shard_map.112 = (bf16[128,1024]{1,0:T(8,128)(2,1)}, bf16[128,1024]{1,0:T(8,128)(2,1)}, bf16[32,512]{1,0:T(8,128)(2,1)}) custom-call(s32[1]{0:T(128)} %bitcast.7.table, bf16[2,64,1024]{2,1,0:T(8,128)(2,1)S(1)} %pad_maximum_fusion.mine, bf16[64,1024]{1,0:T(8,128)(2,1)S(1)} %collective-permute-done.1.fetched, bf16[64,1024]{1,0:T(8,128)(2,1)} %collective-permute-done.3.shared, ...), custom_call_target="tpu_custom_call" | custom-call | flops 1 | bytes 1 | tf_op jit(solution)/shard_map/pallas_call | solution.py:103
  28.5 3.2 %collective-permute-start.7 = (bf16[32,512]{1,0:T(8,128)(2,1)}, bf16[32,512]{1,0:T(8,128)(2,1)S(1)}, u32[]{:S(2)}, u32[]{:S(2)}) collective-permute-start(bf16[32,512]{1,0:T(8,128)(2,1)} %get-tuple-element.520.refs_0_), channel_id=1, source_target_pairs={{0,12},{4,0},{8,4},{12,8},{1,13},{5,1},{9,5},{13,9},{2,14},{6,2},{... | collective-permute-start | bytes 98312 | tf_op jit(solution)/shard_map/ppermute | solution.py:650
  31.8 4.1 %shard_map.113 = (bf16[512,1024]{1,0:T(8,128)(2,1)}, bf16[512,512]{1,0:T(8,128)(2,1)S(1)}) custom-call(s32[3]{0:T(128)S(1)} %get-tuple-element.920.table, bf16[512,1024]{1,0:T(8,128)(2,1)S(1)} %get-tuple-element.804.refs_2_.grads.refs_6_.refs_4_.refs_8_, bf16[4096,1024]{1,0:T(8,128)(2,1)} %refs_25_, ...), custom_call_target="tpu_custom_call" | custom-call | flops 1 | bytes 1 | tf_op jit(solution)/shard_map/pallas_call | solution.py:103
  36.0 3.3 %collective-permute-start.13 = (bf16[512,1024]{1,0:T(8,128)(2,1)}, bf16[512,1024]{1,0:T(8,128)(2,1)}, u32[]{:S(2)}, u32[]{:S(2)}) collective-permute-start(bf16[512,1024]{1,0:T(8,128)(2,1)} %get-tuple-element.588), channel_id=1, source_target_pairs={{0,4},{5,1},{4,8},{9,5},{8,12},{13,9},{2,6},{7,3},{6,10},{11,7},{1... | collective-permute-start | bytes 3145736 | tf_op jit(solution)/shard_map/ppermute | solution.py:547
  39.3 3.0 %shard_map.114 = (bf16[128,512]{1,0:T(8,128)(2,1)}, bf16[128,512]{1,0:T(8,128)(2,1)}, f32[128,1024]{1,0:T(8,128)}, bf16[128,1024]{1,0:T(8,128)(2,1)}) custom-call(s32[1]{0:T(128)} %bitcast.7.table, bf16[32,512]{1,0:T(8,128)(2,1)S(1)} %copy-done.14, bf16[32,512]{1,0:T(8,128)(2,1)S(1)} %collective-permute-done.5.refs_1_, ...), custom_call_target="tpu_custom_call" | custom-call | flops 1 | bytes 1 | tf_op jit(solution)/shard_map/pallas_call | solution.py:103
  42.3 4.5 %shard_map.115 = (bf16[512,1024]{1,0:T(8,128)(2,1)}, bf16[512,512]{1,0:T(8,128)(2,1)}) custom-call(s32[3]{0:T(128)S(1)} %get-tuple-element.920.table, bf16[512,1024]{1,0:T(8,128)(2,1)S(1)} %get-tuple-element.805.refs_3_.grads.refs_5_.refs_9_, bf16[4096,1024]{1,0:T(8,128)(2,1)} %refs_25_, bf16[512,1024]{1,0:T(8,128)(2,1)} %collective-permute-done.9.came.refs_3_.refs_5_.refs_11_), custom_call_target="tpu_custom_call" | custom-call | flops 1 | bytes 1 | tf_op jit(solution)/shard_map/pallas_call | solution.py:103
  46.9 1.8 %collective-permute-start.15 = (bf16[512,1024]{1,0:T(8,128)(2,1)}, bf16[512,1024]{1,0:T(8,128)(2,1)S(1)}, u32[]{:S(2)}, u32[]{:S(2)}) collective-permute-start(bf16[512,1024]{1,0:T(8,128)(2,1)} %get-tuple-element.636), channel_id=1, source_target_pairs={{0,4},{5,1},{4,8},{9,5},{8,12},{13,9},{2,6},{7,3},{6,10},{11,7},{1... | collective-permute-start | bytes 3145736 | tf_op jit(solution)/shard_map/ppermute | solution.py:547
  49.1 4.3 %shard_map.116.a = bf16[512,1024]{1,0:T(8,128)(2,1)} custom-call(s32[2]{0:T(128)S(1)} %pad_add_fusion.1.table, bf16[512,512]{1,0:T(8,128)(2,1)} %collective-permute-done.12.refs_0_.refs_2_.refs_6_, bf16[512,1024]{1,0:T(8,128)(2,1)} %copy-done, bf16[512,512]{1,0:T(8,128)(2,1)} %copy-done.16, ...), custom_call_target="tpu_custom_call" | custom-call | flops 1 | bytes 1 | tf_op jit(solution)/shard_map/pallas_call | solution.py:103
  53.4 4.4 %shard_map.117 = (bf16[512,1024]{1,0:T(8,128)(2,1)S(1)}, bf16[512,512]{1,0:T(8,128)(2,1)}) custom-call(s32[3]{0:T(128)S(1)} %get-tuple-element.921.table, bf16[512,1024]{1,0:T(8,128)(2,1)S(1)} %get-tuple-element.804.refs_2_.grads.refs_6_.refs_4_.refs_8_, bf16[4096,1024]{1,0:T(8,128)(2,1)} %refs_25_, ...), custom_call_target="tpu_custom_call" | custom-call | flops 1 | bytes 1 | tf_op jit(solution)/shard_map/pallas_call | solution.py:103
  60.3 3.9 %collective-permute-start.18 = (bf16[512,1024]{1,0:T(8,128)(2,1)}, bf16[512,1024]{1,0:T(8,128)(2,1)}, u32[]{:S(2)}, u32[]{:S(2)}) collective-permute-start(bf16[512,1024]{1,0:T(8,128)(2,1)} %copy-done.15), channel_id=1, source_target_pairs={{0,4},{5,1},{4,8},{9,5},{8,12},{13,9},{2,6},{7,3},{6,10},{11,7},{1... | collective-permute-start | bytes 3145736 | tf_op jit(solution)/shard_map/ppermute | solution.py:547
  64.2 2.6 %shard_map.118 = (bf16[4096,1024]{1,0:T(8,128)(2,1)}, bf16[512,1024]{1,0:T(8,128)(2,1)}) custom-call(s32[1]{0:T(128)} %bitcast.14.table, bf16[512,1024]{1,0:T(8,128)(2,1)} %shard_map.111.a, bf16[512,1024]{1,0:T(8,128)(2,1)} %collective-permute-done.10.b), custom_call_target="tpu_custom_call" | custom-call | flops 1 | bytes 1 | tf_op jit(solution)/shard_map/pallas_call | solution.py:103
  66.8 3.6 %shard_map.119.term = bf16[512,1024]{1,0:T(8,128)(2,1)} custom-call(s32[1]{0:T(128)} %bitcast.15.table, bf16[512,1024]{1,0:T(8,128)(2,1)S(1)} %get-tuple-element.804.refs_2_.grads.refs_6_.refs_4_.refs_8_, bf16[4096,1024]{1,0:T(8,128)(2,1)} %refs_25_), custom_call_target="tpu_custom_call" | custom-call | flops 1 | bytes 1 | tf_op jit(solution)/shard_map/pallas_call | solution.py:103
  70.4 4.3 %shard_map.120 = (bf16[512,1024]{1,0:T(8,128)(2,1)}, bf16[512,512]{1,0:T(8,128)(2,1)}) custom-call(s32[3]{0:T(128)S(1)} %get-tuple-element.921.table, bf16[512,1024]{1,0:T(8,128)(2,1)S(1)} %get-tuple-element.805.refs_3_.grads.refs_5_.refs_9_, bf16[4096,1024]{1,0:T(8,128)(2,1)} %refs_25_, ...), custom_call_target="tpu_custom_call" | custom-call | flops 1 | bytes 1 | tf_op jit(solution)/shard_map/pallas_call | solution.py:103
  74.8 2.9 %collective-permute-start.22 = (bf16[512,1024]{1,0:T(8,128)(2,1)}, bf16[512,1024]{1,0:T(8,128)(2,1)}, u32[]{:S(2)}, u32[]{:S(2)}) collective-permute-start(bf16[512,1024]{1,0:T(8,128)(2,1)} %get-tuple-element.774), channel_id=1, source_target_pairs={{0,4},{5,1},{4,8},{9,5},{8,12},{13,9},{2,6},{7,3},{6,10},{11,7},{1... | collective-permute-start | bytes 3145736 | tf_op jit(solution)/shard_map/ppermute | solution.py:547
  78.8 4.4 %shard_map.121 = (bf16[512,1024]{1,0:T(8,128)(2,1)}, f32[64,1024]{1,0:T(8,128)S(1)}, bf16[64,1024]{1,0:T(8,128)(2,1)S(1)}) custom-call(s32[2]{0:T(128)S(1)} %pad_add_fusion.2.table, bf16[512,512]{1,0:T(8,128)(2,1)} %collective-permute-done.12.refs_0_.refs_2_.refs_6_, bf16[512,1024]{1,0:T(8,128)(2,1)} %copy-done, ...), custom_call_target="tpu_custom_call" | custom-call | flops 1 | bytes 1 | tf_op jit(solution)/shard_map/pallas_call | solution.py:103
  86.3 4.3 %shard_map.122 = (bf16[512,1024]{1,0:T(8,128)(2,1)}, bf16[512,512]{1,0:T(8,128)(2,1)S(1)}) custom-call(s32[3]{0:T(128)S(1)} %add_add_fusion.2.table, bf16[512,1024]{1,0:T(8,128)(2,1)S(1)} %get-tuple-element.804.refs_2_.grads.refs_6_.refs_4_.refs_8_, bf16[4096,1024]{1,0:T(8,128)(2,1)} %refs_25_, bf16[512,1024]{1,0:T(8,128)(2,1)} %collective-permute-done.18.came.refs_3_.refs_17_), custom_call_target="tpu_custom_call" | custom-call | flops 1 | bytes 1 | tf_op jit(solution)/shard_map/pallas_call | solution.py:103
  91.3 3.4 %collective-permute-start.25 = (bf16[512,1024]{1,0:T(8,128)(2,1)}, bf16[512,1024]{1,0:T(8,128)(2,1)}, u32[]{:S(2)}, u32[]{:S(2)}) collective-permute-start(bf16[512,1024]{1,0:T(8,128)(2,1)} %get-tuple-element.851), channel_id=1, source_target_pairs={{0,4},{5,1},{4,8},{9,5},{8,12},{13,9},{2,6},{7,3},{6,10},{11,7},{1... | collective-permute-start | bytes 3145736 | tf_op jit(solution)/shard_map/ppermute | solution.py:547
  94.7 2.7 %shard_map.123 = (bf16[4096,1024]{1,0:T(8,128)(2,1)}, bf16[512,1024]{1,0:T(8,128)(2,1)}) custom-call(s32[1]{0:T(128)} %bitcast.20.table, bf16[512,1024]{1,0:T(8,128)(2,1)} %shard_map.116.a, bf16[512,1024]{1,0:T(8,128)(2,1)} %collective-permute-done.17.b, bf16[4096,1024]{1,0:T(8,128)(2,1)} %get-tuple-element.758.refs_0_), custom_call_target="tpu_custom_call", output_to_operand_aliasing={{0}: (3, {})} | custom-call | flops 1 | bytes 1 | tf_op jit(solution)/shard_map/pallas_call | solution.py:103
  97.4 2.1 %shard_map.124.refs_0_ = bf16[4096,1024]{1,0:T(8,128)(2,1)} custom-call(s32[1]{0:T(128)} %bitcast.19.table, bf16[512,1024]{1,0:T(8,128)(2,1)} %collective-permute-done.19.value, bf16[4096,1024]{1,0:T(8,128)(2,1)} %get-tuple-element.759.refs_0_), custom_call_target="tpu_custom_call", output_to_operand_aliasing={{}: (2, {})} | custom-call | flops 1 | bytes 1 | tf_op jit(solution)/shard_map/pallas_call | solution.py:103
  99.6 1.9 %shard_map.125 = (bf16[512,1024]{1,0:T(8,128)(2,1)}, bf16[512,1024]{1,0:T(8,128)(2,1)}) custom-call(s32[1]{0:T(128)} %constant.35.clone.1.table, bf16[128,512]{1,0:T(8,128)(2,1)S(1)} %copy-done.12, bf16[128,1024]{1,0:T(8,128)(2,1)S(1)} %copy-done.11, bf16[128,512]{1,0:T(8,128)(2,1)S(1)} %copy-done.13, bf16[128,1024]{1,0:T(8,128)(2,1)S(1)} %copy-done.10), custom_call_target="tpu_custom_call" | custom-call | flops 1 | bytes 1 | tf_op jit(solution)/shard_map/pallas_call | solution.py:103
  101.5 4.3 %shard_map.126 = (bf16[512,1024]{1,0:T(8,128)(2,1)}, bf16[512,512]{1,0:T(8,128)(2,1)S(1)}) custom-call(s32[3]{0:T(128)S(1)} %add_add_fusion.2.table, bf16[512,1024]{1,0:T(8,128)(2,1)S(1)} %get-tuple-element.805.refs_3_.grads.refs_5_.refs_9_, bf16[4096,1024]{1,0:T(8,128)(2,1)} %refs_25_, bf16[512,1024]{1,0:T(8,128)(2,1)} %collective-permute-done.22.came.refs_7_.refs_21_), custom_call_target="tpu_custom_call" | custom-call | flops 1 | bytes 1 | tf_op jit(solution)/shard_map/pallas_call | solution.py:103
  105.7 3.6 %collective-permute-start.27 = (bf16[512,1024]{1,0:T(8,128)(2,1)}, bf16[512,1024]{1,0:T(8,128)(2,1)}, u32[]{:S(2)}, u32[]{:S(2)}) collective-permute-start(bf16[512,1024]{1,0:T(8,128)(2,1)} %get-tuple-element.884), channel_id=1, source_target_pairs={{0,4},{5,1},{4,8},{9,5},{8,12},{13,9},{2,6},{7,3},{6,10},{11,7},{1... | collective-permute-start | bytes 3145736 | tf_op jit(solution)/shard_map/ppermute | solution.py:547
  109.5 2.0 %collective-permute-done.23.refs_2_.refs_16_ = bf16[512,512]{1,0:T(8,128)(2,1)} collective-permute-done((bf16[512,512]{1,0:T(8,128)(2,1)S(1)}, bf16[512,512]{1,0:T(8,128)(2,1)}, u32[]{:S(2)}, u32[]{:S(2)}) %collective-permute-start.23) | collective-permute-done | bytes 524320 | tf_op jit(solution)/shard_map/ppermute | solution.py:553
  111.4 3.5 %shard_map.127.a = bf16[512,1024]{1,0:T(8,128)(2,1)S(1)} custom-call(s32[2]{0:T(128)S(1)} %pad_add_fusion.3.table, bf16[512,512]{1,0:T(8,128)(2,1)} %collective-permute-done.16.refs_2_.refs_0_.refs_8_.refs_14_, bf16[512,1024]{1,0:T(8,128)(2,1)} %collective-permute-done.13.came.refs_3_.refs_1_.refs_9_.refs_15_, ...), custom_call_target="tpu_custom_call" | custom-call | flops 1 | bytes 1 | tf_op jit(solution)/shard_map/pallas_call | solution.py:103
  117.3 2.8 %shard_map.128 = (bf16[4096,1024]{1,0:T(8,128)(2,1)}, bf16[512,1024]{1,0:T(8,128)(2,1)}) custom-call(s32[1]{0:T(128)} %bitcast.23.table, bf16[512,1024]{1,0:T(8,128)(2,1)} %get-tuple-element.863.a, bf16[512,1024]{1,0:T(8,128)(2,1)} %collective-permute-done.24.b, bf16[4096,1024]{1,0:T(8,128)(2,1)} %shard_map.124.refs_0_), custom_call_target="tpu_custom_call", output_to_operand_aliasing={{0}: (3, {})} | custom-call | flops 1 | bytes 1 | tf_op jit(solution)/shard_map/pallas_call | solution.py:103
  120.1 2.2 %shard_map.129.refs_0_ = bf16[4096,1024]{1,0:T(8,128)(2,1)} custom-call(s32[1]{0:T(128)} %bitcast.22.table, bf16[512,1024]{1,0:T(8,128)(2,1)} %collective-permute-done.26.value, bf16[4096,1024]{1,0:T(8,128)(2,1)} %get-tuple-element.866.refs_0_), custom_call_target="tpu_custom_call", output_to_operand_aliasing={{}: (2, {})} | custom-call | flops 1 | bytes 1 | tf_op jit(solution)/shard_map/pallas_call | solution.py:103
  123.2 8.7 %shard_map.130 = (f32[512,1024]{1,0:T(8,128)}, bf16[256,1024]{1,0:T(8,128)(2,1)S(1)}, bf16[256,1024]{1,0:T(8,128)(2,1)S(1)}) custom-call(s32[9]{0:T(128)S(1)} %stack.148.table, bf16[512,1024]{1,0:T(8,128)(2,1)} %refs_0_.1, bf16[512,1024]{1,0:T(8,128)(2,1)} %collective-permute-done.refs_1_, bf16[512,512]{1,0:T(8,128)(2,1)} %collective-permute-done.12.refs_0_.refs_2_.refs_6_, ...), custom_call_target="tpu_custom_call" | custom-call | flops 1 | bytes 1 | tf_op jit(solution)/shard_map/pallas_call | solution.py:103
  137.0 4.4 %shard_map.131 = (bf16[512,1024]{1,0:T(8,128)(2,1)}, bf16[512,1024]{1,0:T(8,128)(2,1)}, f32[64,1024]{1,0:T(8,128)}, f32[64,1024]{1,0:T(8,128)}) custom-call(s32[1]{0:T(128)} %bitcast.7.table, f32[512,1024]{1,0:T(8,128)} %get-tuple-element.890.here, f32[512,1]{1,0:T(8,128)S(1)} %copy-done.7, bf16[512,1024]{1,0:T(8,128)(2,1)S(1)} %copy-done.4, ...), custom_call_target="tpu_custom_call" | custom-call | flops 1 | bytes 1 | tf_op jit(solution)/shard_map/pallas_call | solution.py:103
  (119 shorter events, 30.3 us)
Async XLA Ops:
  0.6 10.4 %collective-permute-start.2 = (bf16[512,1024]{1,0:T(8,128)(2,1)}, bf16[512,1024]{1,0:T(8,128)(2,1)}, u32[]{:S(2)}, u32[]{:S(2)}) collective-permute-start(bf16[512,1024]{1,0:T(8,128)(2,1)} %mine.1), channel_id=1, source_target_pairs={{0,1},{1,0},{2,3},{3,2},{4,5},{5,4},{6,7},{7,6},{8,9},{9,8},{10,11... | collective-permute-start | bytes 3145736 | tf_op jit(solution)/shard_map/ppermute | solution.py:553
  1.1 13.1 %collective-permute-start = (bf16[512,1024]{1,0:T(8,128)(2,1)}, bf16[512,1024]{1,0:T(8,128)(2,1)}, u32[]{:S(2)}, u32[]{:S(2)}) collective-permute-start(bf16[512,1024]{1,0:T(8,128)(2,1)} %refs_0_.1), channel_id=1, source_target_pairs={{0,1},{1,0},{2,3},{3,2},{4,5},{5,4},{6,7},{7,6},{8,9},{9,8},{10,11... | collective-permute-start | bytes 3145736 | tf_op jit(solution)/shard_map/ppermute | solution.py:553
  1.2 26.6 %collective-permute-start.4 = (bf16[512,1024]{1,0:T(8,128)(2,1)}, bf16[512,1024]{1,0:T(8,128)(2,1)S(1)}, u32[]{:S(2)}, u32[]{:S(2)}) collective-permute-start(bf16[512,1024]{1,0:T(8,128)(2,1)} %refs_0_.1), channel_id=1, source_target_pairs={{0,4},{5,1},{4,8},{9,5},{8,12},{13,9},{2,6},{7,3},{6,10},{11,7},{1... | collective-permute-start | bytes 3145736 | tf_op jit(solution)/shard_map/ppermute | solution.py:547
  7.8 6.4 %collective-permute-start.1 = (bf16[64,1024]{1,0:T(8,128)(2,1)}, bf16[64,1024]{1,0:T(8,128)(2,1)S(1)}, u32[]{:S(2)}, u32[]{:S(2)}) collective-permute-start(bf16[64,1024]{1,0:T(8,128)(2,1)} %fusion.1), channel_id=1, source_target_pairs={{0,2},{2,0},{1,3},{3,1},{4,6},{6,4},{5,7},{7,5},{8,10},{10,8},{9,1... | collective-permute-start | bytes 393224 | tf_op jit(solution)/shard_map/ppermute | solution.py:550
  14.2 28.0 %collective-permute-start.9 = (bf16[512,1024]{1,0:T(8,128)(2,1)}, bf16[512,1024]{1,0:T(8,128)(2,1)}, u32[]{:S(2)}, u32[]{:S(2)}) collective-permute-start(bf16[512,1024]{1,0:T(8,128)(2,1)} %collective-permute-done.refs_1_), channel_id=1, source_target_pairs={{0,4},{5,1},{4,8},{9,5},{8,12},{13,9},{2,6},{7,3},{6,10},{11,7},{1... | collective-permute-start | bytes 3145736 | tf_op jit(solution)/shard_map/ppermute | solution.py:547
  22.9 23.8 %collective-permute-start.10 = (bf16[512,1024]{1,0:T(8,128)(2,1)}, bf16[512,1024]{1,0:T(8,128)(2,1)}, u32[]{:S(2)}, u32[]{:S(2)}) collective-permute-start(bf16[512,1024]{1,0:T(8,128)(2,1)} %shard_map.111.a), channel_id=1, source_target_pairs={{0,2},{2,0},{1,3},{3,1},{4,6},{6,4},{5,7},{7,5},{8,10},{10,8},{9,1... | collective-permute-start | bytes 3145736 | tf_op jit(solution)/shard_map/ppermute | solution.py:550
  27.8 8.1 %collective-permute-start.5 = (bf16[32,512]{1,0:T(8,128)(2,1)}, bf16[32,512]{1,0:T(8,128)(2,1)S(1)}, u32[]{:S(2)}, u32[]{:S(2)}) collective-permute-start(bf16[32,512]{1,0:T(8,128)(2,1)} %get-tuple-element.520.refs_0_), channel_id=1, source_target_pairs={{0,4},{4,8},{8,12},{12,0},{1,5},{5,9},{9,13},{13,1},{2,6},{6,10},{... | collective-permute-start | bytes 98312 | tf_op jit(solution)/shard_map/ppermute | solution.py:650
  28.5 7.4 %collective-permute-start.6 = (bf16[32,512]{1,0:T(8,128)(2,1)}, bf16[32,512]{1,0:T(8,128)(2,1)S(1)}, u32[]{:S(2)}, u32[]{:S(2)}) collective-permute-start(bf16[32,512]{1,0:T(8,128)(2,1)} %get-tuple-element.520.refs_0_), channel_id=1, source_target_pairs={{0,8},{4,12},{8,0},{12,4},{1,9},{5,13},{9,1},{13,5},{2,10},{6,14},... | collective-permute-start | bytes 98312 | tf_op jit(solution)/shard_map/ppermute | solution.py:650
  28.5 7.4 %collective-permute-start.7 = (bf16[32,512]{1,0:T(8,128)(2,1)}, bf16[32,512]{1,0:T(8,128)(2,1)S(1)}, u32[]{:S(2)}, u32[]{:S(2)}) collective-permute-start(bf16[32,512]{1,0:T(8,128)(2,1)} %get-tuple-element.520.refs_0_), channel_id=1, source_target_pairs={{0,12},{4,0},{8,4},{12,8},{1,13},{5,1},{9,5},{13,9},{2,14},{6,2},{... | collective-permute-start | bytes 98312 | tf_op jit(solution)/shard_map/ppermute | solution.py:650
  35.9 6.3 %collective-permute-start.8 = (bf16[512,512]{1,0:T(8,128)(2,1)S(1)}, bf16[512,512]{1,0:T(8,128)(2,1)S(1)}, u32[]{:S(2)}, u32[]{:S(2)}) collective-permute-start(bf16[512,512]{1,0:T(8,128)(2,1)S(1)} %get-tuple-element.519), channel_id=1, source_target_pairs={{0,1},{1,0},{2,3},{3,2},{4,5},{5,4},{6,7},{7,6},{8,9},{9,8},{10,11... | collective-permute-start | bytes 1572872 | tf_op jit(solution)/shard_map/ppermute | solution.py:553
  36.0 17.4 %collective-permute-start.13 = (bf16[512,1024]{1,0:T(8,128)(2,1)}, bf16[512,1024]{1,0:T(8,128)(2,1)}, u32[]{:S(2)}, u32[]{:S(2)}) collective-permute-start(bf16[512,1024]{1,0:T(8,128)(2,1)} %get-tuple-element.588), channel_id=1, source_target_pairs={{0,4},{5,1},{4,8},{9,5},{8,12},{13,9},{2,6},{7,3},{6,10},{11,7},{1... | collective-permute-start | bytes 3145736 | tf_op jit(solution)/shard_map/ppermute | solution.py:547
  42.3 4.5 %collective-permute-start.11 = (bf16[128,1024]{1,0:T(8,128)(2,1)}, bf16[128,1024]{1,0:T(8,128)(2,1)S(1)}, u32[]{:S(2)}, u32[]{:S(2)}) collective-permute-start(bf16[128,1024]{1,0:T(8,128)(2,1)} %get-tuple-element.547), channel_id=1, source_target_pairs={{0,1},{1,0},{2,3},{3,2},{4,5},{5,4},{6,7},{7,6},{8,9},{9,8},{10,11... | collective-permute-start | bytes 786440 | tf_op jit(solution)/shard_map/ppermute | solution.py:553
  46.8 2.3 %collective-permute-start.12 = (bf16[512,512]{1,0:T(8,128)(2,1)}, bf16[512,512]{1,0:T(8,128)(2,1)}, u32[]{:S(2)}, u32[]{:S(2)}) collective-permute-start(bf16[512,512]{1,0:T(8,128)(2,1)} %get-tuple-element.567), channel_id=1, source_target_pairs={{0,1},{1,0},{2,3},{3,2},{4,5},{5,4},{6,7},{7,6},{8,9},{9,8},{10,11... | collective-permute-start | bytes 1572872 | tf_op jit(solution)/shard_map/ppermute | solution.py:553
  46.9 23.5 %collective-permute-start.15 = (bf16[512,1024]{1,0:T(8,128)(2,1)}, bf16[512,1024]{1,0:T(8,128)(2,1)S(1)}, u32[]{:S(2)}, u32[]{:S(2)}) collective-permute-start(bf16[512,1024]{1,0:T(8,128)(2,1)} %get-tuple-element.636), channel_id=1, source_target_pairs={{0,4},{5,1},{4,8},{9,5},{8,12},{13,9},{2,6},{7,3},{6,10},{11,7},{1... | collective-permute-start | bytes 3145736 | tf_op jit(solution)/shard_map/ppermute | solution.py:547
  58.8 11.6 %collective-permute-start.14 = (bf16[512,512]{1,0:T(8,128)(2,1)}, bf16[512,512]{1,0:T(8,128)(2,1)}, u32[]{:S(2)}, u32[]{:S(2)}) collective-permute-start(bf16[512,512]{1,0:T(8,128)(2,1)} %get-tuple-element.631), channel_id=1, source_target_pairs={{0,1},{1,0},{2,3},{3,2},{4,5},{5,4},{6,7},{7,6},{8,9},{9,8},{10,11... | collective-permute-start | bytes 1572872 | tf_op jit(solution)/shard_map/ppermute | solution.py:553
  58.8 25.9 %collective-permute-start.17 = (bf16[512,1024]{1,0:T(8,128)(2,1)}, bf16[512,1024]{1,0:T(8,128)(2,1)}, u32[]{:S(2)}, u32[]{:S(2)}) collective-permute-start(bf16[512,1024]{1,0:T(8,128)(2,1)} %shard_map.116.a), channel_id=1, source_target_pairs={{0,2},{2,0},{1,3},{3,1},{4,6},{6,4},{5,7},{7,5},{8,10},{10,8},{9,1... | collective-permute-start | bytes 3145736 | tf_op jit(solution)/shard_map/ppermute | solution.py:550
  60.3 24.4 %collective-permute-start.18 = (bf16[512,1024]{1,0:T(8,128)(2,1)}, bf16[512,1024]{1,0:T(8,128)(2,1)}, u32[]{:S(2)}, u32[]{:S(2)}) collective-permute-start(bf16[512,1024]{1,0:T(8,128)(2,1)} %copy-done.15), channel_id=1, source_target_pairs={{0,4},{5,1},{4,8},{9,5},{8,12},{13,9},{2,6},{7,3},{6,10},{11,7},{1... | collective-permute-start | bytes 3145736 | tf_op jit(solution)/shard_map/ppermute | solution.py:547
  66.8 17.9 %collective-permute-start.19 = (bf16[512,1024]{1,0:T(8,128)(2,1)}, bf16[512,1024]{1,0:T(8,128)(2,1)}, u32[]{:S(2)}, u32[]{:S(2)}) collective-permute-start(bf16[512,1024]{1,0:T(8,128)(2,1)} %get-tuple-element.635), channel_id=1, source_target_pairs={{0,1},{1,0},{2,3},{3,2},{4,5},{5,4},{6,7},{7,6},{8,9},{9,8},{10,11... | collective-permute-start | bytes 3145736 | tf_op jit(solution)/shard_map/ppermute | solution.py:553
  74.8 3.0 %collective-permute-start.16 = (bf16[512,512]{1,0:T(8,128)(2,1)}, bf16[512,512]{1,0:T(8,128)(2,1)}, u32[]{:S(2)}, u32[]{:S(2)}) collective-permute-start(bf16[512,512]{1,0:T(8,128)(2,1)} %get-tuple-element.669), channel_id=1, source_target_pairs={{0,1},{1,0},{2,3},{3,2},{4,5},{5,4},{6,7},{7,6},{8,9},{9,8},{10,11... | collective-permute-start | bytes 1572872 | tf_op jit(solution)/shard_map/ppermute | solution.py:553
  74.8 26.7 %collective-permute-start.22 = (bf16[512,1024]{1,0:T(8,128)(2,1)}, bf16[512,1024]{1,0:T(8,128)(2,1)}, u32[]{:S(2)}, u32[]{:S(2)}) collective-permute-start(bf16[512,1024]{1,0:T(8,128)(2,1)} %get-tuple-element.774), channel_id=1, source_target_pairs={{0,4},{5,1},{4,8},{9,5},{8,12},{13,9},{2,6},{7,3},{6,10},{11,7},{1... | collective-permute-start | bytes 3145736 | tf_op jit(solution)/shard_map/ppermute | solution.py:547
  84.7 5.9 %collective-permute-start.20 = (bf16[64,1024]{1,0:T(8,128)(2,1)S(1)}, bf16[64,1024]{1,0:T(8,128)(2,1)S(1)}, u32[]{:S(2)}, u32[]{:S(2)}) collective-permute-start(bf16[64,1024]{1,0:T(8,128)(2,1)S(1)} %get-tuple-element.741), channel_id=1, source_target_pairs={{0,2},{2,0},{1,3},{3,1},{4,6},{6,4},{5,7},{7,5},{8,10},{10,8},{9,1... | collective-permute-start | bytes 393224 | tf_op jit(solution)/shard_map/ppermute | solution.py:550
  90.6 10.8 %collective-permute-start.21 = (bf16[512,512]{1,0:T(8,128)(2,1)S(1)}, bf16[512,512]{1,0:T(8,128)(2,1)S(1)}, u32[]{:S(2)}, u32[]{:S(2)}) collective-permute-start(bf16[512,512]{1,0:T(8,128)(2,1)S(1)} %get-tuple-element.766), channel_id=1, source_target_pairs={{0,1},{1,0},{2,3},{3,2},{4,5},{5,4},{6,7},{7,6},{8,9},{9,8},{10,11... | collective-permute-start | bytes 1572872 | tf_op jit(solution)/shard_map/ppermute | solution.py:553
  90.6 25.9 %collective-permute-start.24 = (bf16[512,1024]{1,0:T(8,128)(2,1)}, bf16[512,1024]{1,0:T(8,128)(2,1)}, u32[]{:S(2)}, u32[]{:S(2)}) collective-permute-start(bf16[512,1024]{1,0:T(8,128)(2,1)} %get-tuple-element.863.a), channel_id=1, source_target_pairs={{0,2},{2,0},{1,3},{3,1},{4,6},{6,4},{5,7},{7,5},{8,10},{10,8},{9,1... | collective-permute-start | bytes 3145736 | tf_op jit(solution)/shard_map/ppermute | solution.py:550
  91.3 26.0 %collective-permute-start.25 = (bf16[512,1024]{1,0:T(8,128)(2,1)}, bf16[512,1024]{1,0:T(8,128)(2,1)}, u32[]{:S(2)}, u32[]{:S(2)}) collective-permute-start(bf16[512,1024]{1,0:T(8,128)(2,1)} %get-tuple-element.851), channel_id=1, source_target_pairs={{0,4},{5,1},{4,8},{9,5},{8,12},{13,9},{2,6},{7,3},{6,10},{11,7},{1... | collective-permute-start | bytes 3145736 | tf_op jit(solution)/shard_map/ppermute | solution.py:547
  97.4 19.9 %collective-permute-start.26 = (bf16[512,1024]{1,0:T(8,128)(2,1)}, bf16[512,1024]{1,0:T(8,128)(2,1)}, u32[]{:S(2)}, u32[]{:S(2)}) collective-permute-start(bf16[512,1024]{1,0:T(8,128)(2,1)} %get-tuple-element.767), channel_id=1, source_target_pairs={{0,1},{1,0},{2,3},{3,2},{4,5},{5,4},{6,7},{7,6},{8,9},{9,8},{10,11... | collective-permute-start | bytes 3145736 | tf_op jit(solution)/shard_map/ppermute | solution.py:553
  105.7 26.2 %collective-permute-start.27 = (bf16[512,1024]{1,0:T(8,128)(2,1)}, bf16[512,1024]{1,0:T(8,128)(2,1)}, u32[]{:S(2)}, u32[]{:S(2)}) collective-permute-start(bf16[512,1024]{1,0:T(8,128)(2,1)} %get-tuple-element.884), channel_id=1, source_target_pairs={{0,4},{5,1},{4,8},{9,5},{8,12},{13,9},{2,6},{7,3},{6,10},{11,7},{1... | collective-permute-start | bytes 3145736 | tf_op jit(solution)/shard_map/ppermute | solution.py:547
  116.5 24.9 %collective-permute-start.33 = (bf16[512,1024]{1,0:T(8,128)(2,1)S(1)}, bf16[512,1024]{1,0:T(8,128)(2,1)}, u32[]{:S(2)}, u32[]{:S(2)}) collective-permute-start(bf16[512,1024]{1,0:T(8,128)(2,1)S(1)} %shard_map.127.a), channel_id=1, source_target_pairs={{0,2},{2,0},{1,3},{3,1},{4,6},{6,4},{5,7},{7,5},{8,10},{10,8},{9,1... | collective-permute-start | bytes 3145736 | tf_op jit(solution)/shard_map/ppermute | solution.py:550
  131.9 3.2 %collective-permute-start.28 = (bf16[256,1024]{1,0:T(8,128)(2,1)S(1)}, bf16[256,1024]{1,0:T(8,128)(2,1)S(1)}, u32[]{:S(2)}, u32[]{:S(2)}) collective-permute-start(bf16[256,1024]{1,0:T(8,128)(2,1)S(1)} %get-tuple-element.895), channel_id=1, source_target_pairs={{0,1},{1,0},{2,3},{3,2},{4,5},{5,4},{6,7},{7,6},{8,9},{9,8},{10,11... | collective-permute-start | bytes 1572872 | tf_op jit(solution)/shard_map/ppermute | solution.py:553
  132.0 3.2 %collective-permute-start.29 = (bf16[256,1024]{1,0:T(8,128)(2,1)S(1)}, bf16[256,1024]{1,0:T(8,128)(2,1)S(1)}, u32[]{:S(2)}, u32[]{:S(2)}) collective-permute-start(bf16[256,1024]{1,0:T(8,128)(2,1)S(1)} %get-tuple-element.896), channel_id=1, source_target_pairs={{0,1},{1,0},{2,3},{3,2},{4,5},{5,4},{6,7},{7,6},{8,9},{9,8},{10,11... | collective-permute-start | bytes 1572872 | tf_op jit(solution)/shard_map/ppermute | solution.py:553
  132.5 2.5 %collective-permute-start.32 = (f32[64,1024]{1,0:T(8,128)S(1)}, f32[64,1024]{1,0:T(8,128)S(1)}, u32[]{:S(2)}, u32[]{:S(2)}) collective-permute-start(f32[64,1024]{1,0:T(8,128)S(1)} %convert_add_fusion.kept), channel_id=1, source_target_pairs={{0,1},{1,0},{2,3},{3,2},{4,5},{5,4},{6,7},{7,6},{8,9},{9,8},{10,11... | collective-permute-start | bytes 786440 | tf_op jit(solution)/shard_map/ppermute | solution.py:553
  141.4 3.3 %collective-permute-start.35 = (bf16[512,1024]{1,0:T(8,128)(2,1)}, bf16[512,1024]{1,0:T(8,128)(2,1)S(1)}, u32[]{:S(2)}, u32[]{:S(2)}) collective-permute-start(bf16[512,1024]{1,0:T(8,128)(2,1)} %get-tuple-element.914), channel_id=1, source_target_pairs={{0,1},{1,0},{2,3},{3,2},{4,5},{5,4},{6,7},{7,6},{8,9},{9,8},{10,11... | collective-permute-start | bytes 3145736 | tf_op jit(solution)/shard_map/ppermute | solution.py:553
  143.3 2.7 %collective-permute-start.34 = (bf16[512,1024]{1,0:T(8,128)(2,1)S(1)}, bf16[512,1024]{1,0:T(8,128)(2,1)S(1)}, u32[]{:S(2)}, u32[]{:S(2)}) collective-permute-start(bf16[512,1024]{1,0:T(8,128)(2,1)S(1)} %shard_map.132.value), channel_id=1, source_target_pairs={{0,1},{1,0},{2,3},{3,2},{4,5},{5,4},{6,7},{7,6},{8,9},{9,8},{10,11... | collective-permute-start | bytes 3145736 | tf_op jit(solution)/shard_map/ppermute | solution.py:553
  (24 other events, 149.0 us)
